TPU v7x, 512 devices: a whole 4x4x16 slice. The times are simulated.
512 devices in a mesh: layer: 8 (over z_lo), lat: 64 (over x, z_hi, y, core).
Axes of the slice: x: 4, y: 4, z: 16 (z_hi: 2, z_lo: 8; z = z_hi * 8 + z_lo), core: 2. Of those that a mesh axis runs over, the one named last changes fastest.
Arguments:
- activations: bfloat16 [512, 9216], P('lat', 'layer'), may hold values from -6 to 6
- enc_weight: bfloat16 [9216, 32768], P('layer', 'lat'), may hold values from -0.0625 to 0.0625
- enc_bias: float32 [32768], P('lat'), may hold values from -3 to 3
- dec_weight: bfloat16 [32768, 9216], P('lat', 'layer'), as said below
- dec_bias: float32 [9216], P('layer'), may hold values from -3 to 3
Outputs:
- enc_grad: bfloat16 [9216, 32768], P('layer', 'lat')
- dec_grad: bfloat16 [32768, 9216], P('lat', 'layer')
Inputs may be any that keep to these rules, and one draw needn't show every extreme that they name: `dec_weight`: entries within 24 / sqrt(32768) in magnitude.
All inputs are finite; a program needn't handle non-finite values.
Results may differ from a plain program's by a relative error of at most 0.0075.
Values may be sent and summed in bfloat16 or wider, within the bound.
No kernel may reach another device: no remote copies, remote signals or barrier semaphores. Data moves between devices by JAX's collectives and lax.ppermute only.
A program may use at most 64 MiB of HBM per device.

v0:
```python
import jax
import jax.numpy as jnp
from jax import lax
from jax.sharding import PartitionSpec as P

norm_eps = 1e-06
sparsity = 0.5
sharpness = 4.0


def back_part(rows_block, dec_weight):
    return lax.dot_general(
        rows_block, dec_weight, (((1,), (1,)), ((), ())), preferred_element_type=jnp.float32
    )


def local(activations, enc_weight, enc_bias, dec_weight, dec_bias):
    all_rows = lax.all_gather(activations, "lat", axis=0, tiled=True)
    squares = jnp.einsum("hf,hf->h", dec_weight, dec_weight, preferred_element_type=jnp.float32)
    block = jnp.dot(all_rows, enc_weight, preferred_element_type=jnp.float32)
    preact, summed_sq = lax.psum((block, squares), "layer")
    preact = preact + enc_bias
    dec_norm = jnp.sqrt(summed_sq + norm_eps)
    gating = jax.nn.sigmoid(sharpness * preact)
    latents = (preact * gating).astype(jnp.bfloat16)
    rebuilt = lax.psum_scatter(
        jnp.dot(latents, dec_weight, preferred_element_type=jnp.float32),
        "lat",
        scatter_dimension=0,
        tiled=True,
    )
    mine = (rebuilt + dec_bias - activations.astype(jnp.float32)).astype(jnp.bfloat16)
    residual = lax.all_gather(mine, "lat", axis=0, tiled=True)
    lat_sums = jnp.sum(latents.astype(jnp.float32), axis=0)
    dec_grad = lax.dot_general(
        latents, residual, (((0,), (0,)), ((), ())), preferred_element_type=jnp.float32
    )
    dec_grad = (
        dec_grad + sparsity * lat_sums[:, None] * dec_weight.astype(jnp.float32) / dec_norm[:, None]
    )
    lat_grad = lax.psum(back_part(residual, dec_weight), "layer")
    lat_grad = lat_grad + sparsity * dec_norm
    pre_grad = (lat_grad * (gating + sharpness * preact * gating * (1.0 - gating))).astype(
        jnp.bfloat16
    )
    enc_grad = lax.dot_general(
        all_rows, pre_grad, (((0,), (0,)), ((), ())), preferred_element_type=jnp.float32
    )
    return (enc_grad.astype(jnp.bfloat16), dec_grad.astype(jnp.bfloat16))


def solution(mesh):
    placed = (P("lat", "layer"), P("layer", "lat"), P("lat"), P("lat", "layer"), P("layer"))
    return jax.shard_map(
        local,
        mesh=mesh,
        in_specs=placed,
        out_specs=(P("layer", "lat"), P("lat", "layer")),
        check_vma=False,
    )
```

profile of v0, /device:TPU:1, one launch (start us, length us, event | category | flops | bytes accessed | tf_op | source)
XLA Modules:
  0.0 1549.8 jit_solution(17274186402663582207)
XLA Ops:
  7.2 0.0 copy-start
  7.2 0.0 all-gather.3.cloned.1.call-start
  7.2 0.7 all-gather.3.cloned.1.call-update
  7.9 0.0 copy-start.4
  7.9 0.0 all-reduce.5.cloned.1.call-start
  8.0 114.2 %all-gather.3.cloned.1.call-done = bf16[512,1152]{1,0:T(8,128)(2,1)} async-done(((bf16[8,1152]{1,0:T(8,128)(2,1)}), bf16[512,1152]{1,0:T(8,128)(2,1)}) %all-gather.3.cloned.1.call-update) | async-done | bytes 1179664 | tf_op jit(solution)/shard_map/all_gather | solution.py:18
  122.1 0.0 copy-done
  122.1 3.1 fusion.12
  125.2 0.0 copy-start.1
  125.2 0.0 all-reduce.5.cloned.1.call-update
  125.2 0.0 all-reduce.9.cloned.1.call-start
  125.3 111.7 %all-reduce.5.cloned.1.call-done = f32[512,512]{1,0:T(8,128)} async-done(((f32[512,512]{1,0:T(8,128)}), f32[512,512]{1,0:T(8,128)}) %all-reduce.5.cloned.1.call-update) | async-done | bytes 1048592 | tf_op jit(solution)/shard_map/psum | solution.py:21
  237.0 0.0 copy-done.4
  237.0 1.5 convert_reduce_fusion
  238.5 0.0 copy-done.1
  238.5 2.2 fusion.13
  240.8 0.0 copy-start.2
  240.8 0.0 copy-start.3
  240.8 0.0 all-reduce.9.cloned.1.call-update
  240.8 0.0 all-gather.5.cloned.1.call-start
  240.9 1.3 dynamic-slice
  242.8 1072.2 %all-reduce.9.cloned.1.call-done = f32[512,1152]{1,0:T(8,128)} async-done(((f32[512,1152]{1,0:T(8,128)}), f32[512,1152]{1,0:T(8,128)}) %all-reduce.9.cloned.1.call-update) | async-done | bytes 2359312
  1315.0 0.0 copy-done.2
  1315.0 0.0 copy-done.3
  1315.0 1.4 fusion.9
  1316.4 0.0 all-gather.5.cloned.1.call-update
  1316.4 0.0 all-reduce.7.cloned.1.call-start
  1316.4 107.2 %all-gather.5.cloned.1.call-done = bf16[512,1152]{1,0:T(8,128)(2,1)} async-done(((bf16[8,1152]{1,0:T(8,128)(2,1)}), bf16[512,1152]{1,0:T(8,128)(2,1)}) %all-gather.5.cloned.1.call-update) | async-done | bytes 1179664 | tf_op jit(solution)/shard_map/all_gather | solution.py:33
  1423.7 3.1 fusion.14
  1426.8 0.0 all-reduce.7.cloned.1.call-update
  1426.8 0.3 fusion.2
  1427.1 22.6 %psum.23 = f32[512]{0:T(512)S(1)} all-reduce(f32[512]{0:T(512)S(1)} %fusion.2), channel_id=1, replica_groups=mesh['layer'=8,'lat'=64] {'layer'}, use_global_device_ids=true, to_apply=%region_3.0 | all-reduce | flops 512 | bytes 4096 | tf_op jit(solution)/shard_map/psum | solution.py:21
  1449.7 3.2 fusion
  1453.0 85.8 %all-reduce.7.cloned.1.call-done = f32[512,512]{1,0:T(8,128)} async-done(((f32[512,512]{1,0:T(8,128)}), f32[512,512]{1,0:T(8,128)}) %all-reduce.7.cloned.1.call-update) | async-done | bytes 1048592 | tf_op jit(solution)/shard_map/psum | solution.py:41
  1538.8 3.0 fusion.1
  1541.8 1.4 copy.8
  (2 shorter events, 0.0 us)
Async XLA Ops:
  7.2 115.0 %copy-start = (bf16[1152,512]{1,0:T(8,128)(2,1)S(1)}, bf16[1152,512]{1,0:T(8,128)(2,1)}, u32[]{:S(2)}) copy-start(bf16[1152,512]{1,0:T(8,128)(2,1)} %param.6) | copy-start | bytes 3538948
  7.2 114.9 %all-gather.3.cloned.1.call-start = ((), (), s32[]{:S(2)}) async-start(), calls=%async_computation | async-start | bytes 1198080 | tf_op jit(solution)/shard_map/all_gather | solution.py:18
  7.9 229.1 %copy-start.4 = (f32[512]{0:T(512)S(1)}, f32[512]{0:T(512)}, u32[]{:S(2)}) copy-start(f32[512]{0:T(512)} %param.7) | copy-start | bytes 6148
  7.9 229.1 %all-reduce.5.cloned.1.call-start = ((), (), s32[]{:S(2)}) async-start(), calls=%async_computation.1 | async-start | bytes 2097152 | tf_op jit(solution)/shard_map/psum | solution.py:21
  125.2 113.3 %copy-start.1 = (bf16[512,1152]{1,0:T(8,128)(2,1)S(1)}, bf16[512,1152]{1,0:T(8,128)(2,1)}, u32[]{:S(2)}) copy-start(bf16[512,1152]{1,0:T(8,128)(2,1)} %param.8) | copy-start | bytes 3538948
  125.2 1189.7 %all-reduce.9.cloned.1.call-start = ((), (), s32[]{:S(2)}) async-start(), calls=%async_computation.4 | async-start | bytes 4718592
  240.8 1074.2 %copy-start.2 = (bf16[8,1152]{1,0:T(8,128)(2,1)S(1)}, bf16[8,1152]{1,0:T(8,128)(2,1)}, u32[]{:S(2)}) copy-start(bf16[8,1152]{1,0:T(8,128)(2,1)} %param.5) | copy-start | bytes 55300
  240.8 1074.2 %copy-start.3 = (f32[1152]{0:T(1024)S(1)}, f32[1152]{0:T(1024)}, u32[]{:S(2)}) copy-start(f32[1152]{0:T(1024)} %param.9) | copy-start | bytes 13828
  240.8 1182.9 %all-gather.5.cloned.1.call-start = ((), (), s32[]{:S(2)}) async-start(), calls=%async_computation.2 | async-start | bytes 1198080 | tf_op jit(solution)/shard_map/all_gather | solution.py:33
  1316.4 222.4 %all-reduce.7.cloned.1.call-start = ((), (), s32[]{:S(2)}) async-start(), calls=%async_computation.3 | async-start | bytes 2097152 | tf_op jit(solution)/shard_map/psum | solution.py:41
Sparse Core Ops, SparseCore 0:
  12.5 109.5 all-gather.2
  125.6 111.3 all-reduce.4
  240.9 1073.9 all-reduce.8
  1320.7 102.8 all-gather.4
  1427.3 111.4 all-reduce.6
where the time goes:
time: 1550 us
  waiting for transfers between devices  1490 us (96%)
  blocking collectives  22.6 us (1%)
    unnamed x6, waiting for transfers between devices  1070 us
    all_gather x1, waiting for transfers between devices, local(): all_rows = lax.all_gather(activations, 'lat', axis=0, tiled=True)  114 us
    psum x1, waiting for transfers between devices, local(): preact, summed_sq = lax.psum((block, squares), 'layer')  112 us
    all_gather x1, waiting for transfers between devices, local(): residual = lax.all_gather(mine, 'lat', axis=0, tiled=True)  107 us
    psum x1, waiting for transfers between devices, local(): lat_grad = lax.psum(back_part(residual, dec_weight), 'layer')  85.8 us
  transfers between devices with their start and end apart: 5, of which 5 were waited for; matrix products, arithmetic and copies ran while one was open for 0% of the time, Pallas kernels for 0%

commit v1 on v0

v1 whole, which is shorter than its diff:
```python
import jax
import jax.numpy as jnp
from jax import lax
from jax.sharding import Mesh
from jax.sharding import PartitionSpec as P

norm_eps = 1e-06
sparsity = 0.5
sharpness = 4.0
bf16, f32 = jnp.bfloat16, jnp.float32

LAYER = ("la", "lb", "lc")
LAT = ("x", "zhi", "y", "core")
PLANE = ("x", "y")
SWAP = ((0, 1), (1, 0))


def swap(x, axis):
    return lax.ppermute(x, axis, SWAP)


def spread(block, plane):
    return lax.all_to_all(
        jnp.broadcast_to(block[None], (plane, *block.shape)), PLANE, 0, 0, tiled=True
    )


def pick(x, at, axis):
    return lax.dynamic_index_in_dim(x, at, axis, keepdims=False)


def in_order(mine, other, at, axis):
    first = jnp.where(at == 0, mine, other)
    second = jnp.where(at == 0, other, mine)
    return jnp.stack([first, second], axis=axis)


def split_sum(value):
    high = lax.reduce_precision(value, 8, 7)
    return jnp.stack([high, value - high], axis=0).astype(bf16)


def sum_over_layer(left, right, plane, rows, extra=None):
    lb, lc = lax.axis_index("lb"), lax.axis_index("lc")
    left = left.reshape(2, plane * 2 * rows, -1)

    def part(at):
        return jnp.dot(pick(left, at, 0), right, preferred_element_type=f32)

    def exchange(sent, axis, extra):
        shape = sent.shape
        sent = sent.reshape(-1, shape[-1]).astype(bf16)
        count = sent.shape[0]
        if extra is not None:
            tail = jnp.pad(split_sum(extra), ((0, 14), (0, 0)))
            sent = jnp.concatenate([sent, tail], axis=0)
        got = swap(sent, axis)
        if extra is not None:
            extra = extra + jnp.sum(got[count : count + 2].astype(f32), axis=0)
        return got[:count].astype(f32).reshape(shape), extra

    sent, kept = part(1 - lc), part(lc)
    got, extra = exchange(sent, "lc", extra)
    total = (kept + got).reshape(plane, 2, rows, -1)
    got, extra = exchange(pick(total, 1 - lb, 1), "lb", extra)
    total = pick(total, lb, 1) + got
    got, extra = exchange(total, "la", extra)
    return total + got, extra


def gather_over_layer(block):
    lb, lc = lax.axis_index("lb"), lax.axis_index("lc")
    half = in_order(block, swap(block, "lb"), lb, 1)
    return in_order(half, swap(half, "lc"), lc, 0).reshape(-1, block.shape[-1])


def gather_over_plane_and_core(block, plane):
    mine = spread(block, plane).reshape(-1, block.shape[-1])
    return jnp.concatenate([mine, swap(mine, "core")], axis=0)


def local(activations, enc_weight, enc_bias, dec_weight, dec_bias):
    rows, features = activations.shape
    plane = lax.axis_size("x") * lax.axis_size("y")
    both = jnp.concatenate([activations, swap(activations, "zhi")], axis=0)
    all_rows = gather_over_plane_and_core(both, plane)

    dec_f32 = dec_weight.astype(f32)
    squares = jnp.sum(dec_f32 * dec_f32, axis=1)
    preact, summed_sq = sum_over_layer(all_rows, enc_weight, plane, rows, squares)
    preact = preact + enc_bias
    dec_norm = jnp.sqrt(summed_sq + norm_eps)
    gating = jax.nn.sigmoid(sharpness * preact)
    latents = gather_over_layer((preact * gating).astype(bf16))

    half = plane * 2 * rows
    sent = jnp.dot(latents[half:], dec_weight, preferred_element_type=f32).astype(bf16)
    kept = jnp.dot(latents[:half], dec_weight, preferred_element_type=f32)
    part = (kept + swap(sent, "core").astype(f32)).astype(bf16)
    parts = lax.all_to_all(part.reshape(plane, 2 * rows, features), PLANE, 0, 0, tiled=True)
    part = jnp.sum(parts.astype(f32), axis=0)
    got = swap(part.astype(bf16), "zhi").astype(f32)
    rebuilt = part + jnp.concatenate([got[rows:], got[:rows]], axis=0)
    residual = (rebuilt + dec_bias - both.astype(f32)).astype(bf16)
    residual = gather_over_plane_and_core(residual, plane)

    lat_grad, _ = sum_over_layer(residual, dec_weight.T, plane, rows)
    lat_sums = jnp.sum(latents.astype(f32), axis=0)
    dec_grad = lax.dot_general(
        latents, residual, (((0,), (0,)), ((), ())), preferred_element_type=f32
    )
    dec_grad = dec_grad + (sparsity * lat_sums / dec_norm)[:, None] * dec_f32
    lat_grad = lat_grad + sparsity * dec_norm
    pre_grad = (lat_grad * (gating + sharpness * preact * gating * (1.0 - gating))).astype(bf16)
    pre_grad = gather_over_layer(pre_grad)
    enc_grad = lax.dot_general(
        all_rows, pre_grad, (((0,), (0,)), ((), ())), preferred_element_type=f32
    )
    return (enc_grad.astype(bf16), dec_grad.astype(bf16))


def solution(mesh):
    fine = Mesh(mesh.devices.reshape(2, 2, 2, 4, 2, 4, 2), (*LAYER, *LAT))
    return jax.shard_map(
        local,
        mesh=fine,
        in_specs=(P(LAT, LAYER), P(LAYER, LAT), P(LAT), P(LAT, LAYER), P(LAYER)),
        out_specs=(P(LAYER, LAT), P(LAT, LAYER)),
        check_vma=False,
    )
```

time: 1550 us -> 228 us (0.15)
  waiting for transfers between devices: 1490 us -> 88.7 us
  starting transfers between devices: 0.2 us -> 71 us
  blocking collectives: 22.6 us -> 43.9 us
    unnamed x6 -> x0, waiting for transfers between devices: 1070 us -> none
    all_gather x2 -> x0, waiting for transfers between devices: 221 us -> none  [the longest x1 114 us: local(): all_rows = lax.all_gather(activations, 'lat', axis=0, tiled=True)]
    psum x2 -> x0, waiting for transfers between devices: 198 us -> none  [the longest x1 112 us: local(): preact, summed_sq = lax.psum((block, squares), 'layer')]
    ppermute x0 -> x15, waiting for transfers between devices: none -> 88.7 us  [swap(): return lax.ppermute(x, axis, SWAP)]
    ppermute x0 -> x15, starting transfers between devices: none -> 71 us  [swap(): return lax.ppermute(x, axis, SWAP)]
    all_to_all x0 -> x3, blocking collectives: none -> 43.9 us  [the longest x2 29.5 us: spread(): lax.all_to_all(jnp.broadcast_to(block[None], (plane, *block.shape)), PLAN...]
    psum x1 -> x0, blocking collectives: 22.6 us -> none  [local(): preact, summed_sq = lax.psum((block, squares), 'layer')]
  transfers between devices with their start and end apart: 5 -> 15, of which waited for: 5 -> 15; matrix products, arithmetic and copies ran while one was open for 0% -> 1% of each run, Pallas kernels for 0% -> 0%
where the time goes in v1:
time: 228 us; the launch traced here: 227 us
  waiting for transfers between devices  88.7 us (39%)
  starting transfers between devices  71 us (31%)
  blocking collectives  43.9 us (19%)
  other arithmetic  9.18 us (4%)
  matrix products  7.96 us (3%)
  local copies, waits for them, and re-layouts  5.69 us (2%)
    ppermute x15, waiting for transfers between devices, swap(): return lax.ppermute(x, axis, SWAP)  88.7 us
    ppermute x15, starting transfers between devices, swap(): return lax.ppermute(x, axis, SWAP)  71 us
    all_to_all x2, blocking collectives, spread(): lax.all_to_all(jnp.broadcast_to(block[None], (plane, *block.shape)), PLAN...  29.5 us
    all_to_all x1, blocking collectives, local(): lax.all_to_all(part.reshape(plane, 2 * rows, features), PLANE, 0, 0, tile...  14.4 us
    unnamed x29, local copies, waits for them, and re-layouts  5.47 us
  transfers between devices with their start and end apart: 15, of which 15 were waited for; matrix products, arithmetic and copies ran while one was open for 1% of the time, Pallas kernels for 0%

profile of v1, /device:TPU:1, one launch (start us, length us, event | category | flops | bytes accessed | tf_op | source)
XLA Modules:
  0.0 227.5 jit_solution(13690472727327642495)
XLA Ops:
  0.7 16.4 %collective-permute-start = (bf16[8,1152]{1,0:T(8,128)(2,1)}, bf16[8,1152]{1,0:T(8,128)(2,1)S(1)}, u32[]{:S(2)}, u32[]{:S(2)}) collective-permute-start(bf16[8,1152]{1,0:T(8,128)(2,1)} %param.5), channel_id=1, source_target_pairs={{0,8},{8,0},{1,9},{9,1},{2,10},{10,2},{3,11},{11,3},{4,12},{12,4},... | collective-permute-start | bytes 55304 | tf_op jit(solution)/shard_map/ppermute | solution.py:19
  17.1 0.7 constant_dynamic-update-slice_fusion.1
  17.8 0.7 collective-permute-done
  18.5 0.6 copy-done.10
  19.2 16.9 %all_to_all.15 = bf16[16,16,1152]{2,1,0:T(8,128)(2,1)S(1)} all-to-all(bf16[16,16,1152]{2,1,0:T(8,128)(2,1)S(1)} %broadcast_in_dim.4), channel_id=1, replica_groups=mesh['la'=2,'lb'=2,'lc'=2,'x'=4,'zhi'=2,'y'=4,'core'=2] {'x','y'}, dimensions={0} | all-to-all | bytes 1179648 | tf_op jit(solution)/shard_map/all_to_all | solution.py:23
  36.1 4.7 %collective-permute-start.1 = (bf16[256,1152]{1,0:T(8,128)(2,1)S(1)}, bf16[256,1152]{1,0:T(8,128)(2,1)S(1)}, u32[]{:S(2)}, u32[]{:S(2)}) collective-permute-start(bf16[256,1152]{1,0:T(8,128)(2,1)S(1)} %bitcast.133), channel_id=1, source_target_pairs={{0,1},{1,0},{2,3},{3,2},{4,5},{5,4},{6,7},{7,6},{8,9},{9,8},{10,11... | collective-permute-start | bytes 1769480 | tf_op jit(solution)/shard_map/ppermute | solution.py:19
  40.8 0.3 fusion.2
  41.2 1.3 collective-permute-done.1
  42.4 0.1 pad_maximum_fusion
  42.5 0.7 copy-done.7
  43.3 0.5 convolution_convert_fusion.3
  43.8 0.5 copy-done.2
  44.3 2.5 %collective-permute-start.2 = (bf16[272,512]{1,0:T(8,128)(2,1)S(1)}, bf16[272,512]{1,0:T(8,128)(2,1)S(1)}, u32[]{:S(2)}, u32[]{:S(2)}) collective-permute-start(bf16[272,512]{1,0:T(8,128)(2,1)S(1)} %pad_maximum_fusion.4), channel_id=1, source_target_pairs={{0,64},{64,0},{1,65},{65,1},{2,66},{66,2},{3,67},{67,3},{4,68},{68... | collective-permute-start | bytes 835592 | tf_op jit(solution)/shard_map/ppermute | solution.py:19
  46.8 7.2 %collective-permute-done.2 = bf16[272,512]{1,0:T(8,128)(2,1)S(1)} collective-permute-done((bf16[272,512]{1,0:T(8,128)(2,1)S(1)}, bf16[272,512]{1,0:T(8,128)(2,1)S(1)}, u32[]{:S(2)}, u32[]{:S(2)}) %collective-permute-start.2) | collective-permute-done | bytes 278560 | tf_op jit(solution)/shard_map/ppermute | solution.py:19
  54.1 0.7 copy-done.9
  54.7 1.6 fusion.12
  56.4 0.7 pad_maximum_fusion.7
  57.1 3.0 %collective-permute-start.3 = (bf16[144,512]{1,0:T(8,128)(2,1)}, bf16[144,512]{1,0:T(8,128)(2,1)}, u32[]{:S(2)}, u32[]{:S(2)}) collective-permute-start(bf16[144,512]{1,0:T(8,128)(2,1)} %pad_maximum_fusion.7), channel_id=1, source_target_pairs={{0,128},{128,0},{1,129},{129,1},{2,130},{130,2},{3,131},{131,3},{4... | collective-permute-start | bytes 442376 | tf_op jit(solution)/shard_map/ppermute | solution.py:19
  60.1 8.6 %collective-permute-done.3 = bf16[144,512]{1,0:T(8,128)(2,1)} collective-permute-done((bf16[144,512]{1,0:T(8,128)(2,1)}, bf16[144,512]{1,0:T(8,128)(2,1)}, u32[]{:S(2)}, u32[]{:S(2)}) %collective-permute-start.3) | collective-permute-done | bytes 147488 | tf_op jit(solution)/shard_map/ppermute | solution.py:19
  68.7 0.7 convert_reduce_fusion.3
  69.4 0.9 fusion.22
  70.4 5.8 %collective-permute-start.4 = (bf16[144,512]{1,0:T(8,128)(2,1)S(1)}, bf16[144,512]{1,0:T(8,128)(2,1)S(1)}, u32[]{:S(2)}, u32[]{:S(2)}) collective-permute-start(bf16[144,512]{1,0:T(8,128)(2,1)S(1)} %pad_maximum_fusion.8), channel_id=1, source_target_pairs={{0,256},{256,0},{1,257},{257,1},{2,258},{258,2},{3,259},{259,3},{4... | collective-permute-start | bytes 442376 | tf_op jit(solution)/shard_map/ppermute | solution.py:19
  76.2 14.3 %collective-permute-done.4 = bf16[144,512]{1,0:T(8,128)(2,1)S(1)} collective-permute-done((bf16[144,512]{1,0:T(8,128)(2,1)S(1)}, bf16[144,512]{1,0:T(8,128)(2,1)S(1)}, u32[]{:S(2)}, u32[]{:S(2)}) %collective-permute-start.4) | collective-permute-done | bytes 147488 | tf_op jit(solution)/shard_map/ppermute | solution.py:19
  90.4 0.7 copy-done.5
  91.1 1.7 multiply_convert_fusion
  92.8 1.9 collective-permute-start.5
  94.7 5.7 %collective-permute-done.5 = bf16[16,8,512]{2,1,0:T(8,128)(2,1)} collective-permute-done((bf16[16,8,512]{2,1,0:T(8,128)(2,1)}, bf16[16,8,512]{2,1,0:T(8,128)(2,1)}, u32[]{:S(2)}, u32[]{:S(2)}) %collective-permute-start.5) | collective-permute-done | bytes 131104 | tf_op jit(solution)/shard_map/ppermute | solution.py:19
  100.4 1.2 select_bitcast_fusion.5
  101.6 0.6 copy-done.3
  102.3 0.7 pad_maximum_fusion.5
  103.0 1.9 collective-permute-start.6
  104.9 6.7 %collective-permute-done.6 = bf16[16,2,8,512]{3,2,1,0:T(8,128)(2,1)} collective-permute-done((bf16[16,2,8,512]{3,2,1,0:T(8,128)(2,1)}, bf16[16,2,8,512]{3,2,1,0:T(8,128)(2,1)}, u32[]{:S(2)}, u32[]{:S(2)}) %collective-permute-start.6) | collective-permute-done | bytes 262176 | tf_op jit(solution)/shard_map/ppermute | solution.py:19
  111.7 1.1 broadcast_select_fusion
  112.7 0.5 convolution_convert_fusion.1
  113.3 4.2 %collective-permute-start.7 = (bf16[256,1152]{1,0:T(8,128)(2,1)S(1)}, bf16[256,1152]{1,0:T(8,128)(2,1)S(1)}, u32[]{:S(2)}, u32[]{:S(2)}) collective-permute-start(bf16[256,1152]{1,0:T(8,128)(2,1)S(1)} %convolution_convert_fusion.1), channel_id=1, source_target_pairs={{0,1},{1,0},{2,3},{3,2},{4,5},{5,4},{6,7},{7,6},{8,9},{9,8},{10,11... | collective-permute-start | bytes 1769480 | tf_op jit(solution)/shard_map/ppermute | solution.py:19
  117.4 1.6 collective-permute-done.7
  119.0 0.5 fusion.1
  119.6 14.4 %all_to_all.16 = bf16[16,16,1152]{2,1,0:T(8,128)(2,1)S(1)} all-to-all(bf16[16,16,1152]{2,1,0:T(8,128)(2,1)S(1)} %bitcast.132), channel_id=1, replica_groups=mesh['la'=2,'lb'=2,'lc'=2,'x'=4,'zhi'=2,'y'=4,'core'=2] {'x','y'}, dimensions={0} | all-to-all | bytes 1179648 | tf_op jit(solution)/shard_map/all_to_all | solution.py:100
  134.0 0.1 convert_reduce_fusion
  134.1 11.2 %collective-permute-start.8 = (bf16[16,1152]{1,0:T(8,128)(2,1)S(1)}, bf16[16,1152]{1,0:T(8,128)(2,1)S(1)}, u32[]{:S(2)}, u32[]{:S(2)}) collective-permute-start(bf16[16,1152]{1,0:T(8,128)(2,1)S(1)} %convert_element_type.119), channel_id=1, source_target_pairs={{0,8},{8,0},{1,9},{9,1},{2,10},{10,2},{3,11},{11,3},{4,12},{12,4},... | collective-permute-start | bytes 110600 | tf_op jit(solution)/shard_map/ppermute | solution.py:19
  145.3 2.3 collective-permute-done.8
  147.7 12.6 %all_to_all.17 = bf16[16,16,1152]{2,1,0:T(8,128)(2,1)S(1)} all-to-all(bf16[16,16,1152]{2,1,0:T(8,128)(2,1)S(1)} %broadcast_in_dim.5), channel_id=1, replica_groups=mesh['la'=2,'lb'=2,'lc'=2,'x'=4,'zhi'=2,'y'=4,'core'=2] {'x','y'}, dimensions={0} | all-to-all | bytes 1179648 | tf_op jit(solution)/shard_map/all_to_all | solution.py:23
  160.2 5.8 %collective-permute-start.9 = (bf16[256,1152]{1,0:T(8,128)(2,1)S(1)}, bf16[256,1152]{1,0:T(8,128)(2,1)S(1)}, u32[]{:S(2)}, u32[]{:S(2)}) collective-permute-start(bf16[256,1152]{1,0:T(8,128)(2,1)S(1)} %bitcast.136), channel_id=1, source_target_pairs={{0,1},{1,0},{2,3},{3,2},{4,5},{5,4},{6,7},{7,6},{8,9},{9,8},{10,11... | collective-permute-start | bytes 1769480 | tf_op jit(solution)/shard_map/ppermute | solution.py:19
  166.1 1.6 collective-permute-done.9
  167.7 0.1 pad_maximum_fusion.1
  167.8 0.5 convolution_convert_fusion.2
  168.3 2.3 %collective-permute-start.10 = (bf16[256,512]{1,0:T(8,128)(2,1)S(1)}, bf16[256,512]{1,0:T(8,128)(2,1)S(1)}, u32[]{:S(2)}, u32[]{:S(2)}) collective-permute-start(bf16[256,512]{1,0:T(8,128)(2,1)S(1)} %convolution_convert_fusion.2), channel_id=1, source_target_pairs={{0,64},{64,0},{1,65},{65,1},{2,66},{66,2},{3,67},{67,3},{4,68},{68... | collective-permute-start | bytes 786440 | tf_op jit(solution)/shard_map/ppermute | solution.py:19
  170.7 0.1 convert_reduce_fusion.1
  170.8 6.9 %collective-permute-done.10 = bf16[256,512]{1,0:T(8,128)(2,1)S(1)} collective-permute-done((bf16[256,512]{1,0:T(8,128)(2,1)S(1)}, bf16[256,512]{1,0:T(8,128)(2,1)S(1)}, u32[]{:S(2)}, u32[]{:S(2)}) %collective-permute-start.10) | collective-permute-done | bytes 262176 | tf_op jit(solution)/shard_map/ppermute | solution.py:19
  177.7 0.5 fusion.6
  178.3 2.9 %collective-permute-start.11 = (bf16[128,512]{1,0:T(8,128)(2,1)S(1)}, bf16[128,512]{1,0:T(8,128)(2,1)S(1)}, u32[]{:S(2)}, u32[]{:S(2)}) collective-permute-start(bf16[128,512]{1,0:T(8,128)(2,1)S(1)} %fusion.30), channel_id=1, source_target_pairs={{0,128},{128,0},{1,129},{129,1},{2,130},{130,2},{3,131},{131,3},{4... | collective-permute-start | bytes 393224 | tf_op jit(solution)/shard_map/ppermute | solution.py:19
  181.3 7.9 %collective-permute-done.11 = bf16[128,512]{1,0:T(8,128)(2,1)S(1)} collective-permute-done((bf16[128,512]{1,0:T(8,128)(2,1)S(1)}, bf16[128,512]{1,0:T(8,128)(2,1)S(1)}, u32[]{:S(2)}, u32[]{:S(2)}) %collective-permute-start.11) | collective-permute-done | bytes 131104 | tf_op jit(solution)/shard_map/ppermute | solution.py:19
  189.2 4.5 %collective-permute-start.12 = (bf16[128,512]{1,0:T(8,128)(2,1)S(1)}, bf16[128,512]{1,0:T(8,128)(2,1)S(1)}, u32[]{:S(2)}, u32[]{:S(2)}) collective-permute-start(bf16[128,512]{1,0:T(8,128)(2,1)S(1)} %fusion.28), channel_id=1, source_target_pairs={{0,256},{256,0},{1,257},{257,1},{2,258},{258,2},{3,259},{259,3},{4... | collective-permute-start | bytes 393224 | tf_op jit(solution)/shard_map/ppermute | solution.py:19
  193.8 13.9 %collective-permute-done.12 = bf16[128,512]{1,0:T(8,128)(2,1)S(1)} collective-permute-done((bf16[128,512]{1,0:T(8,128)(2,1)S(1)}, bf16[128,512]{1,0:T(8,128)(2,1)S(1)}, u32[]{:S(2)}, u32[]{:S(2)}) %collective-permute-start.12) | collective-permute-done | bytes 131104 | tf_op jit(solution)/shard_map/ppermute | solution.py:19
  207.7 1.1 fusion.27
  208.8 1.9 collective-permute-start.13
  210.7 0.1 pad_maximum_fusion.3
  210.8 5.4 %collective-permute-done.13 = bf16[16,8,512]{2,1,0:T(8,128)(2,1)S(1)} collective-permute-done((bf16[16,8,512]{2,1,0:T(8,128)(2,1)S(1)}, bf16[16,8,512]{2,1,0:T(8,128)(2,1)S(1)}, u32[]{:S(2)}, u32[]{:S(2)}) %collective-permute-start.13) | collective-permute-done | bytes 131104 | tf_op jit(solution)/shard_map/ppermute | solution.py:19
  216.2 1.9 collective-permute-start.14
  218.1 1.9 fusion
  220.0 4.5 %collective-permute-done.14 = bf16[16,2,8,512]{3,2,0,1:T(8,128)(2,1)S(1)} collective-permute-done((bf16[16,2,8,512]{3,2,0,1:T(8,128)(2,1)S(1)}, bf16[16,2,8,512]{3,2,0,1:T(8,128)(2,1)S(1)}, u32[]{:S(2)}, u32[]{:S(2)}) %collective-permute-start.14) | collective-permute-done | bytes 262176 | tf_op jit(solution)/shard_map/ppermute | solution.py:19
  224.7 0.1 copy.10
  224.7 0.9 copy-done.8
  225.7 1.8 convolution_convert_fusion
  (47 shorter events, 0.6 us)
Async XLA Ops:
  0.6 42.6 %copy-start = (bf16[1152,512]{1,0:T(8,128)(2,1)S(1)}, bf16[1152,512]{1,0:T(8,128)(2,1)}, u32[]{:S(2)}) copy-start(bf16[1152,512]{1,0:T(8,128)(2,1)} %param.6) | copy-start | bytes 3538948
  0.6 40.2 %copy-start.1 = (bf16[512,1152]{1,0:T(8,128)(2,1)S(1)}, bf16[512,1152]{1,0:T(8,128)(2,1)}, u32[]{:S(2)}) copy-start(bf16[512,1152]{1,0:T(8,128)(2,1)} %param.8) | copy-start | bytes 3538948
  0.7 17.9 %collective-permute-start = (bf16[8,1152]{1,0:T(8,128)(2,1)}, bf16[8,1152]{1,0:T(8,128)(2,1)S(1)}, u32[]{:S(2)}, u32[]{:S(2)}) collective-permute-start(bf16[8,1152]{1,0:T(8,128)(2,1)} %param.5), channel_id=1, source_target_pairs={{0,8},{8,0},{1,9},{9,1},{2,10},{10,2},{3,11},{11,3},{4,12},{12,4},... | collective-permute-start | bytes 55304 | tf_op jit(solution)/shard_map/ppermute | solution.py:19
  18.5 0.6 copy-start.10
  36.1 6.4 %collective-permute-start.1 = (bf16[256,1152]{1,0:T(8,128)(2,1)S(1)}, bf16[256,1152]{1,0:T(8,128)(2,1)S(1)}, u32[]{:S(2)}, u32[]{:S(2)}) collective-permute-start(bf16[256,1152]{1,0:T(8,128)(2,1)S(1)} %bitcast.133), channel_id=1, source_target_pairs={{0,1},{1,0},{2,3},{3,2},{4,5},{5,4},{6,7},{7,6},{8,9},{9,8},{10,11... | collective-permute-start | bytes 1769480 | tf_op jit(solution)/shard_map/ppermute | solution.py:19
  42.4 0.8 copy-start.7
  43.2 1.0 copy-start.2
  44.3 9.8 %collective-permute-start.2 = (bf16[272,512]{1,0:T(8,128)(2,1)S(1)}, bf16[272,512]{1,0:T(8,128)(2,1)S(1)}, u32[]{:S(2)}, u32[]{:S(2)}) collective-permute-start(bf16[272,512]{1,0:T(8,128)(2,1)S(1)} %pad_maximum_fusion.4), channel_id=1, source_target_pairs={{0,64},{64,0},{1,65},{65,1},{2,66},{66,2},{3,67},{67,3},{4,68},{68... | collective-permute-start | bytes 835592 | tf_op jit(solution)/shard_map/ppermute | solution.py:19
  54.0 0.7 copy-start.9
  56.4 34.7 %copy-start.12 = (f32[512]{0:T(512)S(1)}, f32[512]{0:T(512)}, u32[]{:S(2)}) copy-start(f32[512]{0:T(512)} %param.7) | copy-start | bytes 6148
  57.1 11.6 %collective-permute-start.3 = (bf16[144,512]{1,0:T(8,128)(2,1)}, bf16[144,512]{1,0:T(8,128)(2,1)}, u32[]{:S(2)}, u32[]{:S(2)}) collective-permute-start(bf16[144,512]{1,0:T(8,128)(2,1)} %pad_maximum_fusion.7), channel_id=1, source_target_pairs={{0,128},{128,0},{1,129},{129,1},{2,130},{130,2},{3,131},{131,3},{4... | collective-permute-start | bytes 442376 | tf_op jit(solution)/shard_map/ppermute | solution.py:19
  70.4 20.0 %collective-permute-start.4 = (bf16[144,512]{1,0:T(8,128)(2,1)S(1)}, bf16[144,512]{1,0:T(8,128)(2,1)S(1)}, u32[]{:S(2)}, u32[]{:S(2)}) collective-permute-start(bf16[144,512]{1,0:T(8,128)(2,1)S(1)} %pad_maximum_fusion.8), channel_id=1, source_target_pairs={{0,256},{256,0},{1,257},{257,1},{2,258},{258,2},{3,259},{259,3},{4... | collective-permute-start | bytes 442376 | tf_op jit(solution)/shard_map/ppermute | solution.py:19
  90.4 0.7 copy-start.5
  92.8 7.7 %collective-permute-start.5 = (bf16[16,8,512]{2,1,0:T(8,128)(2,1)}, bf16[16,8,512]{2,1,0:T(8,128)(2,1)}, u32[]{:S(2)}, u32[]{:S(2)}) collective-permute-start(bf16[16,8,512]{2,1,0:T(8,128)(2,1)} %multiply_convert_fusion), channel_id=1, source_target_pairs={{0,128},{128,0},{1,129},{129,1},{2,130},{130,2},{3,131},{131,3},{4... | collective-permute-start | bytes 393224 | tf_op jit(solution)/shard_map/ppermute | solution.py:19
  101.6 0.6 copy-start.3
  101.6 1.4 copy-start.4
  103.0 8.7 %collective-permute-start.6 = (bf16[16,2,8,512]{3,2,1,0:T(8,128)(2,1)}, bf16[16,2,8,512]{3,2,1,0:T(8,128)(2,1)}, u32[]{:S(2)}, u32[]{:S(2)}) collective-permute-start(bf16[16,2,8,512]{3,2,1,0:T(8,128)(2,1)} %pad_maximum_fusion.5), channel_id=1, source_target_pairs={{0,64},{64,0},{1,65},{65,1},{2,66},{66,2},{3,67},{67,3},{4,68},{68... | collective-permute-start | bytes 786440 | tf_op jit(solution)/shard_map/ppermute | solution.py:19
  113.3 5.8 %collective-permute-start.7 = (bf16[256,1152]{1,0:T(8,128)(2,1)S(1)}, bf16[256,1152]{1,0:T(8,128)(2,1)S(1)}, u32[]{:S(2)}, u32[]{:S(2)}) collective-permute-start(bf16[256,1152]{1,0:T(8,128)(2,1)S(1)} %convolution_convert_fusion.1), channel_id=1, source_target_pairs={{0,1},{1,0},{2,3},{3,2},{4,5},{5,4},{6,7},{7,6},{8,9},{9,8},{10,11... | collective-permute-start | bytes 1769480 | tf_op jit(solution)/shard_map/ppermute | solution.py:19
  119.6 28.0 %copy-start.11 = (bf16[16,1152]{1,0:T(8,128)(2,1)S(1)}, bf16[16,1152]{1,0:T(8,128)(2,1)}, u32[]{:S(2)}) copy-start(bf16[16,1152]{1,0:T(8,128)(2,1)} %copy-done.10) | copy-start | bytes 110596
  119.6 28.0 %copy-start.13 = (f32[1152]{0:T(1024)S(1)}, f32[1152]{0:T(1024)}, u32[]{:S(2)}) copy-start(f32[1152]{0:T(1024)} %param.9) | copy-start | bytes 13828
  134.1 13.4 %collective-permute-start.8 = (bf16[16,1152]{1,0:T(8,128)(2,1)S(1)}, bf16[16,1152]{1,0:T(8,128)(2,1)S(1)}, u32[]{:S(2)}, u32[]{:S(2)}) collective-permute-start(bf16[16,1152]{1,0:T(8,128)(2,1)S(1)} %convert_element_type.119), channel_id=1, source_target_pairs={{0,8},{8,0},{1,9},{9,1},{2,10},{10,2},{3,11},{11,3},{4,12},{12,4},... | collective-permute-start | bytes 110600 | tf_op jit(solution)/shard_map/ppermute | solution.py:19
  160.2 7.4 %collective-permute-start.9 = (bf16[256,1152]{1,0:T(8,128)(2,1)S(1)}, bf16[256,1152]{1,0:T(8,128)(2,1)S(1)}, u32[]{:S(2)}, u32[]{:S(2)}) collective-permute-start(bf16[256,1152]{1,0:T(8,128)(2,1)S(1)} %bitcast.136), channel_id=1, source_target_pairs={{0,1},{1,0},{2,3},{3,2},{4,5},{5,4},{6,7},{7,6},{8,9},{9,8},{10,11... | collective-permute-start | bytes 1769480 | tf_op jit(solution)/shard_map/ppermute | solution.py:19
  167.8 2.9 %copy-start.6 = (bf16[144,512]{1,0:T(8,128)(2,1)S(1)}, bf16[144,512]{1,0:T(8,128)(2,1)}, u32[]{:S(2)}) copy-start(bf16[144,512]{1,0:T(8,128)(2,1)} %copy-done.5) | copy-start | bytes 442372
  168.3 9.4 %collective-permute-start.10 = (bf16[256,512]{1,0:T(8,128)(2,1)S(1)}, bf16[256,512]{1,0:T(8,128)(2,1)S(1)}, u32[]{:S(2)}, u32[]{:S(2)}) collective-permute-start(bf16[256,512]{1,0:T(8,128)(2,1)S(1)} %convolution_convert_fusion.2), channel_id=1, source_target_pairs={{0,64},{64,0},{1,65},{65,1},{2,66},{66,2},{3,67},{67,3},{4,68},{68... | collective-permute-start | bytes 786440 | tf_op jit(solution)/shard_map/ppermute | solution.py:19
  178.3 10.9 %collective-permute-start.11 = (bf16[128,512]{1,0:T(8,128)(2,1)S(1)}, bf16[128,512]{1,0:T(8,128)(2,1)S(1)}, u32[]{:S(2)}, u32[]{:S(2)}) collective-permute-start(bf16[128,512]{1,0:T(8,128)(2,1)S(1)} %fusion.30), channel_id=1, source_target_pairs={{0,128},{128,0},{1,129},{129,1},{2,130},{130,2},{3,131},{131,3},{4... | collective-permute-start | bytes 393224 | tf_op jit(solution)/shard_map/ppermute | solution.py:19
  189.2 18.5 %collective-permute-start.12 = (bf16[128,512]{1,0:T(8,128)(2,1)S(1)}, bf16[128,512]{1,0:T(8,128)(2,1)S(1)}, u32[]{:S(2)}, u32[]{:S(2)}) collective-permute-start(bf16[128,512]{1,0:T(8,128)(2,1)S(1)} %fusion.28), channel_id=1, source_target_pairs={{0,256},{256,0},{1,257},{257,1},{2,258},{258,2},{3,259},{259,3},{4... | collective-permute-start | bytes 393224 | tf_op jit(solution)/shard_map/ppermute | solution.py:19
  208.8 7.4 %collective-permute-start.13 = (bf16[16,8,512]{2,1,0:T(8,128)(2,1)S(1)}, bf16[16,8,512]{2,1,0:T(8,128)(2,1)S(1)}, u32[]{:S(2)}, u32[]{:S(2)}) collective-permute-start(bf16[16,8,512]{2,1,0:T(8,128)(2,1)S(1)} %fusion.27), channel_id=1, source_target_pairs={{0,128},{128,0},{1,129},{129,1},{2,130},{130,2},{3,131},{131,3},{4... | collective-permute-start | bytes 393224 | tf_op jit(solution)/shard_map/ppermute | solution.py:19
  216.2 8.4 %collective-permute-start.14 = (bf16[16,2,8,512]{3,2,0,1:T(8,128)(2,1)S(1)}, bf16[16,2,8,512]{3,2,0,1:T(8,128)(2,1)S(1)}, u32[]{:S(2)}, u32[]{:S(2)}) collective-permute-start(bf16[16,2,8,512]{3,2,0,1:T(8,128)(2,1)S(1)} %pad_maximum_fusion.6), channel_id=1, source_target_pairs={{0,64},{64,0},{1,65},{65,1},{2,66},{66,2},{3,67},{67,3},{4,68},{68... | collective-permute-start | bytes 786440 | tf_op jit(solution)/shard_map/ppermute | solution.py:19
  224.6 1.1 copy-start.8

commit v2 on v1

v2 whole, which is shorter than its diff:
```python
import jax
import jax.numpy as jnp
from jax import lax
from jax.sharding import Mesh
from jax.sharding import PartitionSpec as P

norm_eps = 1e-06
sparsity = 0.5
sharpness = 4.0
bf16, f32 = jnp.bfloat16, jnp.float32

LAYER = ("la", "lb", "lc")
LAT = ("x", "zhi", "y", "core")
PLANE = ("x", "y")
SWAP = ((0, 1), (1, 0))

QUARTER = ("lc", "lb")


def swap(x, axis):
    return lax.ppermute(x, axis, SWAP)


def spread(block, plane):
    blocks = jnp.broadcast_to(block[None], (plane, *block.shape))
    return lax.all_to_all(blocks, PLANE, 0, 0, tiled=True).reshape(-1, block.shape[-1])


def in_order(mine, other, at):
    first = jnp.where(at == 0, mine, other)
    second = jnp.where(at == 0, other, mine)
    return jnp.concatenate([first, second], axis=0)


def dot(a, b, dims=((1,), (0,))):
    return lax.dot_general(a, b, (dims, ((), ())), preferred_element_type=f32)


def sum_over_layer(halves, extra=None):
    parts = jnp.concatenate([h.astype(bf16) for h in halves], axis=0).reshape(4, -1, halves[0].shape[-1])
    count = parts.shape[1]
    if extra is not None:
        tail = jnp.broadcast_to(extra.astype(bf16), (4, 8, *extra.shape))
        parts = jnp.concatenate([parts, tail], axis=1)
    total = jnp.sum(lax.all_to_all(parts, QUARTER, 0, 0, tiled=True).astype(f32), axis=0)
    total = total + swap(total.astype(bf16), "la").astype(f32)
    return (total[:count], total[count]) if extra is not None else total


def gather_over_layer(block):
    half = in_order(block, swap(block, "lb"), lax.axis_index("lb"))
    return half, swap(half, "lc")


def local(activations, enc_weight, enc_bias, dec_weight, dec_bias):
    rows, features = activations.shape
    plane = lax.axis_size("x") * lax.axis_size("y")
    lc = lax.axis_index("lc")

    def at(pair, index):
        return lax.dynamic_index_in_dim(jnp.stack(pair, axis=0), index, 0, keepdims=False)

    both = jnp.concatenate([activations, swap(activations, "zhi")], axis=0)
    near = spread(both, plane)
    acts = (near, swap(near, "core"))

    dec_f32 = dec_weight.astype(f32)
    squares = jnp.sum(dec_f32 * dec_f32, axis=1)
    preact, summed_sq = sum_over_layer([dot(a, enc_weight) for a in acts], squares)
    preact = preact + enc_bias
    dec_norm = jnp.sqrt(summed_sq + norm_eps)
    gating = jax.nn.sigmoid(sharpness * preact)
    latents, far_latents = gather_over_layer((preact * gating).astype(bf16))

    here, there = dot(latents, dec_weight), dot(far_latents, dec_weight)
    sent = jnp.where(lc == 1, here, there).astype(bf16)
    part = (jnp.where(lc == 1, there, here) + swap(sent, "core").astype(f32)).astype(bf16)
    parts = lax.all_to_all(part.reshape(plane, 2 * rows, features), PLANE, 0, 0, tiled=True)
    part = jnp.sum(parts.astype(f32), axis=0)
    got = swap(part.astype(bf16), "zhi").astype(f32)
    rebuilt = part + jnp.concatenate([got[rows:], got[:rows]], axis=0)
    near = spread((rebuilt + dec_bias - both.astype(f32)).astype(bf16), plane)
    residual = (near, swap(near, "core"))

    lat_grad = sum_over_layer([dot(r, dec_weight, ((1,), (1,))) for r in residual])
    lat_sums = jnp.sum(latents.astype(f32), axis=0) + jnp.sum(far_latents.astype(f32), axis=0)
    dec_grad = dot(latents, at(residual, lc), ((0,), (0,)))
    dec_grad = dec_grad + dot(far_latents, at(residual, 1 - lc), ((0,), (0,)))
    dec_grad = dec_grad + (sparsity * lat_sums / dec_norm)[:, None] * dec_f32
    lat_grad = lat_grad + sparsity * dec_norm
    pre_grad = (lat_grad * (gating + sharpness * preact * gating * (1.0 - gating))).astype(bf16)
    pre_grad, far_grad = gather_over_layer(pre_grad)
    enc_grad = dot(at(acts, 1 - lc), far_grad, ((0,), (0,)))
    enc_grad = enc_grad + dot(at(acts, lc), pre_grad, ((0,), (0,)))
    return (enc_grad.astype(bf16), dec_grad.astype(bf16))


def solution(mesh):
    fine = Mesh(mesh.devices.reshape(2, 2, 2, 4, 2, 4, 2), (*LAYER, *LAT))
    return jax.shard_map(
        local,
        mesh=fine,
        in_specs=(P(LAT, LAYER), P(LAYER, LAT), P(LAT), P(LAT, LAYER), P(LAYER)),
        out_specs=(P(LAYER, LAT), P(LAT, LAYER)),
        check_vma=False,
    )
```

time: 228 us -> 215 us (0.943)
  waiting for transfers between devices: 88.7 us -> 68 us
  blocking collectives: 43.9 us -> 61.4 us
  starting transfers between devices: 71 us -> 64.6 us
  local copies, waits for them, and re-layouts: 5.69 us -> 1.17 us
    ppermute x15 -> x11, waiting for transfers between devices: 88.7 us -> 57 us  [swap(): return lax.ppermute(x, axis, SWAP)]
    all_to_all x2 -> x3, blocking collectives: 29.5 us -> 46.9 us  [the longest x2 29.5 us: spread(): lax.all_to_all(blocks, PLANE, 0, 0, tiled=True).reshape(-1, block.shape[-1])]
    all_to_all x0 -> x1, waiting for transfers between devices: none -> 11 us  [sum_over_layer(): lax.all_to_all(parts, QUARTER, 0, 0, tiled=True).astype(f32)]
    ppermute x15 -> x11, starting transfers between devices: 71 us -> 60.4 us  [swap(): return lax.ppermute(x, axis, SWAP)]
    unnamed x29 -> x31, local copies, waits for them, and re-layouts: 5.47 us -> 1.07 us
    all_to_all x0 -> x1, starting transfers between devices: none -> 4.15 us  [sum_over_layer(): lax.all_to_all(parts, QUARTER, 0, 0, tiled=True).astype(f32)]
    reduce_sum x4, other arithmetic: 0.87 us -> 3.34 us  [the longest x2 1.3 us: sum_over_layer(): jnp.sum(lax.all_to_all(parts, QUARTER, 0, 0, tiled=True).astype(f32), axi...]
    convert_element_type x4 -> x5, other arithmetic: 2.66 us -> 0.31 us  [the longest x1 0.16 us: local(): (jnp.where(lc == 1, there, here) + swap(sent, 'core').astype(f32)).astype...]
  transfers between devices with their start and end apart: 15 -> 12, of which waited for: 15 -> 12; matrix products, arithmetic and copies ran while one was open for 1% -> 4% of each run, Pallas kernels for 0% -> 0%
where the time goes in v2:
time: 215 us; the launch traced here: 214 us
  waiting for transfers between devices  68 us (32%)
  starting transfers between devices  64.6 us (30%)
  blocking collectives  61.4 us (29%)
  matrix products  9.56 us (4%)
  other arithmetic  8.27 us (4%)
    ppermute x11, starting transfers between devices, swap(): return lax.ppermute(x, axis, SWAP)  60.4 us
    ppermute x11, waiting for transfers between devices, swap(): return lax.ppermute(x, axis, SWAP)  57 us
    all_to_all x2, blocking collectives, spread(): lax.all_to_all(blocks, PLANE, 0, 0, tiled=True).reshape(-1, block.shape[-1])  29.5 us
    all_to_all x1, blocking collectives, sum_over_layer(): lax.all_to_all(parts, QUARTER, 0, 0, tiled=True).astype(f32)  17.5 us
    all_to_all x1, blocking collectives, local(): lax.all_to_all(part.reshape(plane, 2 * rows, features), PLANE, 0, 0, tile...  14.4 us
    all_to_all x1, waiting for transfers between devices, sum_over_layer(): lax.all_to_all(parts, QUARTER, 0, 0, tiled=True).astype(f32)  11 us
    dot_general x10, matrix products, dot(): return lax.dot_general(a, b, (dims, ((), ())), preferred_element_type=f32)  9.56 us
  transfers between devices with their start and end apart: 12, of which 12 were waited for; matrix products, arithmetic and copies ran while one was open for 4% of the time, Pallas kernels for 0%

profile of v2, /device:TPU:1, one launch (start us, length us, event | category | flops | bytes accessed | tf_op | source)
XLA Modules:
  0.0 214.0 jit_solution(17674612240884708984)
XLA Ops:
  0.6 0.0 copy-start
  0.6 0.0 copy-start.1
  0.7 16.4 %collective-permute-start = (bf16[8,1152]{1,0:T(8,128)(2,1)}, bf16[8,1152]{1,0:T(8,128)(2,1)S(1)}, u32[]{:S(2)}, u32[]{:S(2)}) collective-permute-start(bf16[8,1152]{1,0:T(8,128)(2,1)} %param.5), channel_id=1, source_target_pairs={{0,8},{8,0},{1,9},{9,1},{2,10},{10,2},{3,11},{11,3},{4,12},{12,4},... | collective-permute-start | bytes 55304 | tf_op jit(solution)/shard_map/ppermute | solution.py:21
  17.1 0.7 constant_dynamic-update-slice_fusion.1
  17.8 0.7 collective-permute-done
  18.6 16.9 %all_to_all.25 = bf16[16,16,1152]{2,1,0:T(8,128)(2,1)S(1)} all-to-all(bf16[16,16,1152]{2,1,0:T(8,128)(2,1)S(1)} %broadcast_in_dim.6), channel_id=1, replica_groups=mesh['la'=2,'lb'=2,'lc'=2,'x'=4,'zhi'=2,'y'=4,'core'=2] {'x','y'}, dimensions={0} | all-to-all | bytes 1179648 | tf_op jit(solution)/shard_map/all_to_all | solution.py:26
  35.5 4.7 %collective-permute-start.1 = (bf16[256,1152]{1,0:T(8,128)(2,1)S(1)}, bf16[256,1152]{1,0:T(8,128)(2,1)S(1)}, u32[]{:S(2)}, u32[]{:S(2)}) collective-permute-start(bf16[256,1152]{1,0:T(8,128)(2,1)S(1)} %bitcast.36), channel_id=1, source_target_pairs={{0,1},{1,0},{2,3},{3,2},{4,5},{5,4},{6,7},{7,6},{8,9},{9,8},{10,11... | collective-permute-start | bytes 1769480 | tf_op jit(solution)/shard_map/ppermute | solution.py:21
  40.2 0.0 copy-done.1
  40.2 0.3 fusion.3
  40.5 0.0 copy-done
  40.5 0.5 convolution_convert_fusion.3
  41.0 0.8 collective-permute-done.1
  41.8 0.5 convolution_convert_fusion.2
  42.4 0.3 copy-done.8
  42.7 17.5 %all_to_all.26 = bf16[4,136,512]{2,1,0:T(8,128)(2,1)S(1)} all-to-all(bf16[4,136,512]{2,1,0:T(8,128)(2,1)S(1)} %pad_maximum_fusion), channel_id=1, replica_groups=mesh['la'=2,'lb'=2,'lc'=2,'x'=4,'zhi'=2,'y'=4,'core'=2] {'lc','lb'}, dimensions={0} | all-to-all | bytes 1114112 | tf_op jit(solution)/shard_map/all_to_all | solution.py:45
  60.1 0.1 convert_reduce_fusion.1
  60.2 8.0 %collective-permute-start.2 = (bf16[136,512]{1,0:T(8,128)(2,1)S(1)}, bf16[136,512]{1,0:T(8,128)(2,1)S(1)}, u32[]{:S(2)}, u32[]{:S(2)}) collective-permute-start(bf16[136,512]{1,0:T(8,128)(2,1)S(1)} %convert_element_type.91), channel_id=1, source_target_pairs={{0,256},{256,0},{1,257},{257,1},{2,258},{258,2},{3,259},{259,3},{4... | collective-permute-start | bytes 417800 | tf_op jit(solution)/shard_map/ppermute | solution.py:21
  68.3 12.6 %collective-permute-done.2 = bf16[136,512]{1,0:T(8,128)(2,1)S(1)} collective-permute-done((bf16[136,512]{1,0:T(8,128)(2,1)S(1)}, bf16[136,512]{1,0:T(8,128)(2,1)S(1)}, u32[]{:S(2)}, u32[]{:S(2)}) %collective-permute-start.2) | collective-permute-done | bytes 139296 | tf_op jit(solution)/shard_map/ppermute | solution.py:21
  81.0 0.0 copy-done.12
  81.0 0.0 copy-start.2
  81.0 0.1 multiply_convert_fusion.1
  81.1 1.9 collective-permute-start.3
  83.0 7.4 %collective-permute-done.3 = bf16[128,512]{1,0:T(8,128)(2,1)} collective-permute-done((bf16[128,512]{1,0:T(8,128)(2,1)S(1)}, bf16[128,512]{1,0:T(8,128)(2,1)}, u32[]{:S(2)}, u32[]{:S(2)}) %collective-permute-start.3) | collective-permute-done | bytes 131104 | tf_op jit(solution)/shard_map/ppermute | solution.py:21
  90.4 1.0 broadcast_select_fusion.3
  91.4 0.8 pad_maximum_fusion.3
  92.2 1.9 collective-permute-start.4
  94.1 7.7 %collective-permute-done.4 = bf16[256,512]{1,0:T(8,128)(2,1)} collective-permute-done((bf16[256,512]{1,0:T(8,128)(2,1)}, bf16[256,512]{1,0:T(8,128)(2,1)}, u32[]{:S(2)}, u32[]{:S(2)}) %collective-permute-start.4) | collective-permute-done | bytes 262176 | tf_op jit(solution)/shard_map/ppermute | solution.py:21
  101.8 1.5 fusion.32
  103.2 0.0 copy-done.2
  103.2 0.0 copy-done.4
  103.3 0.0 copy-done.6
  103.3 0.5 select_convert_fusion
  103.8 3.2 %collective-permute-start.5 = (bf16[256,1152]{1,0:T(8,128)(2,1)S(1)}, bf16[256,1152]{1,0:T(8,128)(2,1)S(1)}, u32[]{:S(2)}, u32[]{:S(2)}) collective-permute-start(bf16[256,1152]{1,0:T(8,128)(2,1)S(1)} %get-tuple-element.10), channel_id=1, source_target_pairs={{0,1},{1,0},{2,3},{3,2},{4,5},{5,4},{6,7},{7,6},{8,9},{9,8},{10,11... | collective-permute-start | bytes 1769480 | tf_op jit(solution)/shard_map/ppermute | solution.py:21
  107.0 1.6 collective-permute-done.5
  108.7 0.2 add_convert_fusion
  108.8 0.0 copy-start.13
  108.8 14.4 %all_to_all.27 = bf16[16,16,1152]{2,1,0:T(8,128)(2,1)S(1)} all-to-all(bf16[16,16,1152]{2,1,0:T(8,128)(2,1)S(1)} %bitcast.48), channel_id=1, replica_groups=mesh['la'=2,'lb'=2,'lc'=2,'x'=4,'zhi'=2,'y'=4,'core'=2] {'x','y'}, dimensions={0} | all-to-all | bytes 1179648 | tf_op jit(solution)/shard_map/all_to_all | solution.py:78
  123.3 0.1 convert_reduce_fusion
  123.4 9.4 %collective-permute-start.6 = (bf16[16,1152]{1,0:T(8,128)(2,1)S(1)}, bf16[16,1152]{1,0:T(8,128)(2,1)S(1)}, u32[]{:S(2)}, u32[]{:S(2)}) collective-permute-start(bf16[16,1152]{1,0:T(8,128)(2,1)S(1)} %convert_element_type.98), channel_id=1, source_target_pairs={{0,8},{8,0},{1,9},{9,1},{2,10},{10,2},{3,11},{11,3},{4,12},{12,4},... | collective-permute-start | bytes 110600 | tf_op jit(solution)/shard_map/ppermute | solution.py:21
  132.8 4.0 %collective-permute-done.6 = bf16[16,1152]{1,0:T(8,128)(2,1)S(1)} collective-permute-done((bf16[16,1152]{1,0:T(8,128)(2,1)S(1)}, bf16[16,1152]{1,0:T(8,128)(2,1)S(1)}, u32[]{:S(2)}, u32[]{:S(2)}) %collective-permute-start.6) | collective-permute-done | bytes 36896 | tf_op jit(solution)/shard_map/ppermute | solution.py:21
  136.9 12.6 %all_to_all.28 = bf16[16,16,1152]{2,1,0:T(8,128)(2,1)S(1)} all-to-all(bf16[16,16,1152]{2,1,0:T(8,128)(2,1)S(1)} %broadcast_in_dim.8), channel_id=1, replica_groups=mesh['la'=2,'lb'=2,'lc'=2,'x'=4,'zhi'=2,'y'=4,'core'=2] {'x','y'}, dimensions={0} | all-to-all | bytes 1179648 | tf_op jit(solution)/shard_map/all_to_all | solution.py:26
  149.5 5.8 %collective-permute-start.7 = (bf16[256,1152]{1,0:T(8,128)(2,1)S(1)}, bf16[256,1152]{1,0:T(8,128)(2,1)S(1)}, u32[]{:S(2)}, u32[]{:S(2)}) collective-permute-start(bf16[256,1152]{1,0:T(8,128)(2,1)S(1)} %bitcast.40), channel_id=1, source_target_pairs={{0,1},{1,0},{2,3},{3,2},{4,5},{5,4},{6,7},{7,6},{8,9},{9,8},{10,11... | collective-permute-start | bytes 1769480 | tf_op jit(solution)/shard_map/ppermute | solution.py:21
  155.3 0.5 convolution_convert_fusion.1
  155.8 1.1 collective-permute-done.7
  156.9 0.5 convolution_convert_fusion
  157.5 0.8 pad_maximum_fusion.2
  158.3 4.1 %all-to-all-start.4 = ((bf16[4,128,512]{2,1,0:T(8,128)(2,1)}), bf16[4,128,512]{2,1,0:T(8,128)(2,1)}, u32[]{:S(2)}, u32[]{:S(2)}) async-start(bf16[4,128,512]{2,1,0:T(8,128)(2,1)} %bitcast.49), calls=%async_computation.4 | async-start | bytes 1048576 | tf_op jit(solution)/shard_map/all_to_all | solution.py:45
  162.5 1.3 fusion.25
  163.8 1.0 convert_reduce_fusion.4
  164.8 1.0 convert_reduce_fusion.3
  165.8 11.0 %all-to-all-done.4 = bf16[4,128,512]{2,1,0:T(8,128)(2,1)} async-done(((bf16[4,128,512]{2,1,0:T(8,128)(2,1)}), bf16[4,128,512]{2,1,0:T(8,128)(2,1)}, u32[]{:S(2)}, u32[]{:S(2)}) %all-to-all-start.4) | async-done | bytes 524320 | tf_op jit(solution)/shard_map/all_to_all | solution.py:45
  176.8 1.2 convert_reduce_fusion.2
  178.0 5.0 %collective-permute-start.8 = (bf16[128,512]{1,0:T(8,128)(2,1)S(1)}, bf16[128,512]{1,0:T(8,128)(2,1)S(1)}, u32[]{:S(2)}, u32[]{:S(2)}) collective-permute-start(bf16[128,512]{1,0:T(8,128)(2,1)S(1)} %convert_element_type.105), channel_id=1, source_target_pairs={{0,256},{256,0},{1,257},{257,1},{2,258},{258,2},{3,259},{259,3},{4... | collective-permute-start | bytes 393224 | tf_op jit(solution)/shard_map/ppermute | solution.py:21
  183.0 13.2 %collective-permute-done.8 = bf16[128,512]{1,0:T(8,128)(2,1)S(1)} collective-permute-done((bf16[128,512]{1,0:T(8,128)(2,1)S(1)}, bf16[128,512]{1,0:T(8,128)(2,1)S(1)}, u32[]{:S(2)}, u32[]{:S(2)}) %collective-permute-start.8) | collective-permute-done | bytes 131104 | tf_op jit(solution)/shard_map/ppermute | solution.py:21
  196.3 0.2 multiply_convert_fusion
  196.4 1.9 collective-permute-start.9
  198.4 1.6 fusion.6
  200.0 3.8 %collective-permute-done.9 = bf16[128,512]{1,0:T(8,128)(2,1)S(1)} collective-permute-done((bf16[128,512]{1,0:T(8,128)(2,1)S(1)}, bf16[128,512]{1,0:T(8,128)(2,1)S(1)}, u32[]{:S(2)}, u32[]{:S(2)}) %collective-permute-start.9) | collective-permute-done | bytes 131104 | tf_op jit(solution)/shard_map/ppermute | solution.py:21
  203.9 0.0 copy-start.9
  203.9 2.1 collective-permute-start.10
  206.0 1.8 fusion.2
  207.8 0.6 fusion.13
  208.3 4.1 %collective-permute-done.10 = bf16[256,512]{1,0:T(8,128)(2,1)S(1)} collective-permute-done((bf16[256,512]{1,0:T(8,128)(2,1)S(1)}, bf16[256,512]{1,0:T(8,128)(2,1)S(1)}, u32[]{:S(2)}, u32[]{:S(2)}) %collective-permute-start.10) | collective-permute-done | bytes 262176 | tf_op jit(solution)/shard_map/ppermute | solution.py:21
  212.4 1.6 fusion.1
  (33 shorter events, 0.4 us)
Async XLA Ops:
  0.6 39.9 %copy-start = (bf16[1152,512]{1,0:T(8,128)(2,1)S(1)}, bf16[1152,512]{1,0:T(8,128)(2,1)}, u32[]{:S(2)}) copy-start(bf16[1152,512]{1,0:T(8,128)(2,1)} %param.6) | copy-start | bytes 3538948
  0.6 39.6 %copy-start.1 = (bf16[512,1152]{1,0:T(8,128)(2,1)S(1)}, bf16[512,1152]{1,0:T(8,128)(2,1)}, u32[]{:S(2)}) copy-start(bf16[512,1152]{1,0:T(8,128)(2,1)} %param.8) | copy-start | bytes 3538948
  0.7 17.9 %collective-permute-start = (bf16[8,1152]{1,0:T(8,128)(2,1)}, bf16[8,1152]{1,0:T(8,128)(2,1)S(1)}, u32[]{:S(2)}, u32[]{:S(2)}) collective-permute-start(bf16[8,1152]{1,0:T(8,128)(2,1)} %param.5), channel_id=1, source_target_pairs={{0,8},{8,0},{1,9},{9,1},{2,10},{10,2},{3,11},{11,3},{4,12},{12,4},... | collective-permute-start | bytes 55304 | tf_op jit(solution)/shard_map/ppermute | solution.py:21
  35.5 6.4 %collective-permute-start.1 = (bf16[256,1152]{1,0:T(8,128)(2,1)S(1)}, bf16[256,1152]{1,0:T(8,128)(2,1)S(1)}, u32[]{:S(2)}, u32[]{:S(2)}) collective-permute-start(bf16[256,1152]{1,0:T(8,128)(2,1)S(1)} %bitcast.36), channel_id=1, source_target_pairs={{0,1},{1,0},{2,3},{3,2},{4,5},{5,4},{6,7},{7,6},{8,9},{9,8},{10,11... | collective-permute-start | bytes 1769480 | tf_op jit(solution)/shard_map/ppermute | solution.py:21
  41.8 0.8 copy-start.8
  60.1 20.8 %copy-start.12 = (f32[512]{0:T(512)S(1)}, f32[512]{0:T(512)}, u32[]{:S(2)}) copy-start(f32[512]{0:T(512)} %param.7) | copy-start | bytes 6148
  60.2 20.7 %collective-permute-start.2 = (bf16[136,512]{1,0:T(8,128)(2,1)S(1)}, bf16[136,512]{1,0:T(8,128)(2,1)S(1)}, u32[]{:S(2)}, u32[]{:S(2)}) collective-permute-start(bf16[136,512]{1,0:T(8,128)(2,1)S(1)} %convert_element_type.91), channel_id=1, source_target_pairs={{0,256},{256,0},{1,257},{257,1},{2,258},{258,2},{3,259},{259,3},{4... | collective-permute-start | bytes 417800 | tf_op jit(solution)/shard_map/ppermute | solution.py:21
  81.0 22.3 %copy-start.2 = (f32[136,512]{1,0:T(8,128)}, f32[136,512]{1,0:T(8,128)S(1)}, u32[]{:S(2)}) copy-start(f32[136,512]{1,0:T(8,128)S(1)} %convert_add_fusion) | copy-start | bytes 835588
  81.1 9.3 %collective-permute-start.3 = (bf16[128,512]{1,0:T(8,128)(2,1)S(1)}, bf16[128,512]{1,0:T(8,128)(2,1)}, u32[]{:S(2)}, u32[]{:S(2)}) collective-permute-start(bf16[128,512]{1,0:T(8,128)(2,1)S(1)} %multiply_convert_fusion.1), channel_id=1, source_target_pairs={{0,128},{128,0},{1,129},{129,1},{2,130},{130,2},{3,131},{131,3},{4... | collective-permute-start | bytes 393224 | tf_op jit(solution)/shard_map/ppermute | solution.py:21
  91.4 11.8 %copy-start.4 = (bf16[128,512]{1,0:T(8,128)(2,1)}, bf16[128,512]{1,0:T(8,128)(2,1)S(1)}, u32[]{:S(2)}) copy-start(bf16[128,512]{1,0:T(8,128)(2,1)S(1)} %get-tuple-element.6) | copy-start | bytes 393220
  91.4 11.8 %copy-start.6 = (bf16[128,512]{1,0:T(8,128)(2,1)}, bf16[128,512]{1,0:T(8,128)(2,1)S(1)}, u32[]{:S(2)}) copy-start(bf16[128,512]{1,0:T(8,128)(2,1)S(1)} %get-tuple-element.7) | copy-start | bytes 393220
  92.2 9.6 %collective-permute-start.4 = (bf16[256,512]{1,0:T(8,128)(2,1)}, bf16[256,512]{1,0:T(8,128)(2,1)}, u32[]{:S(2)}, u32[]{:S(2)}) collective-permute-start(bf16[256,512]{1,0:T(8,128)(2,1)} %pad_maximum_fusion.3), channel_id=1, source_target_pairs={{0,64},{64,0},{1,65},{65,1},{2,66},{66,2},{3,67},{67,3},{4,68},{68... | collective-permute-start | bytes 786440 | tf_op jit(solution)/shard_map/ppermute | solution.py:21
  103.8 4.9 %collective-permute-start.5 = (bf16[256,1152]{1,0:T(8,128)(2,1)S(1)}, bf16[256,1152]{1,0:T(8,128)(2,1)S(1)}, u32[]{:S(2)}, u32[]{:S(2)}) collective-permute-start(bf16[256,1152]{1,0:T(8,128)(2,1)S(1)} %get-tuple-element.10), channel_id=1, source_target_pairs={{0,1},{1,0},{2,3},{3,2},{4,5},{5,4},{6,7},{7,6},{8,9},{9,8},{10,11... | collective-permute-start | bytes 1769480 | tf_op jit(solution)/shard_map/ppermute | solution.py:21
  108.8 28.0 %copy-start.13 = (f32[1152]{0:T(1024)S(1)}, f32[1152]{0:T(1024)}, u32[]{:S(2)}) copy-start(f32[1152]{0:T(1024)} %param.9) | copy-start | bytes 13828
  123.4 13.4 %collective-permute-start.6 = (bf16[16,1152]{1,0:T(8,128)(2,1)S(1)}, bf16[16,1152]{1,0:T(8,128)(2,1)S(1)}, u32[]{:S(2)}, u32[]{:S(2)}) collective-permute-start(bf16[16,1152]{1,0:T(8,128)(2,1)S(1)} %convert_element_type.98), channel_id=1, source_target_pairs={{0,8},{8,0},{1,9},{9,1},{2,10},{10,2},{3,11},{11,3},{4,12},{12,4},... | collective-permute-start | bytes 110600 | tf_op jit(solution)/shard_map/ppermute | solution.py:21
  149.5 7.4 %collective-permute-start.7 = (bf16[256,1152]{1,0:T(8,128)(2,1)S(1)}, bf16[256,1152]{1,0:T(8,128)(2,1)S(1)}, u32[]{:S(2)}, u32[]{:S(2)}) collective-permute-start(bf16[256,1152]{1,0:T(8,128)(2,1)S(1)} %bitcast.40), channel_id=1, source_target_pairs={{0,1},{1,0},{2,3},{3,2},{4,5},{5,4},{6,7},{7,6},{8,9},{9,8},{10,11... | collective-permute-start | bytes 1769480 | tf_op jit(solution)/shard_map/ppermute | solution.py:21
  156.9 1.4 copy-start.10
  158.3 18.5 %all-to-all-start.4 = ((bf16[4,128,512]{2,1,0:T(8,128)(2,1)}), bf16[4,128,512]{2,1,0:T(8,128)(2,1)}, u32[]{:S(2)}, u32[]{:S(2)}) async-start(bf16[4,128,512]{2,1,0:T(8,128)(2,1)} %bitcast.49), calls=%async_computation.4 | async-start | bytes 1048576 | tf_op jit(solution)/shard_map/all_to_all | solution.py:45
  176.8 6.2 %copy-start.14 = (f32[1,512]{1,0:T(1,128)S(1)}, f32[1,512]{1,0:T(1,128)}, u32[]{:S(2)}) copy-start(f32[1,512]{1,0:T(1,128)} %get-tuple-element.2) | copy-start | bytes 6148
  176.8 19.5 %copy-start.3 = (f32[136,512]{1,0:T(8,128)S(1)}, f32[136,512]{1,0:T(8,128)}, u32[]{:S(2)}) copy-start(f32[136,512]{1,0:T(8,128)} %copy-done.2) | copy-start | bytes 835588
  176.8 21.6 %copy-start.11 = (bf16[256,1152]{1,0:T(8,128)(2,1)S(1)}, bf16[256,1152]{1,0:T(8,128)(2,1)}, u32[]{:S(2)}) copy-start(bf16[256,1152]{1,0:T(8,128)(2,1)} %copy-done.10) | copy-start | bytes 1769476
  178.0 18.2 %collective-permute-start.8 = (bf16[128,512]{1,0:T(8,128)(2,1)S(1)}, bf16[128,512]{1,0:T(8,128)(2,1)S(1)}, u32[]{:S(2)}, u32[]{:S(2)}) collective-permute-start(bf16[128,512]{1,0:T(8,128)(2,1)S(1)} %convert_element_type.105), channel_id=1, source_target_pairs={{0,256},{256,0},{1,257},{257,1},{2,258},{258,2},{3,259},{259,3},{4... | collective-permute-start | bytes 393224 | tf_op jit(solution)/shard_map/ppermute | solution.py:21
  196.4 7.4 %collective-permute-start.9 = (bf16[128,512]{1,0:T(8,128)(2,1)S(1)}, bf16[128,512]{1,0:T(8,128)(2,1)S(1)}, u32[]{:S(2)}, u32[]{:S(2)}) collective-permute-start(bf16[128,512]{1,0:T(8,128)(2,1)S(1)} %multiply_convert_fusion), channel_id=1, source_target_pairs={{0,128},{128,0},{1,129},{129,1},{2,130},{130,2},{3,131},{131,3},{4... | collective-permute-start | bytes 393224 | tf_op jit(solution)/shard_map/ppermute | solution.py:21
  198.3 7.6 %copy-start.5 = (bf16[128,512]{1,0:T(8,128)(2,1)S(1)}, bf16[128,512]{1,0:T(8,128)(2,1)}, u32[]{:S(2)}) copy-start(bf16[128,512]{1,0:T(8,128)(2,1)} %copy-done.4) | copy-start | bytes 393220
  198.4 7.6 %copy-start.7 = (bf16[128,512]{1,0:T(8,128)(2,1)S(1)}, bf16[128,512]{1,0:T(8,128)(2,1)}, u32[]{:S(2)}) copy-start(bf16[128,512]{1,0:T(8,128)(2,1)} %copy-done.6) | copy-start | bytes 393220
  203.9 3.9 %copy-start.9 = (bf16[256,1152]{1,0:T(8,128)(2,1)S(1)}, bf16[256,1152]{1,0:T(8,128)(2,1)}, u32[]{:S(2)}) copy-start(bf16[256,1152]{1,0:T(8,128)(2,1)} %copy-done.8) | copy-start | bytes 1769476
  203.9 8.5 %collective-permute-start.10 = (bf16[256,512]{1,0:T(8,128)(2,1)S(1)}, bf16[256,512]{1,0:T(8,128)(2,1)S(1)}, u32[]{:S(2)}, u32[]{:S(2)}) collective-permute-start(bf16[256,512]{1,0:T(8,128)(2,1)S(1)} %pad_maximum_fusion.4), channel_id=1, source_target_pairs={{0,64},{64,0},{1,65},{65,1},{2,66},{66,2},{3,67},{67,3},{4,68},{68... | collective-permute-start | bytes 786440 | tf_op jit(solution)/shard_map/ppermute | solution.py:21

commit v3 on v2

v3 whole, which is shorter than its diff:
```python
import jax
import jax.numpy as jnp
from jax import lax
from jax.sharding import Mesh
from jax.sharding import PartitionSpec as P

norm_eps = 1e-06
sparsity = 0.5
sharpness = 4.0
bf16, f32 = jnp.bfloat16, jnp.float32

LAYER = ("la", "lb", "lc")
LAT = ("x", "zhi", "y", "core")
PLANE = ("x", "y")
SWAP = ((0, 1), (1, 0))

QUARTER = ("lc", "lb")


def swap(x, axis):
    return lax.ppermute(x, axis, SWAP)


def spread(block, plane):
    blocks = jnp.broadcast_to(block[None], (plane, *block.shape))
    return lax.all_to_all(blocks, PLANE, 0, 0, tiled=True).reshape(-1, block.shape[-1])


def in_order(mine, other, at, axis):
    first = jnp.where(at == 0, mine, other)
    second = jnp.where(at == 0, other, mine)
    return jnp.concatenate([first, second], axis=axis)


def dot(a, b, dims=((1,), (0,))):
    return lax.dot_general(a, b, (dims, ((), ())), preferred_element_type=f32)


def sum_over_layer(sides, tail=None):
    parts = [s.astype(bf16).reshape(4, -1, s.shape[-1]) for s in sides]
    if tail is not None:
        parts.append(jnp.broadcast_to(tail.astype(bf16), (4, *tail.shape)))
    parts = jnp.concatenate(parts, axis=1)
    total = jnp.sum(lax.all_to_all(parts, QUARTER, 0, 0, tiled=True).astype(f32), axis=0)
    return total + swap(total.astype(bf16), "la").astype(f32)


def gather_over_layer(block):
    half = in_order(block, swap(block, "lb"), lax.axis_index("lb"), 1)
    return half, swap(half, "lc")


def local(activations, enc_weight, enc_bias, dec_weight, dec_bias):
    rows, features = activations.shape
    plane = lax.axis_size("x") * lax.axis_size("y")
    lc = lax.axis_index("lc")
    count = plane * 2 * rows

    both = jnp.concatenate([activations, swap(activations, "zhi")], axis=0)
    acts = spread(both, plane)
    enc_other = swap(enc_weight, "core")
    dec = (dec_weight, swap(dec_weight, "core"))
    bias = jnp.stack([enc_bias, swap(enc_bias, "core")])[:, None, :]
    far_acts = swap(acts, "core")

    dec_f32 = [d.astype(f32) for d in dec]
    squares = jnp.pad(jnp.stack([jnp.sum(d * d, axis=1) for d in dec_f32]), ((0, 6), (0, 0)))
    total = sum_over_layer([dot(acts, enc_weight), dot(acts, enc_other)], squares)
    preact = total[: count // 2].reshape(2, count // 4, -1) + bias
    dec_norm = jnp.sqrt(total[count // 2 : count // 2 + 2] + norm_eps)
    gating = jax.nn.sigmoid(sharpness * preact)
    latents = gather_over_layer((preact * gating).astype(bf16))

    def decode(half):
        return (dot(half[0], dec[0]) + dot(half[1], dec[1])).astype(bf16)

    part = in_order(decode(latents[0]), decode(latents[1]), lc, 0)
    parts = lax.all_to_all(part.reshape(plane, 2 * rows, features), PLANE, 0, 0, tiled=True)
    part = jnp.sum(parts.astype(f32), axis=0)
    got = swap(part.astype(bf16), "zhi").astype(f32)
    rebuilt = part + jnp.concatenate([got[rows:], got[:rows]], axis=0)
    residual = spread((rebuilt + dec_bias - both.astype(f32)).astype(bf16), plane)

    lat_grad = sum_over_layer([dot(residual, d, ((1,), (1,))) for d in dec])
    lat_grad = lat_grad.reshape(2, count // 4, -1) + sparsity * dec_norm[:, None, :]

    latents = in_order(*latents, lc, 1)
    lat_sums = jnp.sum(latents.astype(f32), axis=1)
    dec_grads = [
        dot(latents[i], residual, ((0,), (0,))) + (sparsity * lat_sums[i] / dec_norm[i])[:, None] * dec_f32[i]
        for i in (0, 1)
    ]
    dec_grad = dec_grads[0] + swap(dec_grads[1].astype(bf16), "core").astype(f32)

    pre_grad = (lat_grad * (gating + sharpness * preact * gating * (1.0 - gating))).astype(bf16)
    pre_grad = jnp.stack([pre_grad[0], swap(pre_grad[1], "core")])
    near_grad, far_grad = gather_over_layer(pre_grad)
    half = count // 2
    all_acts = jnp.stack(
        [jnp.concatenate([a[i * half : (i + 1) * half] for a in (acts, far_acts)]) for i in (0, 1)]
    )

    def encode(index, grad):
        rows = lax.dynamic_index_in_dim(all_acts, index, 0, keepdims=False)
        return dot(rows, grad.reshape(count, -1), ((0,), (0,)))

    enc_grad = encode(1 - lc, far_grad)
    enc_grad = enc_grad + encode(lc, near_grad)
    return (enc_grad.astype(bf16), dec_grad.astype(bf16))


def solution(mesh):
    fine = Mesh(mesh.devices.reshape(2, 2, 2, 4, 2, 4, 2), (*LAYER, *LAT))
    return jax.shard_map(
        local,
        mesh=fine,
        in_specs=(P(LAT, LAYER), P(LAYER, LAT), P(LAT), P(LAT, LAYER), P(LAYER)),
        out_specs=(P(LAYER, LAT), P(LAT, LAYER)),
        check_vma=False,
    )
```

time: 215 us -> 206 us (0.958)
  blocking collectives: 61.4 us -> 42.3 us
  starting transfers between devices: 64.6 us -> 80.5 us
  waiting for transfers between devices: 68 us -> 58.7 us
  local copies, waits for them, and re-layouts: 1.17 us -> 4.43 us
  matrix products: 9.56 us -> 12.6 us
  other arithmetic: 8.27 us -> 5.33 us
    all_to_all x2 -> x1, blocking collectives: 29.5 us -> 12.4 us  [spread(): lax.all_to_all(blocks, PLANE, 0, 0, tiled=True).reshape(-1, block.shape[-1])]
    all_to_all x1, waiting for transfers between devices: 11 us -> 0.01 us  [sum_over_layer(): lax.all_to_all(parts, QUARTER, 0, 0, tiled=True).astype(f32)]
    all_to_all x0 -> x1, waiting for transfers between devices: none -> 10.6 us  [spread(): lax.all_to_all(blocks, PLANE, 0, 0, tiled=True).reshape(-1, block.shape[-1])]
    ppermute x11 -> x14, starting transfers between devices: 60.4 us -> 69.6 us  [swap(): return lax.ppermute(x, axis, SWAP)]
    ppermute x11 -> x14, waiting for transfers between devices: 57 us -> 48.1 us  [swap(): return lax.ppermute(x, axis, SWAP)]
    all_to_all x0 -> x1, starting transfers between devices: none -> 6.75 us  [spread(): lax.all_to_all(blocks, PLANE, 0, 0, tiled=True).reshape(-1, block.shape[-1])]
    dot_general x10 -> x12, matrix products: 9.56 us -> 12.6 us  [dot(): return lax.dot_general(a, b, (dims, ((), ())), preferred_element_type=f32)]
  transfers between devices with their start and end apart: 12 -> 16, of which waited for: 12 -> 10; matrix products, arithmetic and copies ran while one was open for 4% -> 7% of each run, Pallas kernels for 0% -> 0%
where the time goes in v3:
time: 206 us; the launch traced here: 205 us
  starting transfers between devices  80.5 us (39%)
  waiting for transfers between devices  58.7 us (28%)
  blocking collectives  42.3 us (21%)
  matrix products  12.6 us (6%)
  other arithmetic  5.33 us (3%)
  local copies, waits for them, and re-layouts  4.43 us (2%)
    ppermute x14, starting transfers between devices, swap(): return lax.ppermute(x, axis, SWAP)  69.6 us
    ppermute x14, waiting for transfers between devices, swap(): return lax.ppermute(x, axis, SWAP)  48.1 us
    all_to_all x1, blocking collectives, sum_over_layer(): lax.all_to_all(parts, QUARTER, 0, 0, tiled=True).astype(f32)  16.9 us
    all_to_all x1, blocking collectives, local(): lax.all_to_all(part.reshape(plane, 2 * rows, features), PLANE, 0, 0, tile...  13 us
    dot_general x12, matrix products, dot(): return lax.dot_general(a, b, (dims, ((), ())), preferred_element_type=f32)  12.6 us
    all_to_all x1, blocking collectives, spread(): lax.all_to_all(blocks, PLANE, 0, 0, tiled=True).reshape(-1, block.shape[-1])  12.4 us
    all_to_all x1, waiting for transfers between devices, spread(): lax.all_to_all(blocks, PLANE, 0, 0, tiled=True).reshape(-1, block.shape[-1])  10.6 us
    all_to_all x1, starting transfers between devices, spread(): lax.all_to_all(blocks, PLANE, 0, 0, tiled=True).reshape(-1, block.shape[-1])  6.75 us
  transfers between devices with their start and end apart: 16, of which 10 were waited for; matrix products, arithmetic and copies ran while one was open for 7% of the time, Pallas kernels for 0%

profile of v3, /device:TPU:1, one launch (start us, length us, event | category | flops | bytes accessed | tf_op | source)
XLA Modules:
  0.0 205.2 jit_solution(3244725241885134228)
XLA Ops:
  0.6 16.4 %collective-permute-start = (bf16[8,1152]{1,0:T(8,128)(2,1)}, bf16[8,1152]{1,0:T(8,128)(2,1)S(1)}, u32[]{:S(2)}, u32[]{:S(2)}) collective-permute-start(bf16[8,1152]{1,0:T(8,128)(2,1)} %param.5), channel_id=1, source_target_pairs={{0,8},{8,0},{1,9},{9,1},{2,10},{10,2},{3,11},{11,3},{4,12},{12,4},... | collective-permute-start | bytes 55304 | tf_op jit(solution)/shard_map/ppermute | solution.py:21
  17.1 2.9 %collective-permute-start.2 = (bf16[1152,512]{1,0:T(8,128)(2,1)}, bf16[1152,512]{1,0:T(8,128)(2,1)}, u32[]{:S(2)}, u32[]{:S(2)}) collective-permute-start(bf16[1152,512]{1,0:T(8,128)(2,1)} %param.6), channel_id=1, source_target_pairs={{0,1},{1,0},{2,3},{3,2},{4,5},{5,4},{6,7},{7,6},{8,9},{9,8},{10,11... | collective-permute-start | bytes 3538952 | tf_op jit(solution)/shard_map/ppermute | solution.py:21
  19.9 1.9 collective-permute-start.3
  21.9 0.7 constant_dynamic-update-slice_fusion.1
  22.6 0.9 broadcast_in_dim.6
  23.4 6.8 %all-to-all-start = ((bf16[16,16,1152]{2,1,0:T(8,128)(2,1)}), bf16[16,16,1152]{2,1,0:T(8,128)(2,1)S(1)}, u32[]{:S(2)}, u32[]{:S(2)}) async-start(bf16[16,16,1152]{2,1,0:T(8,128)(2,1)} %broadcast_in_dim.6), calls=%async_computation | async-start | bytes 1179648 | tf_op jit(solution)/shard_map/all_to_all | solution.py:26
  30.2 0.3 fusion.3
  30.5 10.6 %all-to-all-done = bf16[16,16,1152]{2,1,0:T(8,128)(2,1)S(1)} async-done(((bf16[16,16,1152]{2,1,0:T(8,128)(2,1)}), bf16[16,16,1152]{2,1,0:T(8,128)(2,1)S(1)}, u32[]{:S(2)}, u32[]{:S(2)}) %all-to-all-start) | async-done | bytes 589856 | tf_op jit(solution)/shard_map/all_to_all | solution.py:26
  41.1 1.8 convolution_convert_fusion.3
  42.9 0.3 fusion.4
  43.3 1.8 convolution_convert_fusion.2
  45.1 0.0 copy-start.14
  45.1 16.9 %all_to_all.25 = bf16[4,136,512]{2,1,0:T(8,128)(2,1)S(1)} all-to-all(bf16[4,136,512]{2,1,0:T(8,128)(2,1)S(1)} %pad_maximum_fusion.2), channel_id=1, replica_groups=mesh['la'=2,'lb'=2,'lc'=2,'x'=4,'zhi'=2,'y'=4,'core'=2] {'lc','lb'}, dimensions={0} | all-to-all | bytes 1114112 | tf_op jit(solution)/shard_map/all_to_all | solution.py:44
  62.0 0.1 convert_reduce_fusion.1
  62.1 3.6 %collective-permute-start.4 = (bf16[136,512]{1,0:T(8,128)(2,1)S(1)}, bf16[136,512]{1,0:T(8,128)(2,1)S(1)}, u32[]{:S(2)}, u32[]{:S(2)}) collective-permute-start(bf16[136,512]{1,0:T(8,128)(2,1)S(1)} %convert_element_type.94), channel_id=1, source_target_pairs={{0,256},{256,0},{1,257},{257,1},{2,258},{258,2},{3,259},{259,3},{4... | collective-permute-start | bytes 417800 | tf_op jit(solution)/shard_map/ppermute | solution.py:21
  65.7 4.3 %collective-permute-start.5 = (f32[512]{0:T(512)S(1)}, f32[512]{0:T(512)S(1)}, u32[]{:S(2)}, u32[]{:S(2)}) collective-permute-start(f32[512]{0:T(512)S(1)} %copy-done.14), channel_id=1, source_target_pairs={{0,1},{1,0},{2,3},{3,2},{4,5},{5,4},{6,7},{7,6},{8,9},{9,8},{10,11... | collective-permute-start | bytes 6152 | tf_op jit(solution)/shard_map/ppermute | solution.py:21
  70.0 0.8 collective-permute-done.5
  70.8 11.2 %collective-permute-done.4 = bf16[136,512]{1,0:T(8,128)(2,1)S(1)} collective-permute-done((bf16[136,512]{1,0:T(8,128)(2,1)S(1)}, bf16[136,512]{1,0:T(8,128)(2,1)S(1)}, u32[]{:S(2)}, u32[]{:S(2)}) %collective-permute-start.4) | collective-permute-done | bytes 139296 | tf_op jit(solution)/shard_map/ppermute | solution.py:21
  82.0 0.0 copy-start.3
  82.0 0.7 copy-done.3
  82.7 0.1 multiply_convert_fusion.1
  82.8 1.9 collective-permute-start.6
  84.8 5.5 %collective-permute-done.6 = bf16[2,64,512]{2,1,0:T(8,128)(2,1)} collective-permute-done((bf16[2,64,512]{2,1,0:T(8,128)(2,1)S(1)}, bf16[2,64,512]{2,1,0:T(8,128)(2,1)}, u32[]{:S(2)}, u32[]{:S(2)}) %collective-permute-start.6) | collective-permute-done | bytes 131104 | tf_op jit(solution)/shard_map/ppermute | solution.py:21
  90.3 1.0 broadcast_select_fusion.7
  91.3 1.9 collective-permute-start.7
  93.3 0.3 fusion.27
  93.6 6.1 %collective-permute-done.7 = bf16[2,128,512]{2,1,0:T(8,128)(2,1)S(1)} collective-permute-done((bf16[2,128,512]{2,1,0:T(8,128)(2,1)S(1)}, bf16[2,128,512]{2,1,0:T(8,128)(2,1)S(1)}, u32[]{:S(2)}, u32[]{:S(2)}) %collective-permute-start.7) | collective-permute-done | bytes 262176 | tf_op jit(solution)/shard_map/ppermute | solution.py:21
  99.7 0.4 fusion.32
  100.0 0.4 fusion.2
  100.4 0.4 broadcast_select_fusion.1
  100.8 0.0 copy-start.13
  100.9 13.0 %all_to_all.26 = bf16[16,16,1152]{2,1,0:T(8,128)(2,1)S(1)} all-to-all(bf16[16,16,1152]{2,1,0:T(8,128)(2,1)S(1)} %bitcast.76), channel_id=1, replica_groups=mesh['la'=2,'lb'=2,'lc'=2,'x'=4,'zhi'=2,'y'=4,'core'=2] {'x','y'}, dimensions={0} | all-to-all | bytes 1179648 | tf_op jit(solution)/shard_map/all_to_all | solution.py:78
  113.9 0.1 convert_reduce_fusion
  114.0 6.9 %collective-permute-start.8 = (bf16[16,1152]{1,0:T(8,128)(2,1)S(1)}, bf16[16,1152]{1,0:T(8,128)(2,1)S(1)}, u32[]{:S(2)}, u32[]{:S(2)}) collective-permute-start(bf16[16,1152]{1,0:T(8,128)(2,1)S(1)} %convert_element_type.100), channel_id=1, source_target_pairs={{0,8},{8,0},{1,9},{9,1},{2,10},{10,2},{3,11},{11,3},{4,12},{12,4},... | collective-permute-start | bytes 110600 | tf_op jit(solution)/shard_map/ppermute | solution.py:21
  120.9 6.6 %collective-permute-done.8 = bf16[16,1152]{1,0:T(8,128)(2,1)S(1)} collective-permute-done((bf16[16,1152]{1,0:T(8,128)(2,1)S(1)}, bf16[16,1152]{1,0:T(8,128)(2,1)S(1)}, u32[]{:S(2)}, u32[]{:S(2)}) %collective-permute-start.8) | collective-permute-done | bytes 36896 | tf_op jit(solution)/shard_map/ppermute | solution.py:21
  127.6 12.4 %all_to_all.27 = bf16[16,16,1152]{2,1,0:T(8,128)(2,1)S(1)} all-to-all(bf16[16,16,1152]{2,1,0:T(8,128)(2,1)S(1)} %broadcast_in_dim.8), channel_id=1, replica_groups=mesh['la'=2,'lb'=2,'lc'=2,'x'=4,'zhi'=2,'y'=4,'core'=2] {'x','y'}, dimensions={0} | all-to-all | bytes 1179648 | tf_op jit(solution)/shard_map/all_to_all | solution.py:26
  140.0 0.5 convolution_convert_fusion.1
  140.5 0.5 convolution_convert_fusion
  141.1 0.8 pad_maximum_fusion.3
  141.9 4.1 %all-to-all-start.4 = ((bf16[4,128,512]{2,1,0:T(8,128)(2,1)}), bf16[4,128,512]{2,1,0:T(8,128)(2,1)}, u32[]{:S(2)}, u32[]{:S(2)}) async-start(bf16[4,128,512]{2,1,0:T(8,128)(2,1)} %pad_maximum_fusion.3), calls=%async_computation.4 | async-start | bytes 1048576 | tf_op jit(solution)/shard_map/all_to_all | solution.py:44
  146.1 0.0 copy-start.11
  146.1 8.6 %collective-permute-start.1 = (bf16[256,1152]{1,0:T(8,128)(2,1)S(1)}, bf16[256,1152]{1,0:T(8,128)(2,1)}, u32[]{:S(2)}, u32[]{:S(2)}) collective-permute-start(bf16[256,1152]{1,0:T(8,128)(2,1)S(1)} %bitcast.75), channel_id=1, source_target_pairs={{0,1},{1,0},{2,3},{3,2},{4,5},{5,4},{6,7},{7,6},{8,9},{9,8},{10,11... | collective-permute-start | bytes 1769480 | tf_op jit(solution)/shard_map/ppermute | solution.py:21
  154.7 0.9 fusion.48
  155.6 0.7 fusion.39
  156.3 0.1 broadcast_select_fusion.3
  156.4 0.1 convert_reduce_fusion.2
  156.6 1.6 fusion.6
  158.1 1.9 collective-permute-start.13
  160.1 1.1 convert_reduce_fusion.3
  161.2 3.1 %collective-permute-start.9 = (bf16[128,512]{1,0:T(8,128)(2,1)S(1)}, bf16[128,512]{1,0:T(8,128)(2,1)S(1)}, u32[]{:S(2)}, u32[]{:S(2)}) collective-permute-start(bf16[128,512]{1,0:T(8,128)(2,1)S(1)} %convert_element_type.107), channel_id=1, source_target_pairs={{0,256},{256,0},{1,257},{257,1},{2,258},{258,2},{3,259},{259,3},{4... | collective-permute-start | bytes 393224 | tf_op jit(solution)/shard_map/ppermute | solution.py:21
  164.4 1.1 fusion.49
  165.5 5.5 %collective-permute-done.9 = bf16[128,512]{1,0:T(8,128)(2,1)S(1)} collective-permute-done((bf16[128,512]{1,0:T(8,128)(2,1)S(1)}, bf16[128,512]{1,0:T(8,128)(2,1)S(1)}, u32[]{:S(2)}, u32[]{:S(2)}) %collective-permute-start.9) | collective-permute-done | bytes 131104 | tf_op jit(solution)/shard_map/ppermute | solution.py:21
  171.0 0.1 multiply_convert_fusion
  171.2 12.4 %collective-permute-start.10 = (bf16[64,512]{1,0:T(8,128)(2,1)S(1)}, bf16[64,512]{1,0:T(8,128)(2,1)S(1)}, u32[]{:S(2)}, u32[]{:S(2)}) collective-permute-start(bf16[64,512]{1,0:T(8,128)(2,1)S(1)} %get-tuple-element.17), channel_id=1, source_target_pairs={{0,1},{1,0},{2,3},{3,2},{4,5},{5,4},{6,7},{7,6},{8,9},{9,8},{10,11... | collective-permute-start | bytes 196616 | tf_op jit(solution)/shard_map/ppermute | solution.py:21
  183.7 0.0 copy-start.12
  183.7 0.1 maximum_bitcast_fusion
  183.8 0.7 collective-permute-done.10
  184.5 1.9 collective-permute-start.11
  186.5 2.9 %add_convert_fusion = bf16[512,1152]{1,0:T(8,128)(2,1)} fusion(bf16[512,1152]{1,0:T(8,128)(2,1)} %collective-permute-done.13, bf16[512,1152]{1,0:T(8,128)(2,1)S(1)} %copy-done, f32[512]{0:T(512)S(1)} %bitcast.93, bf16[256,1152]{1,0:T(8,128)(2,1)S(1)} %bitcast.84, bf16[2,128,512]{2,1,0:T(8,128)(2,1)S(1)} %copy-done.5, bf16[2,128,512]{2,1,0:T(8,128)(2,1)S(1)} %copy-done.7), kind=kOutput, calls=%fused_computation.15 | convolution fusion | flops 306053120 | bytes 4655104 | tf_op jit(solution)/shard_map/dot_general | solution.py:36
  189.4 4.8 %collective-permute-done.11 = bf16[2,64,512]{2,1,0:T(8,128)(2,1)S(1)} collective-permute-done((bf16[2,64,512]{2,1,0:T(8,128)(2,1)S(1)}, bf16[2,64,512]{2,1,0:T(8,128)(2,1)S(1)}, u32[]{:S(2)}, u32[]{:S(2)}) %collective-permute-start.11) | collective-permute-done | bytes 131104 | tf_op jit(solution)/shard_map/ppermute | solution.py:21
  194.3 1.9 collective-permute-start.12
  196.2 0.6 fusion.9
  196.8 6.8 %collective-permute-done.12 = bf16[2,128,512]{2,1,0:T(8,128)(2,1)S(1)} collective-permute-done((bf16[2,128,512]{2,1,0:T(8,128)(2,1)S(1)}, bf16[2,128,512]{2,1,0:T(8,128)(2,1)S(1)}, u32[]{:S(2)}, u32[]{:S(2)}) %collective-permute-start.12) | collective-permute-done | bytes 262176 | tf_op jit(solution)/shard_map/ppermute | solution.py:21
  203.6 1.6 fusion
  (53 shorter events, 0.5 us)
Async XLA Ops:
  0.6 29.6 %copy-start = (bf16[512,1152]{1,0:T(8,128)(2,1)S(1)}, bf16[512,1152]{1,0:T(8,128)(2,1)}, u32[]{:S(2)}) copy-start(bf16[512,1152]{1,0:T(8,128)(2,1)} %param.8) | copy-start | bytes 3538948
  0.6 21.9 %collective-permute-start = (bf16[8,1152]{1,0:T(8,128)(2,1)}, bf16[8,1152]{1,0:T(8,128)(2,1)S(1)}, u32[]{:S(2)}, u32[]{:S(2)}) collective-permute-start(bf16[8,1152]{1,0:T(8,128)(2,1)} %param.5), channel_id=1, source_target_pairs={{0,8},{8,0},{1,9},{9,1},{2,10},{10,2},{3,11},{11,3},{4,12},{12,4},... | collective-permute-start | bytes 55304 | tf_op jit(solution)/shard_map/ppermute | solution.py:21
  17.1 26.2 %collective-permute-start.2 = (bf16[1152,512]{1,0:T(8,128)(2,1)}, bf16[1152,512]{1,0:T(8,128)(2,1)}, u32[]{:S(2)}, u32[]{:S(2)}) collective-permute-start(bf16[1152,512]{1,0:T(8,128)(2,1)} %param.6), channel_id=1, source_target_pairs={{0,1},{1,0},{2,3},{3,2},{4,5},{5,4},{6,7},{7,6},{8,9},{9,8},{10,11... | collective-permute-start | bytes 3538952 | tf_op jit(solution)/shard_map/ppermute | solution.py:21
  19.9 23.0 %collective-permute-start.3 = (bf16[512,1152]{1,0:T(8,128)(2,1)}, bf16[512,1152]{1,0:T(8,128)(2,1)S(1)}, u32[]{:S(2)}, u32[]{:S(2)}) collective-permute-start(bf16[512,1152]{1,0:T(8,128)(2,1)} %param.8), channel_id=1, source_target_pairs={{0,1},{1,0},{2,3},{3,2},{4,5},{5,4},{6,7},{7,6},{8,9},{9,8},{10,11... | collective-permute-start | bytes 3538952 | tf_op jit(solution)/shard_map/ppermute | solution.py:21
  23.4 17.7 %all-to-all-start = ((bf16[16,16,1152]{2,1,0:T(8,128)(2,1)}), bf16[16,16,1152]{2,1,0:T(8,128)(2,1)S(1)}, u32[]{:S(2)}, u32[]{:S(2)}) async-start(bf16[16,16,1152]{2,1,0:T(8,128)(2,1)} %broadcast_in_dim.6), calls=%async_computation | async-start | bytes 1179648 | tf_op jit(solution)/shard_map/all_to_all | solution.py:26
  45.1 20.6 %copy-start.14 = (f32[512]{0:T(512)S(1)}, f32[512]{0:T(512)}, u32[]{:S(2)}) copy-start(f32[512]{0:T(512)} %param.7) | copy-start | bytes 6148
  62.1 19.9 %collective-permute-start.4 = (bf16[136,512]{1,0:T(8,128)(2,1)S(1)}, bf16[136,512]{1,0:T(8,128)(2,1)S(1)}, u32[]{:S(2)}, u32[]{:S(2)}) collective-permute-start(bf16[136,512]{1,0:T(8,128)(2,1)S(1)} %convert_element_type.94), channel_id=1, source_target_pairs={{0,256},{256,0},{1,257},{257,1},{2,258},{258,2},{3,259},{259,3},{4... | collective-permute-start | bytes 417800 | tf_op jit(solution)/shard_map/ppermute | solution.py:21
  65.7 5.1 %collective-permute-start.5 = (f32[512]{0:T(512)S(1)}, f32[512]{0:T(512)S(1)}, u32[]{:S(2)}, u32[]{:S(2)}) collective-permute-start(f32[512]{0:T(512)S(1)} %copy-done.14), channel_id=1, source_target_pairs={{0,1},{1,0},{2,3},{3,2},{4,5},{5,4},{6,7},{7,6},{8,9},{9,8},{10,11... | collective-permute-start | bytes 6152 | tf_op jit(solution)/shard_map/ppermute | solution.py:21
  82.0 0.7 copy-start.3
  82.8 7.5 %collective-permute-start.6 = (bf16[2,64,512]{2,1,0:T(8,128)(2,1)S(1)}, bf16[2,64,512]{2,1,0:T(8,128)(2,1)}, u32[]{:S(2)}, u32[]{:S(2)}) collective-permute-start(bf16[2,64,512]{2,1,0:T(8,128)(2,1)S(1)} %multiply_convert_fusion.1), channel_id=1, source_target_pairs={{0,128},{128,0},{1,129},{129,1},{2,130},{130,2},{3,131},{131,3},{4... | collective-permute-start | bytes 393224 | tf_op jit(solution)/shard_map/ppermute | solution.py:21
  91.3 8.4 %collective-permute-start.7 = (bf16[2,128,512]{2,1,0:T(8,128)(2,1)S(1)}, bf16[2,128,512]{2,1,0:T(8,128)(2,1)S(1)}, u32[]{:S(2)}, u32[]{:S(2)}) collective-permute-start(bf16[2,128,512]{2,1,0:T(8,128)(2,1)S(1)} %pad_maximum_fusion.4), channel_id=1, source_target_pairs={{0,64},{64,0},{1,65},{65,1},{2,66},{66,2},{3,67},{67,3},{4,68},{68... | collective-permute-start | bytes 786440 | tf_op jit(solution)/shard_map/ppermute | solution.py:21
  99.7 0.7 copy-start.8
  100.8 26.7 %copy-start.13 = (f32[1152]{0:T(1024)S(1)}, f32[1152]{0:T(1024)}, u32[]{:S(2)}) copy-start(f32[1152]{0:T(1024)} %param.9) | copy-start | bytes 13828
  114.0 13.5 %collective-permute-start.8 = (bf16[16,1152]{1,0:T(8,128)(2,1)S(1)}, bf16[16,1152]{1,0:T(8,128)(2,1)S(1)}, u32[]{:S(2)}, u32[]{:S(2)}) collective-permute-start(bf16[16,1152]{1,0:T(8,128)(2,1)S(1)} %convert_element_type.100), channel_id=1, source_target_pairs={{0,8},{8,0},{1,9},{9,1},{2,10},{10,2},{3,11},{11,3},{4,12},{12,4},... | collective-permute-start | bytes 110600 | tf_op jit(solution)/shard_map/ppermute | solution.py:21
  140.0 1.1 copy-start.10
  141.9 18.1 %all-to-all-start.4 = ((bf16[4,128,512]{2,1,0:T(8,128)(2,1)}), bf16[4,128,512]{2,1,0:T(8,128)(2,1)}, u32[]{:S(2)}, u32[]{:S(2)}) async-start(bf16[4,128,512]{2,1,0:T(8,128)(2,1)} %pad_maximum_fusion.3), calls=%async_computation.4 | async-start | bytes 1048576 | tf_op jit(solution)/shard_map/all_to_all | solution.py:44
  146.1 10.2 %copy-start.9 = (bf16[2,128,512]{2,1,0:T(8,128)(2,1)S(1)}, bf16[2,128,512]{2,1,0:T(8,128)(2,1)}, u32[]{:S(2)}) copy-start(bf16[2,128,512]{2,1,0:T(8,128)(2,1)} %copy-done.8) | copy-start | bytes 786436
  146.1 10.5 %copy-start.11 = (bf16[16,16,1152]{2,1,0:T(8,128)(2,1)S(1)}, bf16[16,16,1152]{2,1,0:T(8,128)(2,1)}, u32[]{:S(2)}) copy-start(bf16[16,16,1152]{2,1,0:T(8,128)(2,1)} %copy-done.10) | copy-start | bytes 1769476
  146.1 18.3 %collective-permute-start.1 = (bf16[256,1152]{1,0:T(8,128)(2,1)S(1)}, bf16[256,1152]{1,0:T(8,128)(2,1)}, u32[]{:S(2)}, u32[]{:S(2)}) collective-permute-start(bf16[256,1152]{1,0:T(8,128)(2,1)S(1)} %bitcast.75), channel_id=1, source_target_pairs={{0,1},{1,0},{2,3},{3,2},{4,5},{5,4},{6,7},{7,6},{8,9},{9,8},{10,11... | collective-permute-start | bytes 1769480 | tf_op jit(solution)/shard_map/ppermute | solution.py:21
  156.4 1.7 copy-start.4
  156.4 1.7 copy-start.6
  158.1 28.3 %collective-permute-start.13 = (bf16[512,1152]{1,0:T(8,128)(2,1)}, bf16[512,1152]{1,0:T(8,128)(2,1)}, u32[]{:S(2)}, u32[]{:S(2)}) collective-permute-start(bf16[512,1152]{1,0:T(8,128)(2,1)} %fusion.6), channel_id=1, source_target_pairs={{0,1},{1,0},{2,3},{3,2},{4,5},{5,4},{6,7},{7,6},{8,9},{9,8},{10,11... | collective-permute-start | bytes 3538952 | tf_op jit(solution)/shard_map/ppermute | solution.py:21
  161.2 22.4 %copy-start.1 = (bf16[8,16,1152]{2,1,0:T(8,128)(2,1)S(1)}, bf16[8,16,1152]{2,1,0:T(8,128)(2,1)}, u32[]{:S(2)}) copy-start(bf16[8,16,1152]{2,1,0:T(8,128)(2,1)} %get-tuple-element.2) | copy-start | bytes 884740
  161.2 22.4 %copy-start.2 = (bf16[8,16,1152]{2,1,0:T(8,128)(2,1)S(1)}, bf16[8,16,1152]{2,1,0:T(8,128)(2,1)}, u32[]{:S(2)}) copy-start(bf16[8,16,1152]{2,1,0:T(8,128)(2,1)} %get-tuple-element.3) | copy-start | bytes 884740
  161.2 9.8 %collective-permute-start.9 = (bf16[128,512]{1,0:T(8,128)(2,1)S(1)}, bf16[128,512]{1,0:T(8,128)(2,1)S(1)}, u32[]{:S(2)}, u32[]{:S(2)}) collective-permute-start(bf16[128,512]{1,0:T(8,128)(2,1)S(1)} %convert_element_type.107), channel_id=1, source_target_pairs={{0,256},{256,0},{1,257},{257,1},{2,258},{258,2},{3,259},{259,3},{4... | collective-permute-start | bytes 393224 | tf_op jit(solution)/shard_map/ppermute | solution.py:21
  171.2 13.3 %collective-permute-start.10 = (bf16[64,512]{1,0:T(8,128)(2,1)S(1)}, bf16[64,512]{1,0:T(8,128)(2,1)S(1)}, u32[]{:S(2)}, u32[]{:S(2)}) collective-permute-start(bf16[64,512]{1,0:T(8,128)(2,1)S(1)} %get-tuple-element.17), channel_id=1, source_target_pairs={{0,1},{1,0},{2,3},{3,2},{4,5},{5,4},{6,7},{7,6},{8,9},{9,8},{10,11... | collective-permute-start | bytes 196616 | tf_op jit(solution)/shard_map/ppermute | solution.py:21
  183.6 2.8 %copy-start.5 = (bf16[2,128,512]{2,1,0:T(8,128)(2,1)S(1)}, bf16[2,128,512]{2,1,0:T(8,128)(2,1)}, u32[]{:S(2)}) copy-start(bf16[2,128,512]{2,1,0:T(8,128)(2,1)} %copy-done.4) | copy-start | bytes 786436
  183.7 2.8 %copy-start.7 = (bf16[2,128,512]{2,1,0:T(8,128)(2,1)S(1)}, bf16[2,128,512]{2,1,0:T(8,128)(2,1)}, u32[]{:S(2)}) copy-start(bf16[2,128,512]{2,1,0:T(8,128)(2,1)} %copy-done.6) | copy-start | bytes 786436
  183.7 2.8 %copy-start.12 = (bf16[16,16,1152]{2,1,0:T(8,128)(2,1)S(1)}, bf16[16,16,1152]{2,1,0:T(8,128)(2,1)}, u32[]{:S(2)}) copy-start(bf16[16,16,1152]{2,1,0:T(8,128)(2,1)} %copy-done.10) | copy-start | bytes 1769476
  184.5 9.7 %collective-permute-start.11 = (bf16[2,64,512]{2,1,0:T(8,128)(2,1)S(1)}, bf16[2,64,512]{2,1,0:T(8,128)(2,1)S(1)}, u32[]{:S(2)}, u32[]{:S(2)}) collective-permute-start(bf16[2,64,512]{2,1,0:T(8,128)(2,1)S(1)} %pad_maximum_fusion.6), channel_id=1, source_target_pairs={{0,128},{128,0},{1,129},{129,1},{2,130},{130,2},{3,131},{131,3},{4... | collective-permute-start | bytes 393224 | tf_op jit(solution)/shard_map/ppermute | solution.py:21
  194.3 9.3 %collective-permute-start.12 = (bf16[2,128,512]{2,1,0:T(8,128)(2,1)S(1)}, bf16[2,128,512]{2,1,0:T(8,128)(2,1)S(1)}, u32[]{:S(2)}, u32[]{:S(2)}) collective-permute-start(bf16[2,128,512]{2,1,0:T(8,128)(2,1)S(1)} %pad_maximum_fusion.5), channel_id=1, source_target_pairs={{0,64},{64,0},{1,65},{65,1},{2,66},{66,2},{3,67},{67,3},{4,68},{68... | collective-permute-start | bytes 786440 | tf_op jit(solution)/shard_map/ppermute | solution.py:21

commit v4 on v3

--- a/solution.py
+++ b/solution.py
@@ -46,14 +46,14 @@
 
 
 def gather_over_layer(block):
-    half = in_order(block, swap(block, "lb"), lax.axis_index("lb"), 1)
-    return half, swap(half, "lc")
+    blocks = jnp.broadcast_to(block[None], (4, *block.shape))
+    blocks = lax.all_to_all(blocks, QUARTER, 0, 0, tiled=True)
+    return jnp.stack([blocks[:, i].reshape(-1, block.shape[-1]) for i in (0, 1)])
 
 
 def local(activations, enc_weight, enc_bias, dec_weight, dec_bias):
     rows, features = activations.shape
     plane = lax.axis_size("x") * lax.axis_size("y")
-    lc = lax.axis_index("lc")
     count = plane * 2 * rows
 
     both = jnp.concatenate([activations, swap(activations, "zhi")], axis=0)
@@ -71,10 +71,7 @@
     gating = jax.nn.sigmoid(sharpness * preact)
     latents = gather_over_layer((preact * gating).astype(bf16))
 
-    def decode(half):
-        return (dot(half[0], dec[0]) + dot(half[1], dec[1])).astype(bf16)
-
-    part = in_order(decode(latents[0]), decode(latents[1]), lc, 0)
+    part = (dot(latents[0], dec[0]) + dot(latents[1], dec[1])).astype(bf16)
     parts = lax.all_to_all(part.reshape(plane, 2 * rows, features), PLANE, 0, 0, tiled=True)
     part = jnp.sum(parts.astype(f32), axis=0)
     got = swap(part.astype(bf16), "zhi").astype(f32)
@@ -84,7 +81,6 @@
     lat_grad = sum_over_layer([dot(residual, d, ((1,), (1,))) for d in dec])
     lat_grad = lat_grad.reshape(2, count // 4, -1) + sparsity * dec_norm[:, None, :]
 
-    latents = in_order(*latents, lc, 1)
     lat_sums = jnp.sum(latents.astype(f32), axis=1)
     dec_grads = [
         dot(latents[i], residual, ((0,), (0,))) + (sparsity * lat_sums[i] / dec_norm[i])[:, None] * dec_f32[i]
@@ -93,19 +89,12 @@
     dec_grad = dec_grads[0] + swap(dec_grads[1].astype(bf16), "core").astype(f32)
 
     pre_grad = (lat_grad * (gating + sharpness * preact * gating * (1.0 - gating))).astype(bf16)
-    pre_grad = jnp.stack([pre_grad[0], swap(pre_grad[1], "core")])
-    near_grad, far_grad = gather_over_layer(pre_grad)
-    half = count // 2
-    all_acts = jnp.stack(
-        [jnp.concatenate([a[i * half : (i + 1) * half] for a in (acts, far_acts)]) for i in (0, 1)]
-    )
-
-    def encode(index, grad):
-        rows = lax.dynamic_index_in_dim(all_acts, index, 0, keepdims=False)
-        return dot(rows, grad.reshape(count, -1), ((0,), (0,)))
-
-    enc_grad = encode(1 - lc, far_grad)
-    enc_grad = enc_grad + encode(lc, near_grad)
+    core = lax.axis_index("core")
+    pre_grad = in_order(pre_grad[:1], pre_grad[1:], core, 0)
+    pre_grad = jnp.broadcast_to(pre_grad[None], (4, *pre_grad.shape))
+    pre_grad = lax.all_to_all(pre_grad.reshape(8, *pre_grad.shape[2:]), (*QUARTER, "core"), 0, 0, tiled=True)
+    rows = in_order(acts.reshape(4, 1, -1, features), far_acts.reshape(4, 1, -1, features), core, 1)
+    enc_grad = dot(rows.reshape(-1, features), pre_grad.reshape(2 * count, -1), ((0,), (0,)))
     return (enc_grad.astype(bf16), dec_grad.astype(bf16))
 
 

time: 206 us -> 200 us (0.971)
  waiting for transfers between devices: 58.7 us -> 40.8 us
  blocking collectives: 42.3 us -> 60.1 us
  starting transfers between devices: 80.5 us -> 71.9 us
  other arithmetic: 5.33 us -> 8.98 us
    ppermute x14 -> x9, waiting for transfers between devices: 48.1 us -> 22.9 us  [swap(): return lax.ppermute(x, axis, SWAP)]
    all_to_all x0 -> x1, blocking collectives: none -> 16.5 us  [gather_over_layer(): blocks = lax.all_to_all(blocks, QUARTER, 0, 0, tiled=True)]
    ppermute x14 -> x9, starting transfers between devices: 69.6 us -> 55.4 us  [swap(): return lax.ppermute(x, axis, SWAP)]
    all_to_all x0 -> x1, waiting for transfers between devices: none -> 5.76 us  [local(): lax.all_to_all(pre_grad.reshape(8, *pre_grad.shape[2:]), (*QUARTER, 'core...]
    all_to_all x0 -> x1, starting transfers between devices: none -> 5.59 us  [local(): lax.all_to_all(pre_grad.reshape(8, *pre_grad.shape[2:]), (*QUARTER, 'core...]
    convert_element_type x0 -> x1, other arithmetic: none -> 2.65 us  [local(): return (enc_grad.astype(bf16), dec_grad.astype(bf16))]
    dot_general x12 -> x9, matrix products: 12.6 us -> 10.8 us  [dot(): return lax.dot_general(a, b, (dims, ((), ())), preferred_element_type=f32)]
  transfers between devices with their start and end apart: 16 -> 12, of which waited for: 10 -> 7; matrix products, arithmetic and copies ran while one was open for 7% -> 7% of each run, Pallas kernels for 0% -> 0%
where the time goes in v4:
time: 200 us; the launch traced here: 197 us
  starting transfers between devices  71.9 us (36%)
  blocking collectives  60.1 us (30%)
  waiting for transfers between devices  40.8 us (20%)
  matrix products  10.8 us (5%)
  other arithmetic  8.98 us (4%)
  local copies, waits for them, and re-layouts  3.41 us (2%)
    ppermute x9, starting transfers between devices, swap(): return lax.ppermute(x, axis, SWAP)  55.4 us
    ppermute x9, waiting for transfers between devices, swap(): return lax.ppermute(x, axis, SWAP)  22.9 us
    all_to_all x1, blocking collectives, sum_over_layer(): lax.all_to_all(parts, QUARTER, 0, 0, tiled=True).astype(f32)  16.9 us
    all_to_all x1, blocking collectives, gather_over_layer(): blocks = lax.all_to_all(blocks, QUARTER, 0, 0, tiled=True)  16.5 us
    all_to_all x1, blocking collectives, local(): lax.all_to_all(part.reshape(plane, 2 * rows, features), PLANE, 0, 0, tile...  14.1 us
    all_to_all x1, blocking collectives, spread(): lax.all_to_all(blocks, PLANE, 0, 0, tiled=True).reshape(-1, block.shape[-1])  12.7 us
    dot_general x9, matrix products, dot(): return lax.dot_general(a, b, (dims, ((), ())), preferred_element_type=f32)  10.8 us
    all_to_all x1, waiting for transfers between devices, spread(): lax.all_to_all(blocks, PLANE, 0, 0, tiled=True).reshape(-1, block.shape[-1])  10.6 us
  transfers between devices with their start and end apart: 12, of which 7 were waited for; matrix products, arithmetic and copies ran while one was open for 7% of the time, Pallas kernels for 0%

profile of v4, /device:TPU:1, one launch (start us, length us, event | category | flops | bytes accessed | tf_op | source)
XLA Modules:
  0.0 197.1 jit_solution(15956431952594051032)
XLA Ops:
  0.6 0.0 copy-start
  0.6 16.4 %collective-permute-start = (bf16[8,1152]{1,0:T(8,128)(2,1)}, bf16[8,1152]{1,0:T(8,128)(2,1)S(1)}, u32[]{:S(2)}, u32[]{:S(2)}) collective-permute-start(bf16[8,1152]{1,0:T(8,128)(2,1)} %param.5), channel_id=1, source_target_pairs={{0,8},{8,0},{1,9},{9,1},{2,10},{10,2},{3,11},{11,3},{4,12},{12,4},... | collective-permute-start | bytes 55304 | tf_op jit(solution)/shard_map/ppermute | solution.py:21
  17.1 2.9 %collective-permute-start.2 = (bf16[1152,512]{1,0:T(8,128)(2,1)}, bf16[1152,512]{1,0:T(8,128)(2,1)}, u32[]{:S(2)}, u32[]{:S(2)}) collective-permute-start(bf16[1152,512]{1,0:T(8,128)(2,1)} %param.6), channel_id=1, source_target_pairs={{0,1},{1,0},{2,3},{3,2},{4,5},{5,4},{6,7},{7,6},{8,9},{9,8},{10,11... | collective-permute-start | bytes 3538952 | tf_op jit(solution)/shard_map/ppermute | solution.py:21
  19.9 1.9 collective-permute-start.3
  21.9 0.7 constant_dynamic-update-slice_fusion.1
  22.6 0.0 collective-permute-done
  22.6 0.9 broadcast_in_dim.10
  23.4 6.8 %all-to-all-start = ((bf16[16,16,1152]{2,1,0:T(8,128)(2,1)}), bf16[16,16,1152]{2,1,0:T(8,128)(2,1)S(1)}, u32[]{:S(2)}, u32[]{:S(2)}) async-start(bf16[16,16,1152]{2,1,0:T(8,128)(2,1)} %broadcast_in_dim.10), calls=%async_computation | async-start | bytes 1179648 | tf_op jit(solution)/shard_map/all_to_all | solution.py:26
  30.2 0.0 copy-done
  30.2 0.3 fusion.1
  30.5 10.6 %all-to-all-done = bf16[16,16,1152]{2,1,0:T(8,128)(2,1)S(1)} async-done(((bf16[16,16,1152]{2,1,0:T(8,128)(2,1)}), bf16[16,16,1152]{2,1,0:T(8,128)(2,1)S(1)}, u32[]{:S(2)}, u32[]{:S(2)}) %all-to-all-start) | async-done | bytes 589856 | tf_op jit(solution)/shard_map/all_to_all | solution.py:26
  41.1 2.0 %convolution_convert_fusion.4 = bf16[256,512]{1,0:T(8,128)(2,1)S(1)} fusion(bf16[256,1152]{1,0:T(8,128)(2,1)S(1)} %bitcast.50, bf16[1152,512]{1,0:T(8,128)(2,1)} %param.6), kind=kOutput, calls=%fused_computation.16 | convolution fusion | flops 302120960 | bytes 2031616 | tf_op jit(solution)/shard_map/dot_general | solution.py:36
  43.1 0.0 collective-permute-done.3
  43.1 0.3 fusion.2
  43.5 0.0 collective-permute-done.2
  43.5 0.0 copy-done.1
  43.5 1.8 convolution_convert_fusion.3
  45.3 0.0 copy-start.8
  45.3 16.9 %all_to_all.35 = bf16[4,136,512]{2,1,0:T(8,128)(2,1)S(1)} all-to-all(bf16[4,136,512]{2,1,0:T(8,128)(2,1)S(1)} %pad_maximum_fusion.1), channel_id=1, replica_groups=mesh['la'=2,'lb'=2,'lc'=2,'x'=4,'zhi'=2,'y'=4,'core'=2] {'lc','lb'}, dimensions={0} | all-to-all | bytes 1114112 | tf_op jit(solution)/shard_map/all_to_all | solution.py:44
  62.2 0.1 convert_reduce_fusion.1
  62.3 3.6 %collective-permute-start.4 = (bf16[136,512]{1,0:T(8,128)(2,1)S(1)}, bf16[136,512]{1,0:T(8,128)(2,1)S(1)}, u32[]{:S(2)}, u32[]{:S(2)}) collective-permute-start(bf16[136,512]{1,0:T(8,128)(2,1)S(1)} %convert_element_type.95), channel_id=1, source_target_pairs={{0,256},{256,0},{1,257},{257,1},{2,258},{258,2},{3,259},{259,3},{4... | collective-permute-start | bytes 417800 | tf_op jit(solution)/shard_map/ppermute | solution.py:21
  65.9 0.0 copy-done.8
  65.9 4.3 %collective-permute-start.5 = (f32[512]{0:T(512)S(1)}, f32[512]{0:T(512)S(1)}, u32[]{:S(2)}, u32[]{:S(2)}) collective-permute-start(f32[512]{0:T(512)S(1)} %copy-done.8), channel_id=1, source_target_pairs={{0,1},{1,0},{2,3},{3,2},{4,5},{5,4},{6,7},{7,6},{8,9},{9,8},{10,11... | collective-permute-start | bytes 6152 | tf_op jit(solution)/shard_map/ppermute | solution.py:21
  70.2 0.8 collective-permute-done.5
  71.0 11.2 %collective-permute-done.4 = bf16[136,512]{1,0:T(8,128)(2,1)S(1)} collective-permute-done((bf16[136,512]{1,0:T(8,128)(2,1)S(1)}, bf16[136,512]{1,0:T(8,128)(2,1)S(1)}, u32[]{:S(2)}, u32[]{:S(2)}) %collective-permute-start.4) | collective-permute-done | bytes 139296 | tf_op jit(solution)/shard_map/ppermute | solution.py:21
  82.3 0.7 copy-done.6
  82.9 0.1 copy-done.3
  83.0 0.1 multiply_convert_fusion.1
  83.2 16.5 %all_to_all.36 = bf16[4,2,64,512]{3,2,1,0:T(8,128)(2,1)S(1)} all-to-all(bf16[4,2,64,512]{3,2,1,0:T(8,128)(2,1)S(1)} %broadcast_in_dim.12), channel_id=1, replica_groups=mesh['la'=2,'lb'=2,'lc'=2,'x'=4,'zhi'=2,'y'=4,'core'=2] {'lc','lb'}, dimensions={0} | all-to-all | bytes 1048576 | tf_op jit(solution)/shard_map/all_to_all | solution.py:50
  99.7 0.5 fusion.14
  100.2 0.5 fusion
  100.8 0.0 copy-start.7
  100.8 14.1 %all_to_all.37 = bf16[16,16,1152]{2,1,0:T(8,128)(2,1)S(1)} all-to-all(bf16[16,16,1152]{2,1,0:T(8,128)(2,1)S(1)} %bitcast.54), channel_id=1, replica_groups=mesh['la'=2,'lb'=2,'lc'=2,'x'=4,'zhi'=2,'y'=4,'core'=2] {'x','y'}, dimensions={0} | all-to-all | bytes 1179648 | tf_op jit(solution)/shard_map/all_to_all | solution.py:75
  114.9 0.1 convert_reduce_fusion
  115.0 6.7 %collective-permute-start.6 = (bf16[16,1152]{1,0:T(8,128)(2,1)S(1)}, bf16[16,1152]{1,0:T(8,128)(2,1)S(1)}, u32[]{:S(2)}, u32[]{:S(2)}) collective-permute-start(bf16[16,1152]{1,0:T(8,128)(2,1)S(1)} %convert_element_type.100), channel_id=1, source_target_pairs={{0,8},{8,0},{1,9},{9,1},{2,10},{10,2},{3,11},{11,3},{4,12},{12,4},... | collective-permute-start | bytes 110600 | tf_op jit(solution)/shard_map/ppermute | solution.py:21
  121.7 6.7 %collective-permute-done.6 = bf16[16,1152]{1,0:T(8,128)(2,1)S(1)} collective-permute-done((bf16[16,1152]{1,0:T(8,128)(2,1)S(1)}, bf16[16,1152]{1,0:T(8,128)(2,1)S(1)}, u32[]{:S(2)}, u32[]{:S(2)}) %collective-permute-start.6) | collective-permute-done | bytes 36896 | tf_op jit(solution)/shard_map/ppermute | solution.py:21
  128.4 0.0 copy-done.7
  128.5 12.7 %all_to_all.38 = bf16[16,16,1152]{2,1,0:T(8,128)(2,1)S(1)} all-to-all(bf16[16,16,1152]{2,1,0:T(8,128)(2,1)S(1)} %broadcast_in_dim.13), channel_id=1, replica_groups=mesh['la'=2,'lb'=2,'lc'=2,'x'=4,'zhi'=2,'y'=4,'core'=2] {'x','y'}, dimensions={0} | all-to-all | bytes 1179648 | tf_op jit(solution)/shard_map/all_to_all | solution.py:26
  141.2 0.5 convolution_convert_fusion.2
  141.7 0.5 convolution_convert_fusion.1
  142.3 0.8 pad_maximum_fusion.2
  143.1 4.1 %all-to-all-start.5 = ((bf16[4,128,512]{2,1,0:T(8,128)(2,1)}), bf16[4,128,512]{2,1,0:T(8,128)(2,1)}, u32[]{:S(2)}, u32[]{:S(2)}) async-start(bf16[4,128,512]{2,1,0:T(8,128)(2,1)} %pad_maximum_fusion.2), calls=%async_computation.5 | async-start | bytes 1048576 | tf_op jit(solution)/shard_map/all_to_all | solution.py:44
  147.2 6.9 %collective-permute-start.1 = (bf16[256,1152]{1,0:T(8,128)(2,1)}, bf16[256,1152]{1,0:T(8,128)(2,1)}, u32[]{:S(2)}, u32[]{:S(2)}) collective-permute-start(bf16[256,1152]{1,0:T(8,128)(2,1)} %bitcast.52), channel_id=1, source_target_pairs={{0,1},{1,0},{2,3},{3,2},{4,5},{5,4},{6,7},{7,6},{8,9},{9,8},{10,11... | collective-permute-start | bytes 1769480 | tf_op jit(solution)/shard_map/ppermute | solution.py:21
  154.2 0.7 fusion.11
  154.9 0.1 convert_reduce_fusion.2
  155.0 1.5 all-to-all-done.5
  156.5 1.1 convert_reduce_fusion.3
  157.7 3.9 %collective-permute-start.7 = (bf16[128,512]{1,0:T(8,128)(2,1)S(1)}, bf16[128,512]{1,0:T(8,128)(2,1)S(1)}, u32[]{:S(2)}, u32[]{:S(2)}) collective-permute-start(bf16[128,512]{1,0:T(8,128)(2,1)S(1)} %convert_element_type.107), channel_id=1, source_target_pairs={{0,256},{256,0},{1,257},{257,1},{2,258},{258,2},{3,259},{259,3},{4... | collective-permute-start | bytes 393224 | tf_op jit(solution)/shard_map/ppermute | solution.py:21
  161.6 1.6 fusion.4
  163.2 8.8 %collective-permute-start.8 = (bf16[512,1152]{1,0:T(8,128)(2,1)}, bf16[512,1152]{1,0:T(8,128)(2,1)}, u32[]{:S(2)}, u32[]{:S(2)}) collective-permute-start(bf16[512,1152]{1,0:T(8,128)(2,1)} %fusion.4), channel_id=1, source_target_pairs={{0,1},{1,0},{2,3},{3,2},{4,5},{5,4},{6,7},{7,6},{8,9},{9,8},{10,11... | collective-permute-start | bytes 3538952 | tf_op jit(solution)/shard_map/ppermute | solution.py:21
  172.0 4.3 %collective-permute-done.7 = bf16[128,512]{1,0:T(8,128)(2,1)S(1)} collective-permute-done((bf16[128,512]{1,0:T(8,128)(2,1)S(1)}, bf16[128,512]{1,0:T(8,128)(2,1)S(1)}, u32[]{:S(2)}, u32[]{:S(2)}) %collective-permute-start.7) | collective-permute-done | bytes 131104 | tf_op jit(solution)/shard_map/ppermute | solution.py:21
  176.3 0.1 multiply_convert_fusion
  176.5 0.0 copy-start.2
  176.5 0.8 broadcast_in_dim.14
  177.4 5.6 %all-to-all-start.6 = ((bf16[8,64,512]{2,1,0:T(8,128)(2,1)}), bf16[8,64,512]{2,1,0:T(8,128)(2,1)}, u32[]{:S(2)}, u32[]{:S(2)}) async-start(bf16[8,64,512]{2,1,0:T(8,128)(2,1)} %bitcast.16), calls=%async_computation.6 | async-start | bytes 1048576 | tf_op jit(solution)/shard_map/all_to_all | solution.py:95
  183.0 0.0 collective-permute-done.1
  183.0 1.2 broadcast_select_fusion.1
  184.1 1.1 pad_maximum_fusion
  185.3 0.6 convolution_add_fusion
  185.8 0.0 copy-start.5
  185.8 0.0 collective-permute-done.8
  185.9 2.7 %add_convert_fusion = bf16[512,1152]{1,0:T(8,128)(2,1)} fusion(f32[512,1152]{1,0:T(8,128)S(1)} %convolution_add_fusion, bf16[512,1152]{1,0:T(8,128)(2,1)} %collective-permute-done.8), kind=kLoop, calls=%fused_computation.12 | loop fusion | flops 1769472 | bytes 4718592 | tf_op jit(solution)/shard_map/convert_element_type | solution.py:98
  188.5 5.8 %all-to-all-done.6 = bf16[8,64,512]{2,1,0:T(8,128)(2,1)} async-done(((bf16[8,64,512]{2,1,0:T(8,128)(2,1)}), bf16[8,64,512]{2,1,0:T(8,128)(2,1)}, u32[]{:S(2)}, u32[]{:S(2)}) %all-to-all-start.6) | async-done | bytes 524320 | tf_op jit(solution)/shard_map/all_to_all | solution.py:95
  194.3 2.9 %convolution_convert_fusion = bf16[1152,512]{1,0:T(8,128)(2,1)} fusion(bf16[512,1152]{1,0:T(8,128)(2,1)S(1)} %bitcast.57, bf16[512,512]{1,0:T(8,128)(2,1)} %bitcast.17), kind=kOutput, calls=%fused_computation.1 | convolution fusion | flops 604569600 | bytes 2883584 | tf_op jit(solution)/shard_map/dot_general | solution.py:36
  (28 shorter events, 0.4 us)
Async XLA Ops:
  0.6 29.6 %copy-start = (bf16[512,1152]{1,0:T(8,128)(2,1)S(1)}, bf16[512,1152]{1,0:T(8,128)(2,1)}, u32[]{:S(2)}) copy-start(bf16[512,1152]{1,0:T(8,128)(2,1)} %param.8) | copy-start | bytes 3538948
  0.6 21.9 %collective-permute-start = (bf16[8,1152]{1,0:T(8,128)(2,1)}, bf16[8,1152]{1,0:T(8,128)(2,1)S(1)}, u32[]{:S(2)}, u32[]{:S(2)}) collective-permute-start(bf16[8,1152]{1,0:T(8,128)(2,1)} %param.5), channel_id=1, source_target_pairs={{0,8},{8,0},{1,9},{9,1},{2,10},{10,2},{3,11},{11,3},{4,12},{12,4},... | collective-permute-start | bytes 55304 | tf_op jit(solution)/shard_map/ppermute | solution.py:21
  17.1 26.4 %collective-permute-start.2 = (bf16[1152,512]{1,0:T(8,128)(2,1)}, bf16[1152,512]{1,0:T(8,128)(2,1)}, u32[]{:S(2)}, u32[]{:S(2)}) collective-permute-start(bf16[1152,512]{1,0:T(8,128)(2,1)} %param.6), channel_id=1, source_target_pairs={{0,1},{1,0},{2,3},{3,2},{4,5},{5,4},{6,7},{7,6},{8,9},{9,8},{10,11... | collective-permute-start | bytes 3538952 | tf_op jit(solution)/shard_map/ppermute | solution.py:21
  19.9 23.2 %collective-permute-start.3 = (bf16[512,1152]{1,0:T(8,128)(2,1)}, bf16[512,1152]{1,0:T(8,128)(2,1)S(1)}, u32[]{:S(2)}, u32[]{:S(2)}) collective-permute-start(bf16[512,1152]{1,0:T(8,128)(2,1)} %param.8), channel_id=1, source_target_pairs={{0,1},{1,0},{2,3},{3,2},{4,5},{5,4},{6,7},{7,6},{8,9},{9,8},{10,11... | collective-permute-start | bytes 3538952 | tf_op jit(solution)/shard_map/ppermute | solution.py:21
  23.4 17.7 %all-to-all-start = ((bf16[16,16,1152]{2,1,0:T(8,128)(2,1)}), bf16[16,16,1152]{2,1,0:T(8,128)(2,1)S(1)}, u32[]{:S(2)}, u32[]{:S(2)}) async-start(bf16[16,16,1152]{2,1,0:T(8,128)(2,1)} %broadcast_in_dim.10), calls=%async_computation | async-start | bytes 1179648 | tf_op jit(solution)/shard_map/all_to_all | solution.py:26
  41.1 2.3 %copy-start.1 = (bf16[16,16,1152]{2,1,0:T(8,128)(2,1)}, bf16[16,16,1152]{2,1,0:T(8,128)(2,1)S(1)}, u32[]{:S(2)}) copy-start(bf16[16,16,1152]{2,1,0:T(8,128)(2,1)S(1)} %all-to-all-done) | copy-start | bytes 1769476
  45.3 20.6 %copy-start.8 = (f32[512]{0:T(512)S(1)}, f32[512]{0:T(512)}, u32[]{:S(2)}) copy-start(f32[512]{0:T(512)} %param.7) | copy-start | bytes 6148
  62.3 19.9 %collective-permute-start.4 = (bf16[136,512]{1,0:T(8,128)(2,1)S(1)}, bf16[136,512]{1,0:T(8,128)(2,1)S(1)}, u32[]{:S(2)}, u32[]{:S(2)}) collective-permute-start(bf16[136,512]{1,0:T(8,128)(2,1)S(1)} %convert_element_type.95), channel_id=1, source_target_pairs={{0,256},{256,0},{1,257},{257,1},{2,258},{258,2},{3,259},{259,3},{4... | collective-permute-start | bytes 417800 | tf_op jit(solution)/shard_map/ppermute | solution.py:21
  65.9 5.1 %collective-permute-start.5 = (f32[512]{0:T(512)S(1)}, f32[512]{0:T(512)S(1)}, u32[]{:S(2)}, u32[]{:S(2)}) collective-permute-start(f32[512]{0:T(512)S(1)} %copy-done.8), channel_id=1, source_target_pairs={{0,1},{1,0},{2,3},{3,2},{4,5},{5,4},{6,7},{7,6},{8,9},{9,8},{10,11... | collective-permute-start | bytes 6152 | tf_op jit(solution)/shard_map/ppermute | solution.py:21
  82.2 0.7 copy-start.6
  82.3 0.8 copy-start.3
  100.8 27.7 %copy-start.7 = (f32[1152]{0:T(1024)S(1)}, f32[1152]{0:T(1024)}, u32[]{:S(2)}) copy-start(f32[1152]{0:T(1024)} %param.9) | copy-start | bytes 13828
  115.0 13.4 %collective-permute-start.6 = (bf16[16,1152]{1,0:T(8,128)(2,1)S(1)}, bf16[16,1152]{1,0:T(8,128)(2,1)S(1)}, u32[]{:S(2)}, u32[]{:S(2)}) collective-permute-start(bf16[16,1152]{1,0:T(8,128)(2,1)S(1)} %convert_element_type.100), channel_id=1, source_target_pairs={{0,8},{8,0},{1,9},{9,1},{2,10},{10,2},{3,11},{11,3},{4,12},{12,4},... | collective-permute-start | bytes 110600 | tf_op jit(solution)/shard_map/ppermute | solution.py:21
  143.1 13.4 %all-to-all-start.5 = ((bf16[4,128,512]{2,1,0:T(8,128)(2,1)}), bf16[4,128,512]{2,1,0:T(8,128)(2,1)}, u32[]{:S(2)}, u32[]{:S(2)}) async-start(bf16[4,128,512]{2,1,0:T(8,128)(2,1)} %pad_maximum_fusion.2), calls=%async_computation.5 | async-start | bytes 1048576 | tf_op jit(solution)/shard_map/all_to_all | solution.py:44
  147.2 35.7 %collective-permute-start.1 = (bf16[256,1152]{1,0:T(8,128)(2,1)}, bf16[256,1152]{1,0:T(8,128)(2,1)}, u32[]{:S(2)}, u32[]{:S(2)}) collective-permute-start(bf16[256,1152]{1,0:T(8,128)(2,1)} %bitcast.52), channel_id=1, source_target_pairs={{0,1},{1,0},{2,3},{3,2},{4,5},{5,4},{6,7},{7,6},{8,9},{9,8},{10,11... | collective-permute-start | bytes 1769480 | tf_op jit(solution)/shard_map/ppermute | solution.py:21
  157.7 18.6 %collective-permute-start.7 = (bf16[128,512]{1,0:T(8,128)(2,1)S(1)}, bf16[128,512]{1,0:T(8,128)(2,1)S(1)}, u32[]{:S(2)}, u32[]{:S(2)}) collective-permute-start(bf16[128,512]{1,0:T(8,128)(2,1)S(1)} %convert_element_type.107), channel_id=1, source_target_pairs={{0,256},{256,0},{1,257},{257,1},{2,258},{258,2},{3,259},{259,3},{4... | collective-permute-start | bytes 393224 | tf_op jit(solution)/shard_map/ppermute | solution.py:21
  161.6 14.7 %copy-start.4 = (f32[128,512]{1,0:T(8,128)S(1)}, f32[128,512]{1,0:T(8,128)}, u32[]{:S(2)}) copy-start(f32[128,512]{1,0:T(8,128)} %copy-done.3) | copy-start | bytes 786436
  163.2 22.7 %collective-permute-start.8 = (bf16[512,1152]{1,0:T(8,128)(2,1)}, bf16[512,1152]{1,0:T(8,128)(2,1)}, u32[]{:S(2)}, u32[]{:S(2)}) collective-permute-start(bf16[512,1152]{1,0:T(8,128)(2,1)} %fusion.4), channel_id=1, source_target_pairs={{0,1},{1,0},{2,3},{3,2},{4,5},{5,4},{6,7},{7,6},{8,9},{9,8},{10,11... | collective-permute-start | bytes 3538952 | tf_op jit(solution)/shard_map/ppermute | solution.py:21
  176.5 6.5 %copy-start.2 = (bf16[16,16,1152]{2,1,0:T(8,128)(2,1)S(1)}, bf16[16,16,1152]{2,1,0:T(8,128)(2,1)}, u32[]{:S(2)}) copy-start(bf16[16,16,1152]{2,1,0:T(8,128)(2,1)} %copy-done.1) | copy-start | bytes 1769476
  177.4 16.9 %all-to-all-start.6 = ((bf16[8,64,512]{2,1,0:T(8,128)(2,1)}), bf16[8,64,512]{2,1,0:T(8,128)(2,1)}, u32[]{:S(2)}, u32[]{:S(2)}) async-start(bf16[8,64,512]{2,1,0:T(8,128)(2,1)} %bitcast.16), calls=%async_computation.6 | async-start | bytes 1048576 | tf_op jit(solution)/shard_map/all_to_all | solution.py:95
  185.8 8.4 %copy-start.5 = (bf16[4,2,64,1152]{3,2,1,0:T(8,128)(2,1)S(1)}, bf16[4,2,64,1152]{3,2,1,0:T(8,128)(2,1)}, u32[]{:S(2)}) copy-start(bf16[4,2,64,1152]{3,2,1,0:T(8,128)(2,1)} %pad_maximum_fusion) | copy-start | bytes 3538948

commit v5 on v4

--- a/solution.py
+++ b/solution.py
@@ -36,12 +36,15 @@
     return lax.dot_general(a, b, (dims, ((), ())), preferred_element_type=f32)
 
 
-def sum_over_layer(sides, tail=None):
+def sum_near(sides, tail=None):
     parts = [s.astype(bf16).reshape(4, -1, s.shape[-1]) for s in sides]
     if tail is not None:
         parts.append(jnp.broadcast_to(tail.astype(bf16), (4, *tail.shape)))
     parts = jnp.concatenate(parts, axis=1)
-    total = jnp.sum(lax.all_to_all(parts, QUARTER, 0, 0, tiled=True).astype(f32), axis=0)
+    return jnp.sum(lax.all_to_all(parts, QUARTER, 0, 0, tiled=True).astype(f32), axis=0)
+
+
+def sum_far(total):
     return total + swap(total.astype(bf16), "la").astype(f32)
 
 
@@ -53,21 +56,27 @@
 
 def local(activations, enc_weight, enc_bias, dec_weight, dec_bias):
     rows, features = activations.shape
+    hidden = dec_weight.shape[0]
     plane = lax.axis_size("x") * lax.axis_size("y")
     count = plane * 2 * rows
 
     both = jnp.concatenate([activations, swap(activations, "zhi")], axis=0)
-    acts = spread(both, plane)
     enc_other = swap(enc_weight, "core")
     dec = (dec_weight, swap(dec_weight, "core"))
+    dec_f32 = [d.astype(f32) for d in dec]
+    square = jnp.broadcast_to(jnp.sum(dec_f32[0] * dec_f32[0], axis=1)[None], (4, hidden)).astype(bf16)
+    both, square = lax.optimization_barrier((both, square))
+    acts = spread(both, plane)
+    near = dot(acts, enc_weight).astype(bf16)
+    near, other = lax.optimization_barrier((near, dec[1]))
+    other = other.astype(f32)
+    other = jnp.broadcast_to(jnp.sum(other * other, axis=1)[None], (4, hidden)).astype(bf16)
+    squares = jnp.concatenate([square, other], axis=0)
     bias = jnp.stack([enc_bias, swap(enc_bias, "core")])[:, None, :]
-    far_acts = swap(acts, "core")
 
-    dec_f32 = [d.astype(f32) for d in dec]
-    squares = jnp.pad(jnp.stack([jnp.sum(d * d, axis=1) for d in dec_f32]), ((0, 6), (0, 0)))
-    total = sum_over_layer([dot(acts, enc_weight), dot(acts, enc_other)], squares)
+    total = sum_far(sum_near([near, dot(acts, enc_other)], squares))
     preact = total[: count // 2].reshape(2, count // 4, -1) + bias
-    dec_norm = jnp.sqrt(total[count // 2 : count // 2 + 2] + norm_eps)
+    dec_norm = jnp.sqrt(total[count // 2 :: 4] + norm_eps)
     gating = jax.nn.sigmoid(sharpness * preact)
     latents = gather_over_layer((preact * gating).astype(bf16))
 
@@ -78,7 +87,10 @@
     rebuilt = part + jnp.concatenate([got[rows:], got[:rows]], axis=0)
     residual = spread((rebuilt + dec_bias - both.astype(f32)).astype(bf16), plane)
 
-    lat_grad = sum_over_layer([dot(residual, d, ((1,), (1,))) for d in dec])
+    lat_grad = sum_near([dot(residual, d, ((1,), (1,))) for d in dec])
+    lat_grad, latents, acts_later, residual = lax.optimization_barrier((lat_grad, latents, acts, residual))
+    far_acts = swap(acts_later, "core")
+    lat_grad = sum_far(lat_grad)
     lat_grad = lat_grad.reshape(2, count // 4, -1) + sparsity * dec_norm[:, None, :]
 
     lat_sums = jnp.sum(latents.astype(f32), axis=1)

time: 200 us -> 196 us (0.980)
  blocking collectives: 60.1 us -> 77.5 us
  starting transfers between devices: 71.9 us -> 60.6 us
  waiting for transfers between devices: 40.8 us -> 34.8 us
  matrix products: 10.8 us -> 8.08 us
    all_to_all x1 -> x2, blocking collectives: 12.7 us -> 30.6 us  [spread(): lax.all_to_all(blocks, PLANE, 0, 0, tiled=True).reshape(-1, block.shape[-1])]
    all_to_all x2 -> x1, starting transfers between devices: 10.9 us -> 4.14 us  [sum_near(): lax.all_to_all(parts, QUARTER, 0, 0, tiled=True).astype(f32)]
    ppermute x9, starting transfers between devices: 55.4 us -> 48.7 us  [swap(): return lax.ppermute(x, axis, SWAP)]
    all_to_all x2 -> x1, waiting for transfers between devices: 12.1 us -> 8.17 us  [sum_near(): lax.all_to_all(parts, QUARTER, 0, 0, tiled=True).astype(f32)]
    dot_general x9, matrix products: 10.8 us -> 8.08 us  [dot(): return lax.dot_general(a, b, (dims, ((), ())), preferred_element_type=f32)]
    ppermute x9, waiting for transfers between devices: 22.9 us -> 20.6 us  [swap(): return lax.ppermute(x, axis, SWAP)]
    all_to_all x1, starting transfers between devices: 5.59 us -> 7.76 us  [local(): lax.all_to_all(pre_grad.reshape(8, *pre_grad.shape[2:]), (*QUARTER, 'core...]
  transfers between devices with their start and end apart: 12 -> 11, of which waited for: 7 -> 5; matrix products, arithmetic and copies ran while one was open for 7% -> 5% of each run, Pallas kernels for 0% -> 0%
where the time goes in v5:
time: 196 us; the launch traced here: 194 us
  blocking collectives  77.5 us (40%)
  starting transfers between devices  60.6 us (31%)
  waiting for transfers between devices  34.8 us (18%)
  other arithmetic  9.56 us (5%)
  matrix products  8.08 us (4%)
  local copies, waits for them, and re-layouts  2.21 us (1%)
    ppermute x9, starting transfers between devices, swap(): return lax.ppermute(x, axis, SWAP)  48.7 us
    all_to_all x2, blocking collectives, spread(): lax.all_to_all(blocks, PLANE, 0, 0, tiled=True).reshape(-1, block.shape[-1])  30.6 us
    ppermute x9, waiting for transfers between devices, swap(): return lax.ppermute(x, axis, SWAP)  20.6 us
    all_to_all x1, blocking collectives, sum_near(): lax.all_to_all(parts, QUARTER, 0, 0, tiled=True).astype(f32)  16.9 us
    all_to_all x1, blocking collectives, gather_over_layer(): blocks = lax.all_to_all(blocks, QUARTER, 0, 0, tiled=True)  16.6 us
    all_to_all x1, blocking collectives, local(): lax.all_to_all(part.reshape(plane, 2 * rows, features), PLANE, 0, 0, tile...  13.5 us
    all_to_all x1, waiting for transfers between devices, sum_near(): lax.all_to_all(parts, QUARTER, 0, 0, tiled=True).astype(f32)  8.17 us
    dot_general x9, matrix products, dot(): return lax.dot_general(a, b, (dims, ((), ())), preferred_element_type=f32)  8.08 us
  transfers between devices with their start and end apart: 11, of which 5 were waited for; matrix products, arithmetic and copies ran while one was open for 5% of the time, Pallas kernels for 0%

profile of v5, /device:TPU:1, one launch (start us, length us, event | category | flops | bytes accessed | tf_op | source)
XLA Modules:
  0.0 194.0 jit_solution(6738606853022989851)
XLA Ops:
  0.6 16.3 %collective-permute-start = (bf16[8,1152]{1,0:T(8,128)(2,1)}, bf16[8,1152]{1,0:T(8,128)(2,1)S(1)}, u32[]{:S(2)}, u32[]{:S(2)}) collective-permute-start(bf16[8,1152]{1,0:T(8,128)(2,1)} %param.5), channel_id=1, source_target_pairs={{0,8},{8,0},{1,9},{9,1},{2,10},{10,2},{3,11},{11,3},{4,12},{12,4},... | collective-permute-start | bytes 55304 | tf_op jit(solution)/shard_map/ppermute | solution.py:21
  16.9 2.9 %collective-permute-start.1 = (bf16[512,1152]{1,0:T(8,128)(2,1)}, bf16[512,1152]{1,0:T(8,128)(2,1)S(1)}, u32[]{:S(2)}, u32[]{:S(2)}) collective-permute-start(bf16[512,1152]{1,0:T(8,128)(2,1)} %param.8), channel_id=1, source_target_pairs={{0,1},{1,0},{2,3},{3,2},{4,5},{5,4},{6,7},{7,6},{8,9},{9,8},{10,11... | collective-permute-start | bytes 3538952 | tf_op jit(solution)/shard_map/ppermute | solution.py:21
  19.8 1.9 collective-permute-start.2
  21.7 1.6 fusion.1
  23.3 0.0 collective-permute-done
  23.4 18.0 %all_to_all.35 = bf16[16,16,1152]{2,1,0:T(8,128)(2,1)S(1)} all-to-all(bf16[16,16,1152]{2,1,0:T(8,128)(2,1)S(1)} %broadcast_in_dim.15), channel_id=1, replica_groups=mesh['la'=2,'lb'=2,'lc'=2,'x'=4,'zhi'=2,'y'=4,'core'=2] {'x','y'}, dimensions={0} | all-to-all | bytes 1179648 | tf_op jit(solution)/shard_map/all_to_all | solution.py:26
  41.4 0.0 copy-done.12
  41.4 0.5 convolution_convert_fusion.4
  41.9 0.0 collective-permute-done.1
  41.9 0.3 multiply_reduce_fusion
  42.3 0.0 collective-permute-done.2
  42.3 0.5 convolution_convert_fusion.3
  42.8 0.0 copy-start.11
  42.9 16.9 %all_to_all.36 = bf16[4,136,512]{2,1,0:T(8,128)(2,1)S(1)} all-to-all(bf16[4,136,512]{2,1,0:T(8,128)(2,1)S(1)} %pad_maximum_fusion.1), channel_id=1, replica_groups=mesh['la'=2,'lb'=2,'lc'=2,'x'=4,'zhi'=2,'y'=4,'core'=2] {'lc','lb'}, dimensions={0} | all-to-all | bytes 1114112 | tf_op jit(solution)/shard_map/all_to_all | solution.py:44
  59.7 0.1 convert_reduce_fusion.1
  59.8 3.7 %collective-permute-start.3 = (bf16[136,512]{1,0:T(8,128)(2,1)S(1)}, bf16[136,512]{1,0:T(8,128)(2,1)S(1)}, u32[]{:S(2)}, u32[]{:S(2)}) collective-permute-start(bf16[136,512]{1,0:T(8,128)(2,1)S(1)} %convert_element_type.97), channel_id=1, source_target_pairs={{0,256},{256,0},{1,257},{257,1},{2,258},{258,2},{3,259},{259,3},{4... | collective-permute-start | bytes 417800 | tf_op jit(solution)/shard_map/ppermute | solution.py:21
  63.5 4.2 %collective-permute-start.4 = (f32[512]{0:T(512)S(1)}, f32[512]{0:T(512)S(1)}, u32[]{:S(2)}, u32[]{:S(2)}) collective-permute-start(f32[512]{0:T(512)S(1)} %copy-done.11), channel_id=1, source_target_pairs={{0,1},{1,0},{2,3},{3,2},{4,5},{5,4},{6,7},{7,6},{8,9},{9,8},{10,11... | collective-permute-start | bytes 6152 | tf_op jit(solution)/shard_map/ppermute | solution.py:21
  67.7 0.8 collective-permute-done.4
  68.5 11.5 %collective-permute-done.3 = bf16[136,512]{1,0:T(8,128)(2,1)S(1)} collective-permute-done((bf16[136,512]{1,0:T(8,128)(2,1)S(1)}, bf16[136,512]{1,0:T(8,128)(2,1)S(1)}, u32[]{:S(2)}, u32[]{:S(2)}) %collective-permute-start.3) | collective-permute-done | bytes 139296 | tf_op jit(solution)/shard_map/ppermute | solution.py:21
  80.1 0.1 multiply_convert_fusion.1
  80.3 0.0 copy-start
  80.3 16.6 %all_to_all.37 = bf16[4,2,64,512]{3,2,1,0:T(8,128)(2,1)S(1)} all-to-all(bf16[4,2,64,512]{3,2,1,0:T(8,128)(2,1)S(1)} %broadcast_in_dim.18), channel_id=1, replica_groups=mesh['la'=2,'lb'=2,'lc'=2,'x'=4,'zhi'=2,'y'=4,'core'=2] {'lc','lb'}, dimensions={0} | all-to-all | bytes 1048576 | tf_op jit(solution)/shard_map/all_to_all | solution.py:53
  96.9 0.0 copy-done.4
  96.9 0.0 copy-start.7
  96.9 0.0 copy-start.6
  96.9 0.0 copy-done
  96.9 0.5 fusion.14
  97.4 0.2 copy-done.7
  97.6 0.1 copy-done.6
  97.7 0.5 fusion
  98.2 0.0 copy-start.10
  98.2 13.5 %all_to_all.38 = bf16[16,16,1152]{2,1,0:T(8,128)(2,1)S(1)} all-to-all(bf16[16,16,1152]{2,1,0:T(8,128)(2,1)S(1)} %bitcast.54), channel_id=1, replica_groups=mesh['la'=2,'lb'=2,'lc'=2,'x'=4,'zhi'=2,'y'=4,'core'=2] {'x','y'}, dimensions={0} | all-to-all | bytes 1179648 | tf_op jit(solution)/shard_map/all_to_all | solution.py:84
  111.7 0.1 convert_reduce_fusion
  111.8 5.4 %collective-permute-start.5 = (bf16[16,1152]{1,0:T(8,128)(2,1)S(1)}, bf16[16,1152]{1,0:T(8,128)(2,1)S(1)}, u32[]{:S(2)}, u32[]{:S(2)}) collective-permute-start(bf16[16,1152]{1,0:T(8,128)(2,1)S(1)} %convert_element_type.102), channel_id=1, source_target_pairs={{0,8},{8,0},{1,9},{9,1},{2,10},{10,2},{3,11},{11,3},{4,12},{12,4},... | collective-permute-start | bytes 110600 | tf_op jit(solution)/shard_map/ppermute | solution.py:21
  117.2 8.3 %collective-permute-done.5 = bf16[16,1152]{1,0:T(8,128)(2,1)S(1)} collective-permute-done((bf16[16,1152]{1,0:T(8,128)(2,1)S(1)}, bf16[16,1152]{1,0:T(8,128)(2,1)S(1)}, u32[]{:S(2)}, u32[]{:S(2)}) %collective-permute-start.5) | collective-permute-done | bytes 36896 | tf_op jit(solution)/shard_map/ppermute | solution.py:21
  125.6 12.6 %all_to_all.39 = bf16[16,16,1152]{2,1,0:T(8,128)(2,1)S(1)} all-to-all(bf16[16,16,1152]{2,1,0:T(8,128)(2,1)S(1)} %broadcast_in_dim.19), channel_id=1, replica_groups=mesh['la'=2,'lb'=2,'lc'=2,'x'=4,'zhi'=2,'y'=4,'core'=2] {'x','y'}, dimensions={0} | all-to-all | bytes 1179648 | tf_op jit(solution)/shard_map/all_to_all | solution.py:26
  138.2 0.5 convolution_convert_fusion.2
  138.7 0.5 convolution_convert_fusion.1
  139.3 0.0 copy-done.1
  139.3 0.8 pad_maximum_fusion.2
  140.1 4.1 %all-to-all-start.5 = ((bf16[4,128,512]{2,1,0:T(8,128)(2,1)}), bf16[4,128,512]{2,1,0:T(8,128)(2,1)}, u32[]{:S(2)}, u32[]{:S(2)}) async-start(bf16[4,128,512]{2,1,0:T(8,128)(2,1)} %pad_maximum_fusion.2), calls=%async_computation.5 | async-start | bytes 1048576 | tf_op jit(solution)/shard_map/all_to_all | solution.py:44
  144.3 1.1 pad_maximum_fusion.3
  145.4 8.2 %all-to-all-done.5 = bf16[4,128,512]{2,1,0:T(8,128)(2,1)} async-done(((bf16[4,128,512]{2,1,0:T(8,128)(2,1)}), bf16[4,128,512]{2,1,0:T(8,128)(2,1)}, u32[]{:S(2)}, u32[]{:S(2)}) %all-to-all-start.5) | async-done | bytes 524320 | tf_op jit(solution)/shard_map/all_to_all | solution.py:44
  153.6 1.2 convert_reduce_fusion.3
  154.8 0.1 convert_reduce_fusion.2
  154.9 3.7 %collective-permute-start.7 = (bf16[128,512]{1,0:T(8,128)(2,1)S(1)}, bf16[128,512]{1,0:T(8,128)(2,1)S(1)}, u32[]{:S(2)}, u32[]{:S(2)}) collective-permute-start(bf16[128,512]{1,0:T(8,128)(2,1)S(1)} %convert_element_type.109), channel_id=1, source_target_pairs={{0,256},{256,0},{1,257},{257,1},{2,258},{258,2},{3,259},{259,3},{4... | collective-permute-start | bytes 393224 | tf_op jit(solution)/shard_map/ppermute | solution.py:21
  158.6 1.6 add_convert_fusion.1
  160.2 8.8 %collective-permute-start.8 = (bf16[512,1152]{1,0:T(8,128)(2,1)}, bf16[512,1152]{1,0:T(8,128)(2,1)}, u32[]{:S(2)}, u32[]{:S(2)}) collective-permute-start(bf16[512,1152]{1,0:T(8,128)(2,1)} %add_convert_fusion.1), channel_id=1, source_target_pairs={{0,1},{1,0},{2,3},{3,2},{4,5},{5,4},{6,7},{7,6},{8,9},{9,8},{10,11... | collective-permute-start | bytes 3538952 | tf_op jit(solution)/shard_map/ppermute | solution.py:21
  169.0 1.9 collective-permute-start.6
  170.9 0.0 collective-permute-done.7
  171.0 0.1 multiply_convert_fusion
  171.1 0.0 copy-start.3
  171.2 0.9 broadcast_in_dim.20
  172.0 7.8 %all-to-all-start.6 = ((bf16[8,64,512]{2,1,0:T(8,128)(2,1)}), bf16[8,64,512]{2,1,0:T(8,128)(2,1)}, u32[]{:S(2)}, u32[]{:S(2)}) async-start(bf16[8,64,512]{2,1,0:T(8,128)(2,1)} %bitcast.18), calls=%async_computation.6 | async-start | bytes 1048576 | tf_op jit(solution)/shard_map/all_to_all | solution.py:107
  179.8 0.5 convolution_add_fusion
  180.3 0.0 collective-permute-done.6
  180.3 0.0 copy-start.8
  180.4 0.8 copy-done.8
  181.2 1.2 broadcast_select_fusion.1
  182.3 0.1 pad_maximum_fusion
  182.5 0.0 collective-permute-done.8
  182.5 2.6 %add_convert_fusion = bf16[512,1152]{1,0:T(8,128)(2,1)} fusion(f32[512,1152]{1,0:T(8,128)S(1)} %convolution_add_fusion, bf16[512,1152]{1,0:T(8,128)(2,1)} %collective-permute-done.8), kind=kLoop, calls=%fused_computation.7 | loop fusion | flops 1769472 | bytes 4718592 | tf_op jit(solution)/shard_map/convert_element_type | solution.py:110
  185.0 6.1 %all-to-all-done.6 = bf16[8,64,512]{2,1,0:T(8,128)(2,1)} async-done(((bf16[8,64,512]{2,1,0:T(8,128)(2,1)}), bf16[8,64,512]{2,1,0:T(8,128)(2,1)}, u32[]{:S(2)}, u32[]{:S(2)}) %all-to-all-start.6) | async-done | bytes 524320 | tf_op jit(solution)/shard_map/all_to_all | solution.py:107
  191.1 2.9 %convolution_convert_fusion = bf16[1152,512]{1,0:T(8,128)(2,1)} fusion(bf16[512,1152]{1,0:T(8,128)(2,1)S(1)} %bitcast.61, bf16[512,512]{1,0:T(8,128)(2,1)} %bitcast.19), kind=kOutput, calls=%fused_computation.1 | convolution fusion | flops 604569600 | bytes 2883584 | tf_op jit(solution)/shard_map/dot_general | solution.py:36
  (36 shorter events, 0.5 us)
Async XLA Ops:
  0.6 22.7 %copy-start.9 = (bf16[8,1152]{1,0:T(8,128)(2,1)S(1)}, bf16[8,1152]{1,0:T(8,128)(2,1)}, u32[]{:S(2)}) copy-start(bf16[8,1152]{1,0:T(8,128)(2,1)} %param.5) | copy-start | bytes 55300
  0.6 22.7 %collective-permute-start = (bf16[8,1152]{1,0:T(8,128)(2,1)}, bf16[8,1152]{1,0:T(8,128)(2,1)S(1)}, u32[]{:S(2)}, u32[]{:S(2)}) collective-permute-start(bf16[8,1152]{1,0:T(8,128)(2,1)} %param.5), channel_id=1, source_target_pairs={{0,8},{8,0},{1,9},{9,1},{2,10},{10,2},{3,11},{11,3},{4,12},{12,4},... | collective-permute-start | bytes 55304 | tf_op jit(solution)/shard_map/ppermute | solution.py:21
  16.9 25.0 %collective-permute-start.1 = (bf16[512,1152]{1,0:T(8,128)(2,1)}, bf16[512,1152]{1,0:T(8,128)(2,1)S(1)}, u32[]{:S(2)}, u32[]{:S(2)}) collective-permute-start(bf16[512,1152]{1,0:T(8,128)(2,1)} %param.8), channel_id=1, source_target_pairs={{0,1},{1,0},{2,3},{3,2},{4,5},{5,4},{6,7},{7,6},{8,9},{9,8},{10,11... | collective-permute-start | bytes 3538952 | tf_op jit(solution)/shard_map/ppermute | solution.py:21
  19.8 22.5 %collective-permute-start.2 = (bf16[1152,512]{1,0:T(8,128)(2,1)}, bf16[1152,512]{1,0:T(8,128)(2,1)S(1)}, u32[]{:S(2)}, u32[]{:S(2)}) collective-permute-start(bf16[1152,512]{1,0:T(8,128)(2,1)} %param.6), channel_id=1, source_target_pairs={{0,1},{1,0},{2,3},{3,2},{4,5},{5,4},{6,7},{7,6},{8,9},{9,8},{10,11... | collective-permute-start | bytes 3538952 | tf_op jit(solution)/shard_map/ppermute | solution.py:21
  23.3 18.1 %copy-start.12 = (bf16[1152,512]{1,0:T(8,128)(2,1)S(1)}, bf16[1152,512]{1,0:T(8,128)(2,1)}, u32[]{:S(2)}) copy-start(bf16[1152,512]{1,0:T(8,128)(2,1)} %param.6) | copy-start | bytes 3538948
  42.8 20.6 %copy-start.11 = (f32[512]{0:T(512)S(1)}, f32[512]{0:T(512)}, u32[]{:S(2)}) copy-start(f32[512]{0:T(512)} %param.7) | copy-start | bytes 6148
  59.8 20.2 %collective-permute-start.3 = (bf16[136,512]{1,0:T(8,128)(2,1)S(1)}, bf16[136,512]{1,0:T(8,128)(2,1)S(1)}, u32[]{:S(2)}, u32[]{:S(2)}) collective-permute-start(bf16[136,512]{1,0:T(8,128)(2,1)S(1)} %convert_element_type.97), channel_id=1, source_target_pairs={{0,256},{256,0},{1,257},{257,1},{2,258},{258,2},{3,259},{259,3},{4... | collective-permute-start | bytes 417800 | tf_op jit(solution)/shard_map/ppermute | solution.py:21
  63.5 5.0 %collective-permute-start.4 = (f32[512]{0:T(512)S(1)}, f32[512]{0:T(512)S(1)}, u32[]{:S(2)}, u32[]{:S(2)}) collective-permute-start(f32[512]{0:T(512)S(1)} %copy-done.11), channel_id=1, source_target_pairs={{0,1},{1,0},{2,3},{3,2},{4,5},{5,4},{6,7},{7,6},{8,9},{9,8},{10,11... | collective-permute-start | bytes 6152 | tf_op jit(solution)/shard_map/ppermute | solution.py:21
  80.1 16.8 %copy-start.4 = (f32[128,512]{1,0:T(8,128)}, f32[128,512]{1,0:T(8,128)S(1)}, u32[]{:S(2)}) copy-start(f32[128,512]{1,0:T(8,128)S(1)} %slice.56) | copy-start | bytes 786436
  80.3 16.7 %copy-start = (bf16[512,1152]{1,0:T(8,128)(2,1)S(1)}, bf16[512,1152]{1,0:T(8,128)(2,1)}, u32[]{:S(2)}) copy-start(bf16[512,1152]{1,0:T(8,128)(2,1)} %param.8) | copy-start | bytes 3538948
  96.9 0.7 copy-start.7
  96.9 0.8 copy-start.6
  98.2 27.3 %copy-start.10 = (f32[1152]{0:T(1024)S(1)}, f32[1152]{0:T(1024)}, u32[]{:S(2)}) copy-start(f32[1152]{0:T(1024)} %param.9) | copy-start | bytes 13828
  111.8 13.7 %collective-permute-start.5 = (bf16[16,1152]{1,0:T(8,128)(2,1)S(1)}, bf16[16,1152]{1,0:T(8,128)(2,1)S(1)}, u32[]{:S(2)}, u32[]{:S(2)}) collective-permute-start(bf16[16,1152]{1,0:T(8,128)(2,1)S(1)} %convert_element_type.102), channel_id=1, source_target_pairs={{0,8},{8,0},{1,9},{9,1},{2,10},{10,2},{3,11},{11,3},{4,12},{12,4},... | collective-permute-start | bytes 110600 | tf_op jit(solution)/shard_map/ppermute | solution.py:21
  138.2 1.1 copy-start.1
  140.1 13.4 %all-to-all-start.5 = ((bf16[4,128,512]{2,1,0:T(8,128)(2,1)}), bf16[4,128,512]{2,1,0:T(8,128)(2,1)}, u32[]{:S(2)}, u32[]{:S(2)}) async-start(bf16[4,128,512]{2,1,0:T(8,128)(2,1)} %pad_maximum_fusion.2), calls=%async_computation.5 | async-start | bytes 1048576 | tf_op jit(solution)/shard_map/all_to_all | solution.py:44
  153.6 5.0 %copy-start.2 = (bf16[16,16,1152]{2,1,0:T(8,128)(2,1)S(1)}, bf16[16,16,1152]{2,1,0:T(8,128)(2,1)}, u32[]{:S(2)}) copy-start(bf16[16,16,1152]{2,1,0:T(8,128)(2,1)} %copy-done.1) | copy-start | bytes 1769476
  154.9 16.0 %collective-permute-start.7 = (bf16[128,512]{1,0:T(8,128)(2,1)S(1)}, bf16[128,512]{1,0:T(8,128)(2,1)S(1)}, u32[]{:S(2)}, u32[]{:S(2)}) collective-permute-start(bf16[128,512]{1,0:T(8,128)(2,1)S(1)} %convert_element_type.109), channel_id=1, source_target_pairs={{0,256},{256,0},{1,257},{257,1},{2,258},{258,2},{3,259},{259,3},{4... | collective-permute-start | bytes 393224 | tf_op jit(solution)/shard_map/ppermute | solution.py:21
  158.6 12.4 %copy-start.5 = (f32[128,512]{1,0:T(8,128)S(1)}, f32[128,512]{1,0:T(8,128)}, u32[]{:S(2)}) copy-start(f32[128,512]{1,0:T(8,128)} %copy-done.4) | copy-start | bytes 786436
  160.2 22.3 %collective-permute-start.8 = (bf16[512,1152]{1,0:T(8,128)(2,1)}, bf16[512,1152]{1,0:T(8,128)(2,1)}, u32[]{:S(2)}, u32[]{:S(2)}) collective-permute-start(bf16[512,1152]{1,0:T(8,128)(2,1)} %add_convert_fusion.1), channel_id=1, source_target_pairs={{0,1},{1,0},{2,3},{3,2},{4,5},{5,4},{6,7},{7,6},{8,9},{9,8},{10,11... | collective-permute-start | bytes 3538952 | tf_op jit(solution)/shard_map/ppermute | solution.py:21
  169.0 11.4 %collective-permute-start.6 = (bf16[256,1152]{1,0:T(8,128)(2,1)S(1)}, bf16[256,1152]{1,0:T(8,128)(2,1)S(1)}, u32[]{:S(2)}, u32[]{:S(2)}) collective-permute-start(bf16[256,1152]{1,0:T(8,128)(2,1)S(1)} %bitcast.48), channel_id=1, source_target_pairs={{0,1},{1,0},{2,3},{3,2},{4,5},{5,4},{6,7},{7,6},{8,9},{9,8},{10,11... | collective-permute-start | bytes 1769480 | tf_op jit(solution)/shard_map/ppermute | solution.py:21
  171.1 8.7 %copy-start.3 = (bf16[16,16,1152]{2,1,0:T(8,128)(2,1)S(1)}, bf16[16,16,1152]{2,1,0:T(8,128)(2,1)}, u32[]{:S(2)}) copy-start(bf16[16,16,1152]{2,1,0:T(8,128)(2,1)} %copy-done.1) | copy-start | bytes 1769476
  172.0 19.1 %all-to-all-start.6 = ((bf16[8,64,512]{2,1,0:T(8,128)(2,1)}), bf16[8,64,512]{2,1,0:T(8,128)(2,1)}, u32[]{:S(2)}, u32[]{:S(2)}) async-start(bf16[8,64,512]{2,1,0:T(8,128)(2,1)} %bitcast.18), calls=%async_computation.6 | async-start | bytes 1048576 | tf_op jit(solution)/shard_map/all_to_all | solution.py:107
  180.3 0.8 copy-start.8

commit v6 on v5

--- a/solution.py
+++ b/solution.py
@@ -1,6 +1,8 @@
 import jax
 import jax.numpy as jnp
 from jax import lax
+from jax.experimental import pallas as pl
+from jax.experimental.pallas import tpu as pltpu
 from jax.sharding import Mesh
 from jax.sharding import PartitionSpec as P
 
@@ -52,6 +54,29 @@
     blocks = jnp.broadcast_to(block[None], (4, *block.shape))
     blocks = lax.all_to_all(blocks, QUARTER, 0, 0, tiled=True)
     return jnp.stack([blocks[:, i].reshape(-1, block.shape[-1]) for i in (0, 1)])
+
+
+def outer_body(rows, grads, out):
+    out[...] = lax.dot_general(
+        rows[...], grads[...], (((0,), (0,)), ((), ())), preferred_element_type=f32
+    ).astype(bf16)
+
+
+def outer(rows, grads):
+    count, features = rows.shape
+    tile = features // 3
+    return pl.pallas_call(
+        outer_body,
+        grid=(features // tile,),
+        in_specs=[
+            pl.BlockSpec((count, tile), lambda i: (0, i)),
+            pl.BlockSpec(grads.shape, lambda i: (0, 0)),
+        ],
+        out_specs=pl.BlockSpec((tile, grads.shape[1]), lambda i: (i, 0)),
+        out_shape=jax.ShapeDtypeStruct((features, grads.shape[1]), bf16),
+        compiler_params=pltpu.CompilerParams(vmem_limit_bytes=24 * 1024 * 1024),
+        cost_estimate=pl.CostEstimate(flops=2 * count * features * grads.shape[1], bytes_accessed=3 << 20, transcendentals=0),
+    )(rows, grads)
 
 
 def local(activations, enc_weight, enc_bias, dec_weight, dec_bias):
@@ -106,8 +131,8 @@
     pre_grad = jnp.broadcast_to(pre_grad[None], (4, *pre_grad.shape))
     pre_grad = lax.all_to_all(pre_grad.reshape(8, *pre_grad.shape[2:]), (*QUARTER, "core"), 0, 0, tiled=True)
     rows = in_order(acts.reshape(4, 1, -1, features), far_acts.reshape(4, 1, -1, features), core, 1)
-    enc_grad = dot(rows.reshape(-1, features), pre_grad.reshape(2 * count, -1), ((0,), (0,)))
-    return (enc_grad.astype(bf16), dec_grad.astype(bf16))
+    enc_grad = outer(rows.reshape(-1, features), pre_grad.reshape(2 * count, -1))
+    return (enc_grad, dec_grad.astype(bf16))
 
 
 def solution(mesh):

time: 196 us -> 195 us (level)
  matrix products: 8.08 us -> 5.22 us
  Pallas kernels: 0 us -> 2.39 us
    dot_general x9 -> x8, matrix products: 8.08 us -> 5.22 us  [dot(): return lax.dot_general(a, b, (dims, ((), ())), preferred_element_type=f32)]
    pallas_call x0 -> x1, Pallas kernels: none -> 2.39 us  [outer(): pl.pallas_call(outer_body, grid=(features // tile,), in_specs=[pl.BlockSp...]
  transfers between devices with their start and end apart: 11 -> 11, of which waited for: 5 -> 5; matrix products, arithmetic and copies ran while one was open for 5% -> 6% of each run, Pallas kernels for 0% -> 0%
where the time goes in v6:
time: 195 us; the launch traced here: 193 us
  blocking collectives  77.5 us (40%)
  starting transfers between devices  60 us (31%)
  waiting for transfers between devices  35.5 us (18%)
  other arithmetic  9.57 us (5%)
  matrix products  5.22 us (3%)
  Pallas kernels  2.39 us (1%)
    ppermute x9, starting transfers between devices, swap(): return lax.ppermute(x, axis, SWAP)  48.7 us
    all_to_all x2, blocking collectives, spread(): lax.all_to_all(blocks, PLANE, 0, 0, tiled=True).reshape(-1, block.shape[-1])  30.6 us
    ppermute x9, waiting for transfers between devices, swap(): return lax.ppermute(x, axis, SWAP)  20.6 us
    all_to_all x1, blocking collectives, sum_near(): lax.all_to_all(parts, QUARTER, 0, 0, tiled=True).astype(f32)  16.9 us
    all_to_all x1, blocking collectives, gather_over_layer(): blocks = lax.all_to_all(blocks, QUARTER, 0, 0, tiled=True)  16.6 us
    all_to_all x1, blocking collectives, local(): lax.all_to_all(part.reshape(plane, 2 * rows, features), PLANE, 0, 0, tile...  13.5 us
    all_to_all x1, waiting for transfers between devices, sum_near(): lax.all_to_all(parts, QUARTER, 0, 0, tiled=True).astype(f32)  8.17 us
    all_to_all x1, starting transfers between devices, local(): lax.all_to_all(pre_grad.reshape(8, *pre_grad.shape[2:]), (*QUARTER, 'core...  7.14 us
  transfers between devices with their start and end apart: 11, of which 5 were waited for; matrix products, arithmetic and copies ran while one was open for 6% of the time, Pallas kernels for 0%

profile of v6, /device:TPU:1, one launch (start us, length us, event | category | flops | bytes accessed | tf_op | source)
XLA Modules:
  0.0 192.7 jit_solution(13177775852337323175)
XLA Ops:
  0.6 0.0 copy-start.8
  0.6 16.3 %collective-permute-start = (bf16[8,1152]{1,0:T(8,128)(2,1)}, bf16[8,1152]{1,0:T(8,128)(2,1)S(1)}, u32[]{:S(2)}, u32[]{:S(2)}) collective-permute-start(bf16[8,1152]{1,0:T(8,128)(2,1)} %param.5), channel_id=1, source_target_pairs={{0,8},{8,0},{1,9},{9,1},{2,10},{10,2},{3,11},{11,3},{4,12},{12,4},... | collective-permute-start | bytes 55304 | tf_op jit(solution)/shard_map/ppermute | solution.py:23
  16.9 2.9 %collective-permute-start.1 = (bf16[512,1152]{1,0:T(8,128)(2,1)}, bf16[512,1152]{1,0:T(8,128)(2,1)S(1)}, u32[]{:S(2)}, u32[]{:S(2)}) collective-permute-start(bf16[512,1152]{1,0:T(8,128)(2,1)} %param.8), channel_id=1, source_target_pairs={{0,1},{1,0},{2,3},{3,2},{4,5},{5,4},{6,7},{7,6},{8,9},{9,8},{10,11... | collective-permute-start | bytes 3538952 | tf_op jit(solution)/shard_map/ppermute | solution.py:23
  19.8 1.9 collective-permute-start.2
  21.7 1.6 fusion.1
  23.3 0.0 collective-permute-done
  23.3 0.0 copy-done.8
  23.4 18.0 %all_to_all.35 = bf16[16,16,1152]{2,1,0:T(8,128)(2,1)S(1)} all-to-all(bf16[16,16,1152]{2,1,0:T(8,128)(2,1)S(1)} %broadcast_in_dim.15), channel_id=1, replica_groups=mesh['la'=2,'lb'=2,'lc'=2,'x'=4,'zhi'=2,'y'=4,'core'=2] {'x','y'}, dimensions={0} | all-to-all | bytes 1179648 | tf_op jit(solution)/shard_map/all_to_all | solution.py:28
  41.4 0.0 copy-done.11
  41.4 0.5 convolution_convert_fusion.3
  41.9 0.0 collective-permute-done.1
  41.9 0.3 multiply_reduce_fusion
  42.3 0.0 collective-permute-done.2
  42.3 0.5 convolution_convert_fusion.2
  42.8 0.0 copy-start.10
  42.9 16.9 %all_to_all.36 = bf16[4,136,512]{2,1,0:T(8,128)(2,1)S(1)} all-to-all(bf16[4,136,512]{2,1,0:T(8,128)(2,1)S(1)} %pad_maximum_fusion.1), channel_id=1, replica_groups=mesh['la'=2,'lb'=2,'lc'=2,'x'=4,'zhi'=2,'y'=4,'core'=2] {'lc','lb'}, dimensions={0} | all-to-all | bytes 1114112 | tf_op jit(solution)/shard_map/all_to_all | solution.py:46
  59.7 0.1 convert_reduce_fusion.1
  59.8 3.7 %collective-permute-start.3 = (bf16[136,512]{1,0:T(8,128)(2,1)S(1)}, bf16[136,512]{1,0:T(8,128)(2,1)S(1)}, u32[]{:S(2)}, u32[]{:S(2)}) collective-permute-start(bf16[136,512]{1,0:T(8,128)(2,1)S(1)} %convert_element_type.94), channel_id=1, source_target_pairs={{0,256},{256,0},{1,257},{257,1},{2,258},{258,2},{3,259},{259,3},{4... | collective-permute-start | bytes 417800 | tf_op jit(solution)/shard_map/ppermute | solution.py:23
  63.5 0.0 copy-done.10
  63.5 4.2 %collective-permute-start.4 = (f32[512]{0:T(512)S(1)}, f32[512]{0:T(512)S(1)}, u32[]{:S(2)}, u32[]{:S(2)}) collective-permute-start(f32[512]{0:T(512)S(1)} %copy-done.10), channel_id=1, source_target_pairs={{0,1},{1,0},{2,3},{3,2},{4,5},{5,4},{6,7},{7,6},{8,9},{9,8},{10,11... | collective-permute-start | bytes 6152 | tf_op jit(solution)/shard_map/ppermute | solution.py:23
  67.7 0.8 collective-permute-done.4
  68.5 11.5 %collective-permute-done.3 = bf16[136,512]{1,0:T(8,128)(2,1)S(1)} collective-permute-done((bf16[136,512]{1,0:T(8,128)(2,1)S(1)}, bf16[136,512]{1,0:T(8,128)(2,1)S(1)}, u32[]{:S(2)}, u32[]{:S(2)}) %collective-permute-start.3) | collective-permute-done | bytes 139296 | tf_op jit(solution)/shard_map/ppermute | solution.py:23
  80.1 0.0 copy-start.4
  80.1 0.1 multiply_convert_fusion.1
  80.3 0.0 copy-start
  80.3 16.6 %all_to_all.37 = bf16[4,2,64,512]{3,2,1,0:T(8,128)(2,1)S(1)} all-to-all(bf16[4,2,64,512]{3,2,1,0:T(8,128)(2,1)S(1)} %broadcast_in_dim.18), channel_id=1, replica_groups=mesh['la'=2,'lb'=2,'lc'=2,'x'=4,'zhi'=2,'y'=4,'core'=2] {'lc','lb'}, dimensions={0} | all-to-all | bytes 1048576 | tf_op jit(solution)/shard_map/all_to_all | solution.py:55
  96.9 0.0 copy-done.4
  96.9 0.5 fusion.14
  97.4 0.2 copy-done.7
  97.6 0.1 copy-done.6
  97.7 0.5 fusion
  98.2 0.0 copy-start.9
  98.2 13.5 %all_to_all.38 = bf16[16,16,1152]{2,1,0:T(8,128)(2,1)S(1)} all-to-all(bf16[16,16,1152]{2,1,0:T(8,128)(2,1)S(1)} %bitcast.54), channel_id=1, replica_groups=mesh['la'=2,'lb'=2,'lc'=2,'x'=4,'zhi'=2,'y'=4,'core'=2] {'x','y'}, dimensions={0} | all-to-all | bytes 1179648 | tf_op jit(solution)/shard_map/all_to_all | solution.py:109
  111.7 0.1 convert_reduce_fusion
  111.8 5.4 %collective-permute-start.5 = (bf16[16,1152]{1,0:T(8,128)(2,1)S(1)}, bf16[16,1152]{1,0:T(8,128)(2,1)S(1)}, u32[]{:S(2)}, u32[]{:S(2)}) collective-permute-start(bf16[16,1152]{1,0:T(8,128)(2,1)S(1)} %convert_element_type.99), channel_id=1, source_target_pairs={{0,8},{8,0},{1,9},{9,1},{2,10},{10,2},{3,11},{11,3},{4,12},{12,4},... | collective-permute-start | bytes 110600 | tf_op jit(solution)/shard_map/ppermute | solution.py:23
  117.2 8.3 %collective-permute-done.5 = bf16[16,1152]{1,0:T(8,128)(2,1)S(1)} collective-permute-done((bf16[16,1152]{1,0:T(8,128)(2,1)S(1)}, bf16[16,1152]{1,0:T(8,128)(2,1)S(1)}, u32[]{:S(2)}, u32[]{:S(2)}) %collective-permute-start.5) | collective-permute-done | bytes 36896 | tf_op jit(solution)/shard_map/ppermute | solution.py:23
  125.6 12.6 %all_to_all.39 = bf16[16,16,1152]{2,1,0:T(8,128)(2,1)S(1)} all-to-all(bf16[16,16,1152]{2,1,0:T(8,128)(2,1)S(1)} %broadcast_in_dim.19), channel_id=1, replica_groups=mesh['la'=2,'lb'=2,'lc'=2,'x'=4,'zhi'=2,'y'=4,'core'=2] {'x','y'}, dimensions={0} | all-to-all | bytes 1179648 | tf_op jit(solution)/shard_map/all_to_all | solution.py:28
  138.2 0.5 convolution_convert_fusion.1
  138.7 0.5 convolution_convert_fusion
  139.3 0.8 pad_maximum_fusion.2
  140.1 4.1 %all-to-all-start.5 = ((bf16[4,128,512]{2,1,0:T(8,128)(2,1)}), bf16[4,128,512]{2,1,0:T(8,128)(2,1)}, u32[]{:S(2)}, u32[]{:S(2)}) async-start(bf16[4,128,512]{2,1,0:T(8,128)(2,1)} %pad_maximum_fusion.2), calls=%async_computation.5 | async-start | bytes 1048576 | tf_op jit(solution)/shard_map/all_to_all | solution.py:46
  144.3 1.1 pad_maximum_fusion.3
  145.4 8.2 %all-to-all-done.5 = bf16[4,128,512]{2,1,0:T(8,128)(2,1)} async-done(((bf16[4,128,512]{2,1,0:T(8,128)(2,1)}), bf16[4,128,512]{2,1,0:T(8,128)(2,1)}, u32[]{:S(2)}, u32[]{:S(2)}) %all-to-all-start.5) | async-done | bytes 524320 | tf_op jit(solution)/shard_map/all_to_all | solution.py:46
  153.6 1.2 convert_reduce_fusion.3
  154.8 0.1 convert_reduce_fusion.2
  154.9 3.7 %collective-permute-start.7 = (bf16[128,512]{1,0:T(8,128)(2,1)S(1)}, bf16[128,512]{1,0:T(8,128)(2,1)S(1)}, u32[]{:S(2)}, u32[]{:S(2)}) collective-permute-start(bf16[128,512]{1,0:T(8,128)(2,1)S(1)} %convert_element_type.106), channel_id=1, source_target_pairs={{0,256},{256,0},{1,257},{257,1},{2,258},{258,2},{3,259},{259,3},{4... | collective-permute-start | bytes 393224 | tf_op jit(solution)/shard_map/ppermute | solution.py:23
  158.6 1.6 add_convert_fusion.1
  160.2 8.8 %collective-permute-start.8 = (bf16[512,1152]{1,0:T(8,128)(2,1)}, bf16[512,1152]{1,0:T(8,128)(2,1)}, u32[]{:S(2)}, u32[]{:S(2)}) collective-permute-start(bf16[512,1152]{1,0:T(8,128)(2,1)} %add_convert_fusion.1), channel_id=1, source_target_pairs={{0,1},{1,0},{2,3},{3,2},{4,5},{5,4},{6,7},{7,6},{8,9},{9,8},{10,11... | collective-permute-start | bytes 3538952 | tf_op jit(solution)/shard_map/ppermute | solution.py:23
  169.0 1.9 collective-permute-start.6
  170.9 0.0 collective-permute-done.7
  170.9 0.0 copy-done.5
  171.0 0.1 multiply_convert_fusion
  171.1 0.0 copy-start.3
  171.1 0.8 broadcast_in_dim.20
  172.0 7.1 %all-to-all-start.6 = ((bf16[8,64,512]{2,1,0:T(8,128)(2,1)}), bf16[8,64,512]{2,1,0:T(8,128)(2,1)S(1)}, u32[]{:S(2)}, u32[]{:S(2)}) async-start(bf16[8,64,512]{2,1,0:T(8,128)(2,1)} %bitcast.61), calls=%async_computation.6 | async-start | bytes 1048576 | tf_op jit(solution)/shard_map/all_to_all | solution.py:132
  179.1 0.0 copy-done.3
  179.1 0.5 convolution_add_fusion
  179.7 0.0 collective-permute-done.6
  179.7 1.2 broadcast_select_fusion.1
  180.9 0.1 pad_maximum_fusion
  181.0 0.0 collective-permute-done.8
  181.0 2.6 %add_convert_fusion = bf16[512,1152]{1,0:T(8,128)(2,1)} fusion(f32[512,1152]{1,0:T(8,128)S(1)} %convolution_add_fusion, bf16[512,1152]{1,0:T(8,128)(2,1)} %collective-permute-done.8), kind=kLoop, calls=%fused_computation.6 | loop fusion | flops 1769472 | bytes 4718592 | tf_op jit(solution)/shard_map/convert_element_type | solution.py:135
  183.6 6.8 %all-to-all-done.6 = bf16[8,64,512]{2,1,0:T(8,128)(2,1)S(1)} async-done(((bf16[8,64,512]{2,1,0:T(8,128)(2,1)}), bf16[8,64,512]{2,1,0:T(8,128)(2,1)S(1)}, u32[]{:S(2)}, u32[]{:S(2)}) %all-to-all-start.6) | async-done | bytes 524320 | tf_op jit(solution)/shard_map/all_to_all | solution.py:132
  190.3 2.4 %shard_map.68 = bf16[1152,512]{1,0:T(8,128)(2,1)} custom-call(bf16[512,1152]{1,0:T(8,128)(2,1)S(1)} %bitcast.44, bf16[512,512]{1,0:T(8,128)(2,1)S(1)} %bitcast.45), custom_call_target="tpu_custom_call" | custom-call | flops 603979776 | bytes 3145728 | tf_op jit(solution)/shard_map/pallas_call | solution.py:68
  (34 shorter events, 0.5 us)
Async XLA Ops:
  0.6 22.7 %copy-start.8 = (bf16[8,1152]{1,0:T(8,128)(2,1)S(1)}, bf16[8,1152]{1,0:T(8,128)(2,1)}, u32[]{:S(2)}) copy-start(bf16[8,1152]{1,0:T(8,128)(2,1)} %param.5) | copy-start | bytes 55300
  0.6 22.7 %collective-permute-start = (bf16[8,1152]{1,0:T(8,128)(2,1)}, bf16[8,1152]{1,0:T(8,128)(2,1)S(1)}, u32[]{:S(2)}, u32[]{:S(2)}) collective-permute-start(bf16[8,1152]{1,0:T(8,128)(2,1)} %param.5), channel_id=1, source_target_pairs={{0,8},{8,0},{1,9},{9,1},{2,10},{10,2},{3,11},{11,3},{4,12},{12,4},... | collective-permute-start | bytes 55304 | tf_op jit(solution)/shard_map/ppermute | solution.py:23
  16.9 25.0 %collective-permute-start.1 = (bf16[512,1152]{1,0:T(8,128)(2,1)}, bf16[512,1152]{1,0:T(8,128)(2,1)S(1)}, u32[]{:S(2)}, u32[]{:S(2)}) collective-permute-start(bf16[512,1152]{1,0:T(8,128)(2,1)} %param.8), channel_id=1, source_target_pairs={{0,1},{1,0},{2,3},{3,2},{4,5},{5,4},{6,7},{7,6},{8,9},{9,8},{10,11... | collective-permute-start | bytes 3538952 | tf_op jit(solution)/shard_map/ppermute | solution.py:23
  19.8 22.5 %collective-permute-start.2 = (bf16[1152,512]{1,0:T(8,128)(2,1)}, bf16[1152,512]{1,0:T(8,128)(2,1)S(1)}, u32[]{:S(2)}, u32[]{:S(2)}) collective-permute-start(bf16[1152,512]{1,0:T(8,128)(2,1)} %param.6), channel_id=1, source_target_pairs={{0,1},{1,0},{2,3},{3,2},{4,5},{5,4},{6,7},{7,6},{8,9},{9,8},{10,11... | collective-permute-start | bytes 3538952 | tf_op jit(solution)/shard_map/ppermute | solution.py:23
  23.3 18.1 %copy-start.11 = (bf16[1152,512]{1,0:T(8,128)(2,1)S(1)}, bf16[1152,512]{1,0:T(8,128)(2,1)}, u32[]{:S(2)}) copy-start(bf16[1152,512]{1,0:T(8,128)(2,1)} %param.6) | copy-start | bytes 3538948
  42.8 20.6 %copy-start.10 = (f32[512]{0:T(512)S(1)}, f32[512]{0:T(512)}, u32[]{:S(2)}) copy-start(f32[512]{0:T(512)} %param.7) | copy-start | bytes 6148
  59.8 20.2 %collective-permute-start.3 = (bf16[136,512]{1,0:T(8,128)(2,1)S(1)}, bf16[136,512]{1,0:T(8,128)(2,1)S(1)}, u32[]{:S(2)}, u32[]{:S(2)}) collective-permute-start(bf16[136,512]{1,0:T(8,128)(2,1)S(1)} %convert_element_type.94), channel_id=1, source_target_pairs={{0,256},{256,0},{1,257},{257,1},{2,258},{258,2},{3,259},{259,3},{4... | collective-permute-start | bytes 417800 | tf_op jit(solution)/shard_map/ppermute | solution.py:23
  63.5 5.0 %collective-permute-start.4 = (f32[512]{0:T(512)S(1)}, f32[512]{0:T(512)S(1)}, u32[]{:S(2)}, u32[]{:S(2)}) collective-permute-start(f32[512]{0:T(512)S(1)} %copy-done.10), channel_id=1, source_target_pairs={{0,1},{1,0},{2,3},{3,2},{4,5},{5,4},{6,7},{7,6},{8,9},{9,8},{10,11... | collective-permute-start | bytes 6152 | tf_op jit(solution)/shard_map/ppermute | solution.py:23
  80.1 16.8 %copy-start.4 = (f32[128,512]{1,0:T(8,128)}, f32[128,512]{1,0:T(8,128)S(1)}, u32[]{:S(2)}) copy-start(f32[128,512]{1,0:T(8,128)S(1)} %slice.56) | copy-start | bytes 786436
  80.3 16.7 %copy-start = (bf16[512,1152]{1,0:T(8,128)(2,1)S(1)}, bf16[512,1152]{1,0:T(8,128)(2,1)}, u32[]{:S(2)}) copy-start(bf16[512,1152]{1,0:T(8,128)(2,1)} %param.8) | copy-start | bytes 3538948
  96.9 0.7 copy-start.7
  96.9 0.8 copy-start.6
  98.2 27.3 %copy-start.9 = (f32[1152]{0:T(1024)S(1)}, f32[1152]{0:T(1024)}, u32[]{:S(2)}) copy-start(f32[1152]{0:T(1024)} %param.9) | copy-start | bytes 13828
  111.8 13.7 %collective-permute-start.5 = (bf16[16,1152]{1,0:T(8,128)(2,1)S(1)}, bf16[16,1152]{1,0:T(8,128)(2,1)S(1)}, u32[]{:S(2)}, u32[]{:S(2)}) collective-permute-start(bf16[16,1152]{1,0:T(8,128)(2,1)S(1)} %convert_element_type.99), channel_id=1, source_target_pairs={{0,8},{8,0},{1,9},{9,1},{2,10},{10,2},{3,11},{11,3},{4,12},{12,4},... | collective-permute-start | bytes 110600 | tf_op jit(solution)/shard_map/ppermute | solution.py:23
  138.2 1.1 copy-start.1
  140.1 13.4 %all-to-all-start.5 = ((bf16[4,128,512]{2,1,0:T(8,128)(2,1)}), bf16[4,128,512]{2,1,0:T(8,128)(2,1)}, u32[]{:S(2)}, u32[]{:S(2)}) async-start(bf16[4,128,512]{2,1,0:T(8,128)(2,1)} %pad_maximum_fusion.2), calls=%async_computation.5 | async-start | bytes 1048576 | tf_op jit(solution)/shard_map/all_to_all | solution.py:46
  153.6 5.0 %copy-start.2 = (bf16[16,16,1152]{2,1,0:T(8,128)(2,1)S(1)}, bf16[16,16,1152]{2,1,0:T(8,128)(2,1)}, u32[]{:S(2)}) copy-start(bf16[16,16,1152]{2,1,0:T(8,128)(2,1)} %copy-done.1) | copy-start | bytes 1769476
  154.9 16.0 %collective-permute-start.7 = (bf16[128,512]{1,0:T(8,128)(2,1)S(1)}, bf16[128,512]{1,0:T(8,128)(2,1)S(1)}, u32[]{:S(2)}, u32[]{:S(2)}) collective-permute-start(bf16[128,512]{1,0:T(8,128)(2,1)S(1)} %convert_element_type.106), channel_id=1, source_target_pairs={{0,256},{256,0},{1,257},{257,1},{2,258},{258,2},{3,259},{259,3},{4... | collective-permute-start | bytes 393224 | tf_op jit(solution)/shard_map/ppermute | solution.py:23
  158.6 12.4 %copy-start.5 = (f32[128,512]{1,0:T(8,128)S(1)}, f32[128,512]{1,0:T(8,128)}, u32[]{:S(2)}) copy-start(f32[128,512]{1,0:T(8,128)} %copy-done.4) | copy-start | bytes 786436
  160.2 20.9 %collective-permute-start.8 = (bf16[512,1152]{1,0:T(8,128)(2,1)}, bf16[512,1152]{1,0:T(8,128)(2,1)}, u32[]{:S(2)}, u32[]{:S(2)}) collective-permute-start(bf16[512,1152]{1,0:T(8,128)(2,1)} %add_convert_fusion.1), channel_id=1, source_target_pairs={{0,1},{1,0},{2,3},{3,2},{4,5},{5,4},{6,7},{7,6},{8,9},{9,8},{10,11... | collective-permute-start | bytes 3538952 | tf_op jit(solution)/shard_map/ppermute | solution.py:23
  169.0 10.7 %collective-permute-start.6 = (bf16[256,1152]{1,0:T(8,128)(2,1)S(1)}, bf16[256,1152]{1,0:T(8,128)(2,1)}, u32[]{:S(2)}, u32[]{:S(2)}) collective-permute-start(bf16[256,1152]{1,0:T(8,128)(2,1)S(1)} %bitcast.48), channel_id=1, source_target_pairs={{0,1},{1,0},{2,3},{3,2},{4,5},{5,4},{6,7},{7,6},{8,9},{9,8},{10,11... | collective-permute-start | bytes 1769480 | tf_op jit(solution)/shard_map/ppermute | solution.py:23
  171.1 8.0 %copy-start.3 = (bf16[16,16,1152]{2,1,0:T(8,128)(2,1)S(1)}, bf16[16,16,1152]{2,1,0:T(8,128)(2,1)}, u32[]{:S(2)}) copy-start(bf16[16,16,1152]{2,1,0:T(8,128)(2,1)} %copy-done.1) | copy-start | bytes 1769476
  172.0 18.4 %all-to-all-start.6 = ((bf16[8,64,512]{2,1,0:T(8,128)(2,1)}), bf16[8,64,512]{2,1,0:T(8,128)(2,1)S(1)}, u32[]{:S(2)}, u32[]{:S(2)}) async-start(bf16[8,64,512]{2,1,0:T(8,128)(2,1)} %bitcast.61), calls=%async_computation.6 | async-start | bytes 1048576 | tf_op jit(solution)/shard_map/all_to_all | solution.py:132

commit v7 on v6

--- a/solution.py
+++ b/solution.py
@@ -64,7 +64,7 @@
 
 def outer(rows, grads):
     count, features = rows.shape
-    tile = features // 3
+    tile = features
     return pl.pallas_call(
         outer_body,
         grid=(features // tile,),

time: 195 us -> 194 us (level)
  no operation moved by 1% of the time
where the time goes in v7:
time: 194 us; the launch traced here: 192 us
  blocking collectives  77.5 us (40%)
  starting transfers between devices  60 us (31%)
  waiting for transfers between devices  35.5 us (18%)
  other arithmetic  9.57 us (5%)
  matrix products  5.22 us (3%)
    ppermute x9, starting transfers between devices, swap(): return lax.ppermute(x, axis, SWAP)  48.7 us
    all_to_all x2, blocking collectives, spread(): lax.all_to_all(blocks, PLANE, 0, 0, tiled=True).reshape(-1, block.shape[-1])  30.6 us
    ppermute x9, waiting for transfers between devices, swap(): return lax.ppermute(x, axis, SWAP)  20.6 us
    all_to_all x1, blocking collectives, sum_near(): lax.all_to_all(parts, QUARTER, 0, 0, tiled=True).astype(f32)  16.9 us
    all_to_all x1, blocking collectives, gather_over_layer(): blocks = lax.all_to_all(blocks, QUARTER, 0, 0, tiled=True)  16.6 us
    all_to_all x1, blocking collectives, local(): lax.all_to_all(part.reshape(plane, 2 * rows, features), PLANE, 0, 0, tile...  13.5 us
    all_to_all x1, waiting for transfers between devices, sum_near(): lax.all_to_all(parts, QUARTER, 0, 0, tiled=True).astype(f32)  8.17 us
    all_to_all x1, starting transfers between devices, local(): lax.all_to_all(pre_grad.reshape(8, *pre_grad.shape[2:]), (*QUARTER, 'core...  7.14 us
  transfers between devices with their start and end apart: 11, of which 5 were waited for; matrix products, arithmetic and copies ran while one was open for 6% of the time, Pallas kernels for 0%

profile of v7, /device:TPU:1, one launch (start us, length us, event | category | flops | bytes accessed | tf_op | source)
XLA Modules:
  0.0 192.2 jit_solution(10634401899131081712)
XLA Ops:
  0.6 0.0 copy-start.8
  0.6 16.3 %collective-permute-start = (bf16[8,1152]{1,0:T(8,128)(2,1)}, bf16[8,1152]{1,0:T(8,128)(2,1)S(1)}, u32[]{:S(2)}, u32[]{:S(2)}) collective-permute-start(bf16[8,1152]{1,0:T(8,128)(2,1)} %param.5), channel_id=1, source_target_pairs={{0,8},{8,0},{1,9},{9,1},{2,10},{10,2},{3,11},{11,3},{4,12},{12,4},... | collective-permute-start | bytes 55304 | tf_op jit(solution)/shard_map/ppermute | solution.py:23
  16.9 2.9 %collective-permute-start.1 = (bf16[512,1152]{1,0:T(8,128)(2,1)}, bf16[512,1152]{1,0:T(8,128)(2,1)S(1)}, u32[]{:S(2)}, u32[]{:S(2)}) collective-permute-start(bf16[512,1152]{1,0:T(8,128)(2,1)} %param.8), channel_id=1, source_target_pairs={{0,1},{1,0},{2,3},{3,2},{4,5},{5,4},{6,7},{7,6},{8,9},{9,8},{10,11... | collective-permute-start | bytes 3538952 | tf_op jit(solution)/shard_map/ppermute | solution.py:23
  19.8 1.9 %collective-permute-start.2 = (bf16[1152,512]{1,0:T(8,128)(2,1)}, bf16[1152,512]{1,0:T(8,128)(2,1)S(1)}, u32[]{:S(2)}, u32[]{:S(2)}) collective-permute-start(bf16[1152,512]{1,0:T(8,128)(2,1)} %param.6), channel_id=1, source_target_pairs={{0,1},{1,0},{2,3},{3,2},{4,5},{5,4},{6,7},{7,6},{8,9},{9,8},{10,11... | collective-permute-start | bytes 3538952 | tf_op jit(solution)/shard_map/ppermute | solution.py:23
  21.7 1.6 fusion.1
  23.3 0.0 collective-permute-done
  23.3 0.0 copy-done.8
  23.4 18.0 %all_to_all.35 = bf16[16,16,1152]{2,1,0:T(8,128)(2,1)S(1)} all-to-all(bf16[16,16,1152]{2,1,0:T(8,128)(2,1)S(1)} %broadcast_in_dim.15), channel_id=1, replica_groups=mesh['la'=2,'lb'=2,'lc'=2,'x'=4,'zhi'=2,'y'=4,'core'=2] {'x','y'}, dimensions={0} | all-to-all | bytes 1179648 | tf_op jit(solution)/shard_map/all_to_all | solution.py:28
  41.4 0.0 copy-done.11
  41.4 0.5 convolution_convert_fusion.3
  41.9 0.0 collective-permute-done.1
  41.9 0.3 multiply_reduce_fusion
  42.3 0.0 collective-permute-done.2
  42.3 0.5 convolution_convert_fusion.2
  42.8 0.0 copy-start.10
  42.9 16.9 %all_to_all.36 = bf16[4,136,512]{2,1,0:T(8,128)(2,1)S(1)} all-to-all(bf16[4,136,512]{2,1,0:T(8,128)(2,1)S(1)} %pad_maximum_fusion.1), channel_id=1, replica_groups=mesh['la'=2,'lb'=2,'lc'=2,'x'=4,'zhi'=2,'y'=4,'core'=2] {'lc','lb'}, dimensions={0} | all-to-all | bytes 1114112 | tf_op jit(solution)/shard_map/all_to_all | solution.py:46
  59.7 0.1 convert_reduce_fusion.1
  59.8 3.7 %collective-permute-start.3 = (bf16[136,512]{1,0:T(8,128)(2,1)S(1)}, bf16[136,512]{1,0:T(8,128)(2,1)S(1)}, u32[]{:S(2)}, u32[]{:S(2)}) collective-permute-start(bf16[136,512]{1,0:T(8,128)(2,1)S(1)} %convert_element_type.94), channel_id=1, source_target_pairs={{0,256},{256,0},{1,257},{257,1},{2,258},{258,2},{3,259},{259,3},{4... | collective-permute-start | bytes 417800 | tf_op jit(solution)/shard_map/ppermute | solution.py:23
  63.5 0.0 copy-done.10
  63.5 4.2 %collective-permute-start.4 = (f32[512]{0:T(512)S(1)}, f32[512]{0:T(512)S(1)}, u32[]{:S(2)}, u32[]{:S(2)}) collective-permute-start(f32[512]{0:T(512)S(1)} %copy-done.10), channel_id=1, source_target_pairs={{0,1},{1,0},{2,3},{3,2},{4,5},{5,4},{6,7},{7,6},{8,9},{9,8},{10,11... | collective-permute-start | bytes 6152 | tf_op jit(solution)/shard_map/ppermute | solution.py:23
  67.7 0.8 collective-permute-done.4
  68.5 11.5 %collective-permute-done.3 = bf16[136,512]{1,0:T(8,128)(2,1)S(1)} collective-permute-done((bf16[136,512]{1,0:T(8,128)(2,1)S(1)}, bf16[136,512]{1,0:T(8,128)(2,1)S(1)}, u32[]{:S(2)}, u32[]{:S(2)}) %collective-permute-start.3) | collective-permute-done | bytes 139296 | tf_op jit(solution)/shard_map/ppermute | solution.py:23
  80.1 0.0 copy-start.4
  80.1 0.1 multiply_convert_fusion.1
  80.3 0.0 copy-start
  80.3 16.6 %all_to_all.37 = bf16[4,2,64,512]{3,2,1,0:T(8,128)(2,1)S(1)} all-to-all(bf16[4,2,64,512]{3,2,1,0:T(8,128)(2,1)S(1)} %broadcast_in_dim.18), channel_id=1, replica_groups=mesh['la'=2,'lb'=2,'lc'=2,'x'=4,'zhi'=2,'y'=4,'core'=2] {'lc','lb'}, dimensions={0} | all-to-all | bytes 1048576 | tf_op jit(solution)/shard_map/all_to_all | solution.py:55
  96.9 0.0 copy-done.4
  96.9 0.0 copy-start.7
  96.9 0.5 fusion.14
  97.4 0.2 copy-done.7
  97.6 0.1 copy-done.6
  97.7 0.5 fusion
  98.2 0.0 copy-start.9
  98.2 13.5 %all_to_all.38 = bf16[16,16,1152]{2,1,0:T(8,128)(2,1)S(1)} all-to-all(bf16[16,16,1152]{2,1,0:T(8,128)(2,1)S(1)} %bitcast.54), channel_id=1, replica_groups=mesh['la'=2,'lb'=2,'lc'=2,'x'=4,'zhi'=2,'y'=4,'core'=2] {'x','y'}, dimensions={0} | all-to-all | bytes 1179648 | tf_op jit(solution)/shard_map/all_to_all | solution.py:109
  111.7 0.1 convert_reduce_fusion
  111.8 5.4 %collective-permute-start.5 = (bf16[16,1152]{1,0:T(8,128)(2,1)S(1)}, bf16[16,1152]{1,0:T(8,128)(2,1)S(1)}, u32[]{:S(2)}, u32[]{:S(2)}) collective-permute-start(bf16[16,1152]{1,0:T(8,128)(2,1)S(1)} %convert_element_type.99), channel_id=1, source_target_pairs={{0,8},{8,0},{1,9},{9,1},{2,10},{10,2},{3,11},{11,3},{4,12},{12,4},... | collective-permute-start | bytes 110600 | tf_op jit(solution)/shard_map/ppermute | solution.py:23
  117.2 8.3 %collective-permute-done.5 = bf16[16,1152]{1,0:T(8,128)(2,1)S(1)} collective-permute-done((bf16[16,1152]{1,0:T(8,128)(2,1)S(1)}, bf16[16,1152]{1,0:T(8,128)(2,1)S(1)}, u32[]{:S(2)}, u32[]{:S(2)}) %collective-permute-start.5) | collective-permute-done | bytes 36896 | tf_op jit(solution)/shard_map/ppermute | solution.py:23
  125.6 12.6 %all_to_all.39 = bf16[16,16,1152]{2,1,0:T(8,128)(2,1)S(1)} all-to-all(bf16[16,16,1152]{2,1,0:T(8,128)(2,1)S(1)} %broadcast_in_dim.19), channel_id=1, replica_groups=mesh['la'=2,'lb'=2,'lc'=2,'x'=4,'zhi'=2,'y'=4,'core'=2] {'x','y'}, dimensions={0} | all-to-all | bytes 1179648 | tf_op jit(solution)/shard_map/all_to_all | solution.py:28
  138.2 0.5 convolution_convert_fusion.1
  138.7 0.5 convolution_convert_fusion
  139.3 0.8 pad_maximum_fusion.2
  140.1 4.1 %all-to-all-start.5 = ((bf16[4,128,512]{2,1,0:T(8,128)(2,1)}), bf16[4,128,512]{2,1,0:T(8,128)(2,1)}, u32[]{:S(2)}, u32[]{:S(2)}) async-start(bf16[4,128,512]{2,1,0:T(8,128)(2,1)} %pad_maximum_fusion.2), calls=%async_computation.5 | async-start | bytes 1048576 | tf_op jit(solution)/shard_map/all_to_all | solution.py:46
  144.3 1.1 pad_maximum_fusion.3
  145.4 8.2 %all-to-all-done.5 = bf16[4,128,512]{2,1,0:T(8,128)(2,1)} async-done(((bf16[4,128,512]{2,1,0:T(8,128)(2,1)}), bf16[4,128,512]{2,1,0:T(8,128)(2,1)}, u32[]{:S(2)}, u32[]{:S(2)}) %all-to-all-start.5) | async-done | bytes 524320 | tf_op jit(solution)/shard_map/all_to_all | solution.py:46
  153.6 1.2 convert_reduce_fusion.3
  154.8 0.1 convert_reduce_fusion.2
  154.9 3.7 %collective-permute-start.7 = (bf16[128,512]{1,0:T(8,128)(2,1)S(1)}, bf16[128,512]{1,0:T(8,128)(2,1)S(1)}, u32[]{:S(2)}, u32[]{:S(2)}) collective-permute-start(bf16[128,512]{1,0:T(8,128)(2,1)S(1)} %convert_element_type.106), channel_id=1, source_target_pairs={{0,256},{256,0},{1,257},{257,1},{2,258},{258,2},{3,259},{259,3},{4... | collective-permute-start | bytes 393224 | tf_op jit(solution)/shard_map/ppermute | solution.py:23
  158.6 1.6 add_convert_fusion.1
  160.2 8.8 %collective-permute-start.8 = (bf16[512,1152]{1,0:T(8,128)(2,1)}, bf16[512,1152]{1,0:T(8,128)(2,1)}, u32[]{:S(2)}, u32[]{:S(2)}) collective-permute-start(bf16[512,1152]{1,0:T(8,128)(2,1)} %add_convert_fusion.1), channel_id=1, source_target_pairs={{0,1},{1,0},{2,3},{3,2},{4,5},{5,4},{6,7},{7,6},{8,9},{9,8},{10,11... | collective-permute-start | bytes 3538952 | tf_op jit(solution)/shard_map/ppermute | solution.py:23
  169.0 1.9 collective-permute-start.6
  170.9 0.0 collective-permute-done.7
  170.9 0.0 copy-done.5
  171.0 0.1 multiply_convert_fusion
  171.1 0.0 copy-start.3
  171.1 0.8 broadcast_in_dim.20
  172.0 7.1 %all-to-all-start.6 = ((bf16[8,64,512]{2,1,0:T(8,128)(2,1)}), bf16[8,64,512]{2,1,0:T(8,128)(2,1)S(1)}, u32[]{:S(2)}, u32[]{:S(2)}) async-start(bf16[8,64,512]{2,1,0:T(8,128)(2,1)} %bitcast.61), calls=%async_computation.6 | async-start | bytes 1048576 | tf_op jit(solution)/shard_map/all_to_all | solution.py:132
  179.1 0.5 convolution_add_fusion
  179.7 0.0 collective-permute-done.6
  179.7 1.2 broadcast_select_fusion.1
  180.9 0.1 pad_maximum_fusion
  181.0 0.0 collective-permute-done.8
  181.0 2.6 %add_convert_fusion = bf16[512,1152]{1,0:T(8,128)(2,1)} fusion(f32[512,1152]{1,0:T(8,128)S(1)} %convolution_add_fusion, bf16[512,1152]{1,0:T(8,128)(2,1)} %collective-permute-done.8), kind=kLoop, calls=%fused_computation.6 | loop fusion | flops 1769472 | bytes 4718592 | tf_op jit(solution)/shard_map/convert_element_type | solution.py:135
  183.6 6.8 %all-to-all-done.6 = bf16[8,64,512]{2,1,0:T(8,128)(2,1)S(1)} async-done(((bf16[8,64,512]{2,1,0:T(8,128)(2,1)}), bf16[8,64,512]{2,1,0:T(8,128)(2,1)S(1)}, u32[]{:S(2)}, u32[]{:S(2)}) %all-to-all-start.6) | async-done | bytes 524320 | tf_op jit(solution)/shard_map/all_to_all | solution.py:132
  190.3 1.8 shard_map.68
  (34 shorter events, 0.5 us)
Async XLA Ops:
  0.6 22.7 %copy-start.8 = (bf16[8,1152]{1,0:T(8,128)(2,1)S(1)}, bf16[8,1152]{1,0:T(8,128)(2,1)}, u32[]{:S(2)}) copy-start(bf16[8,1152]{1,0:T(8,128)(2,1)} %param.5) | copy-start | bytes 55300
  0.6 22.7 %collective-permute-start = (bf16[8,1152]{1,0:T(8,128)(2,1)}, bf16[8,1152]{1,0:T(8,128)(2,1)S(1)}, u32[]{:S(2)}, u32[]{:S(2)}) collective-permute-start(bf16[8,1152]{1,0:T(8,128)(2,1)} %param.5), channel_id=1, source_target_pairs={{0,8},{8,0},{1,9},{9,1},{2,10},{10,2},{3,11},{11,3},{4,12},{12,4},... | collective-permute-start | bytes 55304 | tf_op jit(solution)/shard_map/ppermute | solution.py:23
  16.9 25.0 %collective-permute-start.1 = (bf16[512,1152]{1,0:T(8,128)(2,1)}, bf16[512,1152]{1,0:T(8,128)(2,1)S(1)}, u32[]{:S(2)}, u32[]{:S(2)}) collective-permute-start(bf16[512,1152]{1,0:T(8,128)(2,1)} %param.8), channel_id=1, source_target_pairs={{0,1},{1,0},{2,3},{3,2},{4,5},{5,4},{6,7},{7,6},{8,9},{9,8},{10,11... | collective-permute-start | bytes 3538952 | tf_op jit(solution)/shard_map/ppermute | solution.py:23
  19.8 22.5 %collective-permute-start.2 = (bf16[1152,512]{1,0:T(8,128)(2,1)}, bf16[1152,512]{1,0:T(8,128)(2,1)S(1)}, u32[]{:S(2)}, u32[]{:S(2)}) collective-permute-start(bf16[1152,512]{1,0:T(8,128)(2,1)} %param.6), channel_id=1, source_target_pairs={{0,1},{1,0},{2,3},{3,2},{4,5},{5,4},{6,7},{7,6},{8,9},{9,8},{10,11... | collective-permute-start | bytes 3538952 | tf_op jit(solution)/shard_map/ppermute | solution.py:23
  23.3 18.1 %copy-start.11 = (bf16[1152,512]{1,0:T(8,128)(2,1)S(1)}, bf16[1152,512]{1,0:T(8,128)(2,1)}, u32[]{:S(2)}) copy-start(bf16[1152,512]{1,0:T(8,128)(2,1)} %param.6) | copy-start | bytes 3538948
  42.8 20.6 %copy-start.10 = (f32[512]{0:T(512)S(1)}, f32[512]{0:T(512)}, u32[]{:S(2)}) copy-start(f32[512]{0:T(512)} %param.7) | copy-start | bytes 6148
  59.8 20.2 %collective-permute-start.3 = (bf16[136,512]{1,0:T(8,128)(2,1)S(1)}, bf16[136,512]{1,0:T(8,128)(2,1)S(1)}, u32[]{:S(2)}, u32[]{:S(2)}) collective-permute-start(bf16[136,512]{1,0:T(8,128)(2,1)S(1)} %convert_element_type.94), channel_id=1, source_target_pairs={{0,256},{256,0},{1,257},{257,1},{2,258},{258,2},{3,259},{259,3},{4... | collective-permute-start | bytes 417800 | tf_op jit(solution)/shard_map/ppermute | solution.py:23
  63.5 5.0 %collective-permute-start.4 = (f32[512]{0:T(512)S(1)}, f32[512]{0:T(512)S(1)}, u32[]{:S(2)}, u32[]{:S(2)}) collective-permute-start(f32[512]{0:T(512)S(1)} %copy-done.10), channel_id=1, source_target_pairs={{0,1},{1,0},{2,3},{3,2},{4,5},{5,4},{6,7},{7,6},{8,9},{9,8},{10,11... | collective-permute-start | bytes 6152 | tf_op jit(solution)/shard_map/ppermute | solution.py:23
  80.1 16.8 %copy-start.4 = (f32[128,512]{1,0:T(8,128)}, f32[128,512]{1,0:T(8,128)S(1)}, u32[]{:S(2)}) copy-start(f32[128,512]{1,0:T(8,128)S(1)} %slice.56) | copy-start | bytes 786436
  80.3 16.7 %copy-start = (bf16[512,1152]{1,0:T(8,128)(2,1)S(1)}, bf16[512,1152]{1,0:T(8,128)(2,1)}, u32[]{:S(2)}) copy-start(bf16[512,1152]{1,0:T(8,128)(2,1)} %param.8) | copy-start | bytes 3538948
  96.9 0.7 copy-start.7
  96.9 0.8 copy-start.6
  98.2 27.3 %copy-start.9 = (f32[1152]{0:T(1024)S(1)}, f32[1152]{0:T(1024)}, u32[]{:S(2)}) copy-start(f32[1152]{0:T(1024)} %param.9) | copy-start | bytes 13828
  111.8 13.7 %collective-permute-start.5 = (bf16[16,1152]{1,0:T(8,128)(2,1)S(1)}, bf16[16,1152]{1,0:T(8,128)(2,1)S(1)}, u32[]{:S(2)}, u32[]{:S(2)}) collective-permute-start(bf16[16,1152]{1,0:T(8,128)(2,1)S(1)} %convert_element_type.99), channel_id=1, source_target_pairs={{0,8},{8,0},{1,9},{9,1},{2,10},{10,2},{3,11},{11,3},{4,12},{12,4},... | collective-permute-start | bytes 110600 | tf_op jit(solution)/shard_map/ppermute | solution.py:23
  138.2 1.1 copy-start.1
  140.1 13.4 %all-to-all-start.5 = ((bf16[4,128,512]{2,1,0:T(8,128)(2,1)}), bf16[4,128,512]{2,1,0:T(8,128)(2,1)}, u32[]{:S(2)}, u32[]{:S(2)}) async-start(bf16[4,128,512]{2,1,0:T(8,128)(2,1)} %pad_maximum_fusion.2), calls=%async_computation.5 | async-start | bytes 1048576 | tf_op jit(solution)/shard_map/all_to_all | solution.py:46
  153.6 5.0 %copy-start.2 = (bf16[16,16,1152]{2,1,0:T(8,128)(2,1)S(1)}, bf16[16,16,1152]{2,1,0:T(8,128)(2,1)}, u32[]{:S(2)}) copy-start(bf16[16,16,1152]{2,1,0:T(8,128)(2,1)} %copy-done.1) | copy-start | bytes 1769476
  154.9 16.0 %collective-permute-start.7 = (bf16[128,512]{1,0:T(8,128)(2,1)S(1)}, bf16[128,512]{1,0:T(8,128)(2,1)S(1)}, u32[]{:S(2)}, u32[]{:S(2)}) collective-permute-start(bf16[128,512]{1,0:T(8,128)(2,1)S(1)} %convert_element_type.106), channel_id=1, source_target_pairs={{0,256},{256,0},{1,257},{257,1},{2,258},{258,2},{3,259},{259,3},{4... | collective-permute-start | bytes 393224 | tf_op jit(solution)/shard_map/ppermute | solution.py:23
  158.6 12.4 %copy-start.5 = (f32[128,512]{1,0:T(8,128)S(1)}, f32[128,512]{1,0:T(8,128)}, u32[]{:S(2)}) copy-start(f32[128,512]{1,0:T(8,128)} %copy-done.4) | copy-start | bytes 786436
  160.2 20.9 %collective-permute-start.8 = (bf16[512,1152]{1,0:T(8,128)(2,1)}, bf16[512,1152]{1,0:T(8,128)(2,1)}, u32[]{:S(2)}, u32[]{:S(2)}) collective-permute-start(bf16[512,1152]{1,0:T(8,128)(2,1)} %add_convert_fusion.1), channel_id=1, source_target_pairs={{0,1},{1,0},{2,3},{3,2},{4,5},{5,4},{6,7},{7,6},{8,9},{9,8},{10,11... | collective-permute-start | bytes 3538952 | tf_op jit(solution)/shard_map/ppermute | solution.py:23
  169.0 10.7 %collective-permute-start.6 = (bf16[256,1152]{1,0:T(8,128)(2,1)S(1)}, bf16[256,1152]{1,0:T(8,128)(2,1)}, u32[]{:S(2)}, u32[]{:S(2)}) collective-permute-start(bf16[256,1152]{1,0:T(8,128)(2,1)S(1)} %bitcast.48), channel_id=1, source_target_pairs={{0,1},{1,0},{2,3},{3,2},{4,5},{5,4},{6,7},{7,6},{8,9},{9,8},{10,11... | collective-permute-start | bytes 1769480 | tf_op jit(solution)/shard_map/ppermute | solution.py:23
  171.1 8.0 %copy-start.3 = (bf16[16,16,1152]{2,1,0:T(8,128)(2,1)S(1)}, bf16[16,16,1152]{2,1,0:T(8,128)(2,1)}, u32[]{:S(2)}) copy-start(bf16[16,16,1152]{2,1,0:T(8,128)(2,1)} %copy-done.1) | copy-start | bytes 1769476
  172.0 18.4 %all-to-all-start.6 = ((bf16[8,64,512]{2,1,0:T(8,128)(2,1)}), bf16[8,64,512]{2,1,0:T(8,128)(2,1)S(1)}, u32[]{:S(2)}, u32[]{:S(2)}) async-start(bf16[8,64,512]{2,1,0:T(8,128)(2,1)} %bitcast.61), calls=%async_computation.6 | async-start | bytes 1048576 | tf_op jit(solution)/shard_map/all_to_all | solution.py:132
